TPU v7x, 128 devices: a whole 4x4x4 slice. The times are simulated.
128 devices in a mesh: gx: 4 (over y), gy: 32 (over x, z, core).
Axes of the slice: x: 4, y: 4, z: 4, core: 2. Of those that a mesh axis runs over, the one named last changes fastest.
Arguments:
- parents: bfloat16 [1024, 64, 256], P(('gx', 'gy')), may hold values from -6 to 6
- parent_dest: int32 [1024], P(('gx', 'gy')), may hold values from -1 to 511, as said below
- skip: bfloat16 [1024, 512, 128], P(('gx', 'gy')), may hold values from -6 to 6
- skip_dest: int32 [1024], P(('gx', 'gy')), may hold values from -1 to 511, as said below
- neighbours: int32 [512, 26], P(('gx', 'gy')), may hold values from -1 to 511, as said below
- up_weight: bfloat16 [8, 256, 128], replicated, may hold values from -0.375 to 0.375
- conv_weight: bfloat16 [27, 256, 128], replicated, may hold values from -0.078125 to 0.078125
Outputs:
- refined: bfloat16 [512, 512, 128], P(('gx', 'gy'))
Inputs may be any that keep to these rules, and one draw needn't show every extreme that they name: `parent_dest`: each child brick index appears exactly once. Child brick c belongs to device c // 4 of the flattened axis gx+gy (gx slowest) and to its slot c % 4; it lies on a device with the same gx index as the slot that names it. One device names at most 1 child bricks of any one device, and in every draw some device names exactly 1 of one device. In every draw some device has all 8 of its slots live. `skip_dest`: each child brick index appears exactly once. Child brick c belongs to device c // 4 of the flattened axis gx+gy (gx slowest) and to its slot c % 4; it lies on a device with the same gx index as the slot that names it. One device names at most 1 child bricks of any one device, and in every draw some device names exactly 1 of one device. In every draw some device has all 8 of its slots live. Direction k = 0..25 enumerates (dx, dy, dz) in the finite set (-1,0,1)^3 with dx slowest and dz fastest, (0,0,0) left out. neighbours[c, k] is the child brick displaced from brick c by (dx, dy, dz) in the brick lattice, or -1 where no brick is there; the relation is symmetric. A brick's neighbours belong to its own device or to the devices just before and just after it on the flattened axis gx+gy.
All inputs are finite; a program needn't handle non-finite values.
Results may differ from a plain program's by a relative error of at most 0.0039.
Values may be sent and summed in bfloat16 or wider, within the bound.
No kernel may reach another device: no remote copies, remote signals or barrier semaphores. Data moves between devices by JAX's collectives and lax.ppermute only.
A program may use at most 64 MiB of HBM per device.

v0:
```python
import jax
import jax.numpy as jnp
from jax import lax
from jax.sharding import PartitionSpec as P

neighbour_steps = [
    (code // 9 - 1, code // 3 % 3 - 1, code % 3 - 1) for code in range(27) if code != 13
]


def padded_2(array, sides, width):
    for axis, dim in sides:
        size, length = (lax.axis_size(axis), array.shape[dim])
        up = [(i, (i + 1) % size) for i in range(size - 1)]
        down = [(j, i) for i, j in up]
        last = lax.slice_in_dim(array, length - width, length, axis=dim)
        initial = lax.slice_in_dim(array, 0, width, axis=dim)
        before = lax.ppermute(last, axis, up)
        after = lax.ppermute(initial, axis, down)
        array = jnp.concatenate([before, array, after], axis=dim)
    return array


def edge_range(offset):
    if offset < 0:
        return slice(7, 8)
    if offset > 0:
        return slice(0, 1)
    return slice(0, 8)


def upsample(bricks_in, up_weight):
    brick_count = bricks_in.shape[0]
    product = jnp.einsum("nvc,tcd->nvtd", bricks_in, up_weight, preferred_element_type=jnp.float32)
    product = product.reshape(brick_count, 4, 4, 4, 2, 2, 2, up_weight.shape[2])
    product = product.transpose(0, 1, 4, 2, 5, 3, 6, 7)
    return product.reshape(brick_count, 512, up_weight.shape[2]).astype(jnp.bfloat16)


def faces_of(volume):
    return jnp.stack(
        [
            volume[:, 0],
            volume[:, 7],
            volume[:, :, 0],
            volume[:, :, 7],
            volume[:, :, :, 0],
            volume[:, :, :, 7],
        ],
        axis=1,
    )


def assemble(center, faces_pool, lookup):
    pieces = {}
    for direction, (off_x, off_y, off_z) in enumerate(neighbour_steps):
        if off_x != 0:
            surface = faces_pool[:, 1 if off_x < 0 else 0][:, edge_range(off_y), edge_range(off_z)][
                :, None
            ]
        elif off_y != 0:
            surface = faces_pool[:, 3 if off_y < 0 else 2][:, edge_range(off_x), edge_range(off_z)][
                :, :, None
            ]
        else:
            surface = faces_pool[:, 5 if off_z < 0 else 4][:, :, :, None]
        column = lookup[:, direction]
        picked = jnp.take(surface, jnp.maximum(column, 0), axis=0)
        pieces[off_x, off_y, off_z] = jnp.where(
            (column >= 0)[:, None, None, None, None], picked, jnp.zeros((), picked.dtype)
        )
    pieces[0, 0, 0] = center
    return jnp.concatenate(
        [
            jnp.concatenate(
                [
                    jnp.concatenate([pieces[off_x, off_y, off_z] for off_z in (-1, 0, 1)], axis=3)
                    for off_y in (-1, 0, 1)
                ],
                axis=2,
            )
            for off_x in (-1, 0, 1)
        ],
        axis=1,
    )


def convolve(padded, conv_weight):
    brick_count = padded.shape[0]
    rows_all = brick_count * 512
    result = jnp.zeros((rows_all, conv_weight.shape[2]), jnp.float32)
    for tap_index in range(27):
        start_x, start_y, start_z = (tap_index // 9, tap_index // 3 % 3, tap_index % 3)
        window = padded[
            :, start_x : start_x + 8, start_y : start_y + 8, start_z : start_z + 8, :
        ].reshape(rows_all, padded.shape[-1])
        result = result + jnp.dot(
            window, conv_weight[tap_index], preferred_element_type=jnp.float32
        )
    return (
        jnp.maximum(result, 0.0)
        .astype(jnp.bfloat16)
        .reshape(brick_count, 512, conv_weight.shape[2])
    )


def pack_rows(target, payload, bricks_dev, gy_count):
    slot_count = target.shape[0]
    capacity = -(-slot_count // gy_count)
    is_live = target >= 0
    owners = jnp.where(is_live, target // bricks_dev % gy_count, gy_count)
    same_owner = owners[:, None] == owners[None, :]
    earlier = jnp.arange(slot_count)[None, :] < jnp.arange(slot_count)[:, None]
    ranking = jnp.sum(same_owner & earlier, axis=1)
    placed = jnp.where(is_live, owners * capacity + ranking, gy_count * capacity)
    matches = placed[None, :] == jnp.arange(gy_count * capacity)[:, None]
    source = jnp.sum(jnp.where(matches, jnp.arange(slot_count)[None, :], 0), axis=1)
    filled = jnp.any(matches, axis=1)
    gathered = jnp.take(payload, source, axis=0)
    gathered = jnp.where(
        filled.reshape((-1,) + (1,) * (payload.ndim - 1)), gathered, jnp.zeros((), payload.dtype)
    )
    landing = jnp.where(filled, jnp.take(target % bricks_dev, source), -1)
    return (
        gathered.reshape((gy_count, capacity) + payload.shape[1:]),
        landing.reshape(gy_count, capacity),
    )


def unpack_rows(arrived, landing, bricks_dev):
    flat_rows = arrived.reshape((-1,) + arrived.shape[2:])
    spots = landing.reshape(-1)
    matches = spots[None, :] == jnp.arange(bricks_dev)[:, None]
    source = jnp.sum(jnp.where(matches, jnp.arange(spots.shape[0])[None, :], 0), axis=1)
    return jnp.take(flat_rows, source, axis=0)


def per_device(parents, parent_dest, skip, skip_dest, neighbours, up_weight, conv_weight):
    bricks_dev = neighbours.shape[0]
    gy_count = lax.axis_size("gy")
    skip_buffer, skip_landing = pack_rows(skip_dest, skip, bricks_dev, gy_count)
    children = upsample(parents, up_weight)
    child_buffer, child_landing = pack_rows(parent_dest, children, bricks_dev, gy_count)
    child_in, child_spots, skip_in, skip_spots = (
        lax.all_to_all(child_buffer, "gy", split_axis=0, concat_axis=0, tiled=True),
        lax.all_to_all(child_landing, "gy", split_axis=0, concat_axis=0, tiled=True),
        lax.all_to_all(skip_buffer, "gy", split_axis=0, concat_axis=0, tiled=True),
        lax.all_to_all(skip_landing, "gy", split_axis=0, concat_axis=0, tiled=True),
    )
    child_local = unpack_rows(child_in, child_spots, bricks_dev)
    skip_local = unpack_rows(skip_in, skip_spots, bricks_dev)
    features = jnp.concatenate([child_local, skip_local], axis=-1)
    features = features.reshape(bricks_dev, 8, 8, 8, features.shape[-1])
    device_index = lax.axis_index(("gx", "gy"))
    lookup = jnp.where(neighbours >= 0, neighbours - (device_index - 1) * bricks_dev, -1)
    pool_bricks = padded_2(features, ((("gx", "gy"), 0),), bricks_dev)
    faces_pool = faces_of(pool_bricks)
    padded = assemble(features, faces_pool, lookup)
    return convolve(padded, conv_weight)


def solution(mesh):
    placed = (
        P(("gx", "gy"), None, None),
        P(("gx", "gy")),
        P(("gx", "gy"), None, None),
        P(("gx", "gy")),
        P(("gx", "gy"), None),
        P(),
        P(),
    )
    return jax.shard_map(
        per_device,
        mesh=mesh,
        in_specs=placed,
        out_specs=P(("gx", "gy"), None, None),
        check_vma=False,
    )
```

profile of v0, /device:TPU:16, one launch (start us, length us, event | category | flops | bytes accessed | tf_op | source)
XLA Modules:
  0.0 290.3 jit_solution(6063655671336139713)
XLA Ops:
  3.2 8.2 %all-to-all-start.3 = ((s32[32,1,1]{2,1,0:T(1,128)}), s32[32,1,1]{2,1,0:T(1,128)S(1)}, u32[]{:S(2)}, u32[]{:S(2)}) async-start(s32[32,1,1]{2,1,0:T(1,128)} %copy.255), calls=%async_computation.3 | async-start | bytes 32768 | tf_op jit(solution)/shard_map/all_to_all | solution.py:148
  14.6 3.1 %gather_fusion.3 = bf16[32,512,128]{2,1,0:T(8,128)(2,1)} fusion(bf16[8,512,128]{2,1,0:T(8,128)(2,1)S(1)} %copy-done, s32[1024]{0:T(1024)S(1)} %pad_clamp_fusion.27), kind=kCustom, calls=%fused_computation.10.clone | custom fusion | bytes 8388736 | tf_op jit(solution)/shard_map/jit(_take)/gather | solution.py:119
  18.1 1.2 copy.252
  23.5 4.7 %fusion = bf16[32,1,512,128]{3,2,1,0:T(8,128)(2,1)} fusion(bf16[32,512,128]{2,1,0:T(8,128)(2,1)} %gather_fusion.3, pred[32]{0:T(512)(128)(4,1)S(1)} %get-tuple-element.70, pred[32]{0:T(512)(128)(4,1)S(1)} %fusion.80), kind=kLoop, calls=%fused_computation.33 | loop fusion | flops 4194304 | bytes 8388672 | tf_op jit(solution)/shard_map/reshape | solution.py:125
  29.6 7.4 %all-to-all-start.1 = ((s32[32,1,1]{2,1,0:T(1,128)}), s32[32,1,1]{2,1,0:T(1,128)S(1)}, u32[]{:S(2)}, u32[]{:S(2)}) async-start(s32[32,1,1]{2,1,0:T(1,128)} %copy.251), calls=%async_computation.1 | async-start | bytes 32768 | tf_op jit(solution)/shard_map/all_to_all | solution.py:146
  37.2 3.1 %gather_fusion = bf16[32,512,128]{2,1,0:T(8,128)(2,1)} fusion(bf16[8,512,128]{2,1,0:T(8,128)(2,1)S(1)} %copy.253, s32[1024]{0:T(1024)S(1)} %pad_clamp_fusion.29), kind=kCustom, calls=%fused_computation.clone | custom fusion | bytes 8388736 | tf_op jit(solution)/shard_map/jit(_take)/gather | solution.py:119
  40.2 4.2 %all-to-all-done.1 = s32[32,1,1]{2,1,0:T(1,128)S(1)} async-done(((s32[32,1,1]{2,1,0:T(1,128)}), s32[32,1,1]{2,1,0:T(1,128)S(1)}, u32[]{:S(2)}, u32[]{:S(2)}) %all-to-all-start.1) | async-done | bytes 160 | tf_op jit(solution)/shard_map/all_to_all | solution.py:146
  44.4 4.8 %all-to-all-start.2 = ((bf16[32,1,512,128]{3,2,1,0:T(8,128)(2,1)}), bf16[32,1,512,128]{3,2,1,0:T(8,128)(2,1)}, u32[]{:S(2)}, u32[]{:S(2)}) async-start(bf16[32,1,512,128]{3,2,1,0:T(8,128)(2,1)} %fusion), calls=%async_computation.2 | async-start | bytes 8388608 | tf_op jit(solution)/shard_map/all_to_all | solution.py:147
  58.8 4.7 %fusion.1 = bf16[32,1,512,128]{3,2,1,0:T(8,128)(2,1)} fusion(bf16[32,512,128]{2,1,0:T(8,128)(2,1)} %gather_fusion, pred[32]{0:T(512)(128)(4,1)S(1)} %get-tuple-element.68, pred[32]{0:T(512)(128)(4,1)S(1)} %fusion.81), kind=kLoop, calls=%fused_computation.35 | loop fusion | flops 4194304 | bytes 8388672 | tf_op jit(solution)/shard_map/reshape | solution.py:125
  63.5 38.4 %all-to-all-done.2 = bf16[32,1,512,128]{3,2,1,0:T(8,128)(2,1)} async-done(((bf16[32,1,512,128]{3,2,1,0:T(8,128)(2,1)}), bf16[32,1,512,128]{3,2,1,0:T(8,128)(2,1)}, u32[]{:S(2)}, u32[]{:S(2)}) %all-to-all-start.2) | async-done | bytes 4194336 | tf_op jit(solution)/shard_map/all_to_all | solution.py:147
  101.9 6.7 %all-to-all-start = ((bf16[32,1,512,128]{3,2,1,0:T(8,128)(2,1)}), bf16[32,1,512,128]{3,2,1,0:T(8,128)(2,1)}, u32[]{:S(2)}, u32[]{:S(2)}) async-start(bf16[32,1,512,128]{3,2,1,0:T(8,128)(2,1)} %fusion.1), calls=%async_computation | async-start | bytes 8388608 | tf_op jit(solution)/shard_map/all_to_all | solution.py:145
  117.9 2.8 gather_fusion.5
  120.7 40.7 %all-to-all-done = bf16[32,1,512,128]{3,2,1,0:T(8,128)(2,1)} async-done(((bf16[32,1,512,128]{3,2,1,0:T(8,128)(2,1)}), bf16[32,1,512,128]{3,2,1,0:T(8,128)(2,1)}, u32[]{:S(2)}, u32[]{:S(2)}) %all-to-all-start) | async-done | bytes 4194336 | tf_op jit(solution)/shard_map/all_to_all | solution.py:145
  161.4 2.8 gather_fusion.2
  164.5 1.4 copy.257
  165.9 2.9 collective-permute-start.1
  168.8 2.1 collective-permute-start
  174.9 6.2 %collective-permute-done.1 = bf16[4,8,8,8,256]{4,0,3,2,1:T(4,128)(2,1)S(1)} collective-permute-done((bf16[4,8,8,8,256]{4,0,3,2,1:T(4,128)(2,1)S(1)}, bf16[4,8,8,8,256]{4,0,3,2,1:T(4,128)(2,1)S(1)}, u32[]{:S(2)}, u32[]{:S(2)}) %collective-permute-start.1) | collective-permute-done | bytes 1048608 | tf_op jit(solution)/shard_map/ppermute | solution.py:19
  181.1 8.0 %collective-permute-done = bf16[4,8,8,8,256]{4,0,3,2,1:T(4,128)(2,1)S(1)} collective-permute-done((bf16[4,8,8,8,256]{4,0,3,2,1:T(4,128)(2,1)S(1)}, bf16[4,8,8,8,256]{4,0,3,2,1:T(4,128)(2,1)S(1)}, u32[]{:S(2)}, u32[]{:S(2)}) %collective-permute-start) | collective-permute-done | bytes 1048608 | tf_op jit(solution)/shard_map/ppermute | solution.py:18
  198.3 1.9 gather_fusion.31
  201.5 1.5 copy.302
  203.0 1.9 gather_fusion.29
  206.3 1.5 copy.299
  207.8 2.1 gather_fusion.28
  211.3 1.5 copy.297
  212.8 2.1 gather_fusion.26
  216.3 2.0 gather_fusion.25
  219.6 1.5 copy.294
  221.0 2.0 gather_fusion.23
  224.4 1.5 copy.284
  225.8 2.1 gather_fusion.22
  229.3 1.5 copy.282
  230.8 2.1 gather_fusion.20
  234.3 2.3 maximum_bitcast_fusion.2
  238.6 1.2 copy.278
  247.5 1.5 gather_fusion.30
  249.6 1.5 gather_fusion.24
  251.1 1.7 gather_fusion.21
  252.8 1.7 gather_fusion.16
  255.2 1.7 gather_fusion.10
  259.3 3.7 %pad_maximum_fusion.1 = (bf16[4,8,9,10,256]{4,3,2,1,0:T(8,128)(2,1)S(1)}, bf16[4,8,9,10,256]{4,3,2,1,0:T(8,128)(2,1)S(1)}) fusion(bf16[4,8,1,10,256]{4,3,2,1,0:T(8,128)(2,1)S(1)} %maximum_bitcast_fusion.8, bf16[4,8,8,1,256]{4,3,2,1,0:T(2,128)(2,1)S(1)} %copy.281, bf16[4,8,8,8,256]{4,3,2,1,0:T(8,128)(2,1)S(1)} %bitcast.383, ...), kind=kLoop, calls=%fused_computation.67 | loop fusion | flops 11796480 | bytes 4587520 | tf_op jit(solution)/shard_map/concatenate | solution.py:75
  264.1 3.7 %pad_maximum_fusion = (bf16[4,9,10,10,256]{4,3,2,1,0:T(8,128)(2,1)S(1)}, bf16[4,9,10,10,256]{4,3,2,1,0:T(8,128)(2,1)S(1)}) fusion(bf16[4,1,10,10,256]{4,3,2,1,0:T(8,128)(2,1)S(1)} %maximum_bitcast_fusion.6, bf16[4,8,1,10,256]{4,3,2,1,0:T(8,128)(2,1)S(1)} %maximum_bitcast_fusion.8, bf16[4,8,8,1,256]{4,3,2,1,0:T(2,128)(2,1)S(1)} %copy.281, ...), kind=kLoop, calls=%fused_computation.37 | loop fusion | flops 22118400 | bytes 5734400 | tf_op jit(solution)/shard_map/concatenate | solution.py:73
  267.9 2.1 fusion.97
  270.0 1.9 fusion.99
  272.6 2.4 fusion.96
  275.0 1.4 fusion.39
  276.4 1.3 convolution_add_fusion.25
  289.1 1.3 fusion.3
  (322 shorter events, 81.4 us)
Async XLA Ops:
  0.0 14.6 %copy-start = (bf16[8,512,128]{2,1,0:T(8,128)(2,1)S(1)}, bf16[8,512,128]{2,1,0:T(8,128)(2,1)}, u32[]{:S(2)}) copy-start(bf16[8,512,128]{2,1,0:T(8,128)(2,1)} %param.29) | copy-start | bytes 3145732
  3.2 26.4 %all-to-all-start.3 = ((s32[32,1,1]{2,1,0:T(1,128)}), s32[32,1,1]{2,1,0:T(1,128)S(1)}, u32[]{:S(2)}, u32[]{:S(2)}) async-start(s32[32,1,1]{2,1,0:T(1,128)} %copy.255), calls=%async_computation.3 | async-start | bytes 32768 | tf_op jit(solution)/shard_map/all_to_all | solution.py:148
  29.6 14.8 %all-to-all-start.1 = ((s32[32,1,1]{2,1,0:T(1,128)}), s32[32,1,1]{2,1,0:T(1,128)S(1)}, u32[]{:S(2)}, u32[]{:S(2)}) async-start(s32[32,1,1]{2,1,0:T(1,128)} %copy.251), calls=%async_computation.1 | async-start | bytes 32768 | tf_op jit(solution)/shard_map/all_to_all | solution.py:146
  44.4 57.5 %all-to-all-start.2 = ((bf16[32,1,512,128]{3,2,1,0:T(8,128)(2,1)}), bf16[32,1,512,128]{3,2,1,0:T(8,128)(2,1)}, u32[]{:S(2)}, u32[]{:S(2)}) async-start(bf16[32,1,512,128]{3,2,1,0:T(8,128)(2,1)} %fusion), calls=%async_computation.2 | async-start | bytes 8388608 | tf_op jit(solution)/shard_map/all_to_all | solution.py:147
  101.9 59.5 %all-to-all-start = ((bf16[32,1,512,128]{3,2,1,0:T(8,128)(2,1)}), bf16[32,1,512,128]{3,2,1,0:T(8,128)(2,1)}, u32[]{:S(2)}, u32[]{:S(2)}) async-start(bf16[32,1,512,128]{3,2,1,0:T(8,128)(2,1)} %fusion.1), calls=%async_computation | async-start | bytes 8388608 | tf_op jit(solution)/shard_map/all_to_all | solution.py:145
  165.9 15.2 %collective-permute-start.1 = (bf16[4,8,8,8,256]{4,0,3,2,1:T(4,128)(2,1)S(1)}, bf16[4,8,8,8,256]{4,0,3,2,1:T(4,128)(2,1)S(1)}, u32[]{:S(2)}, u32[]{:S(2)}) collective-permute-start(bf16[4,8,8,8,256]{4,0,3,2,1:T(4,128)(2,1)S(1)} %copy.257), channel_id=1, source_target_pairs={{1,0},{2,1},{3,2},{4,3},{5,4},{6,5},{7,6},{8,7},{9,8},{10,9},{11,1... | collective-permute-start | bytes 3145736 | tf_op jit(solution)/shard_map/ppermute | solution.py:19
  168.8 20.3 %collective-permute-start = (bf16[4,8,8,8,256]{4,0,3,2,1:T(4,128)(2,1)S(1)}, bf16[4,8,8,8,256]{4,0,3,2,1:T(4,128)(2,1)S(1)}, u32[]{:S(2)}, u32[]{:S(2)}) collective-permute-start(bf16[4,8,8,8,256]{4,0,3,2,1:T(4,128)(2,1)S(1)} %copy.257), channel_id=1, source_target_pairs={{0,1},{1,2},{2,3},{3,4},{4,5},{5,6},{6,7},{7,8},{8,9},{9,10},{10,1... | collective-permute-start | bytes 3145736 | tf_op jit(solution)/shard_map/ppermute | solution.py:18
  236.6 4.2 %copy-start.13 = (bf16[12,8,256]{2,0,1:T(8,128)(2,1)S(1)}, bf16[12,8,256]{2,0,1:T(8,128)(2,1)}, u32[]{:S(2)}) copy-start(bf16[12,8,256]{2,0,1:T(8,128)(2,1)} %get-tuple-element.124) | copy-start | bytes 147460
  236.6 4.9 %copy-start.31 = (pred[4]{0:T(512)(128)(4,1)S(1)}, pred[4]{0:T(512)(128)(4,1)}, u32[]{:S(2)}) copy-start(pred[4]{0:T(512)(128)(4,1)} %get-tuple-element.29) | copy-start | bytes 16
  236.6 4.9 %copy-start.47 = (pred[4]{0:T(512)(128)(4,1)S(1)}, pred[4]{0:T(512)(128)(4,1)}, u32[]{:S(2)}) copy-start(pred[4]{0:T(512)(128)(4,1)} %get-tuple-element.170) | copy-start | bytes 16
  236.6 5.0 %copy-start.12 = (bf16[12,8,256]{2,0,1:T(8,128)(2,1)S(1)}, bf16[12,8,256]{2,0,1:T(8,128)(2,1)}, u32[]{:S(2)}) copy-start(bf16[12,8,256]{2,0,1:T(8,128)(2,1)} %get-tuple-element.123) | copy-start | bytes 147460
  236.7 5.7 %copy-start.30 = (pred[4]{0:T(512)(128)(4,1)S(1)}, pred[4]{0:T(512)(128)(4,1)}, u32[]{:S(2)}) copy-start(pred[4]{0:T(512)(128)(4,1)} %get-tuple-element.31) | copy-start | bytes 16
  236.7 5.7 %copy-start.46 = (pred[4]{0:T(512)(128)(4,1)S(1)}, pred[4]{0:T(512)(128)(4,1)}, u32[]{:S(2)}) copy-start(pred[4]{0:T(512)(128)(4,1)} %get-tuple-element.172) | copy-start | bytes 16
  236.7 5.8 %copy-start.19 = (bf16[12,256]{1,0:T(8,128)(2,1)S(1)}, bf16[12,256]{1,0:T(8,128)(2,1)}, u32[]{:S(2)}) copy-start(bf16[12,256]{1,0:T(8,128)(2,1)} %get-tuple-element.116) | copy-start | bytes 18436
  236.7 6.5 %copy-start.37 = (pred[4]{0:T(512)(128)(4,1)S(1)}, pred[4]{0:T(512)(128)(4,1)}, u32[]{:S(2)}) copy-start(pred[4]{0:T(512)(128)(4,1)} %get-tuple-element.32) | copy-start | bytes 16
  236.7 6.5 %copy-start.56 = (pred[4]{0:T(512)(128)(4,1)S(1)}, pred[4]{0:T(512)(128)(4,1)}, u32[]{:S(2)}) copy-start(pred[4]{0:T(512)(128)(4,1)} %get-tuple-element.173) | copy-start | bytes 16
  236.7 6.6 %copy-start.11 = (bf16[12,8,256]{2,0,1:T(8,128)(2,1)S(1)}, bf16[12,8,256]{2,0,1:T(8,128)(2,1)}, u32[]{:S(2)}) copy-start(bf16[12,8,256]{2,0,1:T(8,128)(2,1)} %get-tuple-element.120) | copy-start | bytes 147460
  236.7 6.6 %copy-start.18 = (bf16[12,256]{1,0:T(8,128)(2,1)S(1)}, bf16[12,256]{1,0:T(8,128)(2,1)}, u32[]{:S(2)}) copy-start(bf16[12,256]{1,0:T(8,128)(2,1)} %get-tuple-element.117) | copy-start | bytes 18436
  236.7 7.3 %copy-start.53 = (pred[4]{0:T(512)(128)(4,1)S(1)}, pred[4]{0:T(512)(128)(4,1)}, u32[]{:S(2)}) copy-start(pred[4]{0:T(512)(128)(4,1)} %get-tuple-element.61) | copy-start | bytes 16
  236.7 7.3 %copy-start.55 = (pred[4]{0:T(512)(128)(4,1)S(1)}, pred[4]{0:T(512)(128)(4,1)}, u32[]{:S(2)}) copy-start(pred[4]{0:T(512)(128)(4,1)} %get-tuple-element.175) | copy-start | bytes 16
  236.7 7.4 %copy-start.10 = (bf16[12,8,256]{2,0,1:T(8,128)(2,1)S(1)}, bf16[12,8,256]{2,0,1:T(8,128)(2,1)}, u32[]{:S(2)}) copy-start(bf16[12,8,256]{2,0,1:T(8,128)(2,1)} %get-tuple-element.122) | copy-start | bytes 147460
  236.8 8.1 %copy-start.36 = (pred[4]{0:T(512)(128)(4,1)S(1)}, pred[4]{0:T(512)(128)(4,1)}, u32[]{:S(2)}) copy-start(pred[4]{0:T(512)(128)(4,1)} %get-tuple-element.62) | copy-start | bytes 16
  236.8 8.1 %copy-start.50 = (pred[4]{0:T(512)(128)(4,1)S(1)}, pred[4]{0:T(512)(128)(4,1)}, u32[]{:S(2)}) copy-start(pred[4]{0:T(512)(128)(4,1)} %get-tuple-element.176) | copy-start | bytes 16
  236.8 8.2 %copy-start.9 = (bf16[12,8,256]{2,0,1:T(8,128)(2,1)S(1)}, bf16[12,8,256]{2,0,1:T(8,128)(2,1)}, u32[]{:S(2)}) copy-start(bf16[12,8,256]{2,0,1:T(8,128)(2,1)} %get-tuple-element.121) | copy-start | bytes 147460
  236.8 8.9 %copy-start.35 = (pred[4]{0:T(512)(128)(4,1)S(1)}, pred[4]{0:T(512)(128)(4,1)}, u32[]{:S(2)}) copy-start(pred[4]{0:T(512)(128)(4,1)} %get-tuple-element.64) | copy-start | bytes 16
  236.8 8.9 %copy-start.49 = (pred[4]{0:T(512)(128)(4,1)S(1)}, pred[4]{0:T(512)(128)(4,1)}, u32[]{:S(2)}) copy-start(pred[4]{0:T(512)(128)(4,1)} %get-tuple-element.178) | copy-start | bytes 16
  236.8 9.7 %copy-start.52 = (pred[4]{0:T(512)(128)(4,1)S(1)}, pred[4]{0:T(512)(128)(4,1)}, u32[]{:S(2)}) copy-start(pred[4]{0:T(512)(128)(4,1)} %get-tuple-element.65) | copy-start | bytes 16
  236.8 9.7 %copy-start.54 = (pred[4]{0:T(512)(128)(4,1)S(1)}, pred[4]{0:T(512)(128)(4,1)}, u32[]{:S(2)}) copy-start(pred[4]{0:T(512)(128)(4,1)} %get-tuple-element.179) | copy-start | bytes 16
  236.8 9.8 %copy-start.8 = (bf16[12,8,256]{2,0,1:T(8,128)(2,1)S(1)}, bf16[12,8,256]{2,0,1:T(8,128)(2,1)}, u32[]{:S(2)}) copy-start(bf16[12,8,256]{2,0,1:T(8,128)(2,1)} %get-tuple-element.119) | copy-start | bytes 147460
  236.8 10.5 %copy-start.51 = (pred[4]{0:T(512)(128)(4,1)S(1)}, pred[4]{0:T(512)(128)(4,1)}, u32[]{:S(2)}) copy-start(pred[4]{0:T(512)(128)(4,1)} %get-tuple-element.60) | copy-start | bytes 16
  236.8 10.5 %copy-start.57 = (pred[4]{0:T(512)(128)(4,1)S(1)}, pred[4]{0:T(512)(128)(4,1)}, u32[]{:S(2)}) copy-start(pred[4]{0:T(512)(128)(4,1)} %compare_and_fusion.25) | copy-start | bytes 16
  248.9 9.6 %copy-start.29 = (pred[4]{0:T(512)(128)(4,1)S(1)}, pred[4]{0:T(512)(128)(4,1)}, u32[]{:S(2)}) copy-start(pred[4]{0:T(512)(128)(4,1)} %get-tuple-element.25) | copy-start | bytes 16
  248.9 9.6 %copy-start.41 = (pred[4]{0:T(512)(128)(4,1)S(1)}, pred[4]{0:T(512)(128)(4,1)}, u32[]{:S(2)}) copy-start(pred[4]{0:T(512)(128)(4,1)} %get-tuple-element.166) | copy-start | bytes 16
  251.1 7.5 %copy-start.14 = (bf16[4,8,1,1,256]{4,3,1,0,2:T(2,128)(2,1)S(1)}, bf16[4,8,1,1,256]{4,3,1,0,2:T(2,128)(2,1)}, u32[]{:S(2)}) copy-start(bf16[4,8,1,1,256]{4,3,1,0,2:T(2,128)(2,1)} %copy.286) | copy-start | bytes 49156
  251.1 7.5 %copy-start.15 = (bf16[4,8,1,1,256]{4,3,1,0,2:T(2,128)(2,1)S(1)}, bf16[4,8,1,1,256]{4,3,1,0,2:T(2,128)(2,1)}, u32[]{:S(2)}) copy-start(bf16[4,8,1,1,256]{4,3,1,0,2:T(2,128)(2,1)} %copy.285) | copy-start | bytes 49156
  254.5 4.3 %copy-start.28 = (pred[4]{0:T(512)(128)(4,1)S(1)}, pred[4]{0:T(512)(128)(4,1)}, u32[]{:S(2)}) copy-start(pred[4]{0:T(512)(128)(4,1)} %get-tuple-element.30) | copy-start | bytes 16
  254.5 4.3 %copy-start.42 = (pred[4]{0:T(512)(128)(4,1)S(1)}, pred[4]{0:T(512)(128)(4,1)}, u32[]{:S(2)}) copy-start(pred[4]{0:T(512)(128)(4,1)} %get-tuple-element.171) | copy-start | bytes 16
  259.2 4.1 %copy-start.25 = (pred[4]{0:T(512)(128)(4,1)S(1)}, pred[4]{0:T(512)(128)(4,1)}, u32[]{:S(2)}) copy-start(pred[4]{0:T(512)(128)(4,1)} %get-tuple-element.22) | copy-start | bytes 16
  259.2 4.2 %copy-start.22 = (bf16[4,1,1,1,256]{4,3,0,2,1:T(2,128)(2,1)S(1)}, bf16[4,1,1,1,256]{4,3,0,2,1:T(2,128)(2,1)}, u32[]{:S(2)}) copy-start(bf16[4,1,1,1,256]{4,3,0,2,1:T(2,128)(2,1)} %copy.296) | copy-start | bytes 6148
  259.2 4.2 %copy-start.23 = (bf16[4,1,1,1,256]{4,3,0,2,1:T(2,128)(2,1)S(1)}, bf16[4,1,1,1,256]{4,3,0,2,1:T(2,128)(2,1)}, u32[]{:S(2)}) copy-start(bf16[4,1,1,1,256]{4,3,0,2,1:T(2,128)(2,1)} %copy.295) | copy-start | bytes 6148
  259.2 4.2 %copy-start.24 = (pred[4]{0:T(512)(128)(4,1)S(1)}, pred[4]{0:T(512)(128)(4,1)}, u32[]{:S(2)}) copy-start(pred[4]{0:T(512)(128)(4,1)} %get-tuple-element.33) | copy-start | bytes 16
  259.2 4.2 %copy-start.43 = (pred[4]{0:T(512)(128)(4,1)S(1)}, pred[4]{0:T(512)(128)(4,1)}, u32[]{:S(2)}) copy-start(pred[4]{0:T(512)(128)(4,1)} %get-tuple-element.174) | copy-start | bytes 16
  259.2 4.3 %copy-start.34 = (pred[4]{0:T(512)(128)(4,1)S(1)}, pred[4]{0:T(512)(128)(4,1)}, u32[]{:S(2)}) copy-start(pred[4]{0:T(512)(128)(4,1)} %get-tuple-element.63) | copy-start | bytes 16
  259.2 4.3 %copy-start.45 = (pred[4]{0:T(512)(128)(4,1)S(1)}, pred[4]{0:T(512)(128)(4,1)}, u32[]{:S(2)}) copy-start(pred[4]{0:T(512)(128)(4,1)} %get-tuple-element.177) | copy-start | bytes 16
  259.2 4.4 %copy-start.33 = (pred[4]{0:T(512)(128)(4,1)S(1)}, pred[4]{0:T(512)(128)(4,1)}, u32[]{:S(2)}) copy-start(pred[4]{0:T(512)(128)(4,1)} %get-tuple-element.66) | copy-start | bytes 16
  259.2 4.4 %copy-start.44 = (pred[4]{0:T(512)(128)(4,1)S(1)}, pred[4]{0:T(512)(128)(4,1)}, u32[]{:S(2)}) copy-start(pred[4]{0:T(512)(128)(4,1)} %get-tuple-element.180) | copy-start | bytes 16
  259.3 4.5 %copy-start.16 = (bf16[4,1,8,1,256]{4,3,2,0,1:T(2,128)(2,1)S(1)}, bf16[4,1,8,1,256]{4,3,2,0,1:T(2,128)(2,1)}, u32[]{:S(2)}) copy-start(bf16[4,1,8,1,256]{4,3,2,0,1:T(2,128)(2,1)} %copy.301) | copy-start | bytes 49156
  259.3 4.5 %copy-start.17 = (bf16[4,1,8,1,256]{4,3,2,0,1:T(2,128)(2,1)S(1)}, bf16[4,1,8,1,256]{4,3,2,0,1:T(2,128)(2,1)}, u32[]{:S(2)}) copy-start(bf16[4,1,8,1,256]{4,3,2,0,1:T(2,128)(2,1)} %copy.300) | copy-start | bytes 49156
  (16 other events, 51.4 us)
where the time goes:
time: 293 us; the launch traced here: 290 us
  waiting for transfers between devices  97.4 us (33%)
  local copies, waits for them, and re-layouts  81.9 us (28%)
  other arithmetic  62.6 us (21%)
  starting transfers between devices  32.1 us (11%)
  matrix products  14.8 us (5%)
    all_to_all x1, waiting for transfers between devices, per_device(): lax.all_to_all(child_buffer, 'gy', split_axis=0, concat_axis=0, tiled=True)  40.7 us
    all_to_all x1, waiting for transfers between devices, per_device(): lax.all_to_all(skip_buffer, 'gy', split_axis=0, concat_axis=0, tiled=True)  38.4 us
    gather x26, local copies, waits for them, and re-layouts, assemble(): picked = jnp.take(surface, jnp.maximum(column, 0), axis=0)  32.8 us
    another operation x26, local copies, waits for them, and re-layouts, assemble(): picked = jnp.take(surface, jnp.maximum(column, 0), axis=0)  18.1 us
    gather x30, other arithmetic  15.5 us
    dot_general x27, matrix products, convolve(): jnp.dot(window, conv_weight[tap_index], preferred_element_type=jnp.float32)  14.3 us
    reshape x2, other arithmetic, pack_rows(): gathered.reshape((gy_count, capacity) + payload.shape[1:])  9.38 us
    select_n x26, other arithmetic, assemble(): jnp.where((column >= 0)[:, None, None, None, None], picked, jnp.zeros((),...  8.25 us
  transfers between devices with their start and end apart: 6, of which 5 were waited for; matrix products, arithmetic and copies ran while one was open for 18% of the time, Pallas kernels for 0%

commit v1 on v0

v1 whole, which is shorter than its diff:
```python
import jax
import jax.numpy as jnp
from jax import lax
from jax.experimental import pallas as pl
from jax.experimental.pallas import tpu as pltpu
from jax.sharding import PartitionSpec as P

LINES, COLUMNS = 4, 8
SLOTS, BRICKS = 8, 4
SKIP_ROWS, PARENT_ROWS, HEAD_ROWS = 512, 128, 16
BODY = SKIP_ROWS + PARENT_ROWS
DEPTH = 2
PIECES = ((SKIP_ROWS, 0, 0), (PARENT_ROWS, SKIP_ROWS, SKIP_ROWS * DEPTH))
BF16, F32, I32 = jnp.bfloat16, jnp.float32, jnp.int32

ANY = pl.BlockSpec(memory_space=pl.ANY)
SMEM = pl.BlockSpec(memory_space=pltpu.SMEM)
VMEM = pl.BlockSpec(memory_space=pltpu.VMEM)


def rows_of(shape, values):
    row = lax.broadcasted_iota(I32, shape, 0)
    out = jnp.full(shape, -1, I32)
    for j, value in enumerate(values):
        out = jnp.where(row == j, value, out)
    return out


def first_kernel(parent_dest, skip_dest, base, parents, skip, out, slot_of, sems):
    for q in range(2 * COLUMNS + 1):
        slot_of[q] = 0
    table = []
    for kind, dest in enumerate((skip_dest, parent_dest)):
        for s in range(SLOTS):
            d = dest[s]
            local = jnp.where(d >= 0, d - base[0], -1)
            table.append(local)
            column = lax.rem(lax.div(jnp.maximum(local, 0), BRICKS), COLUMNS)
            slot_of[jnp.where(d >= 0, kind * COLUMNS + column, 2 * COLUMNS)] = s
    copies = []
    for q in range(COLUMNS):
        s, p = slot_of[q], slot_of[COLUMNS + q]
        copies.append(pltpu.make_async_copy(skip.at[s], out.at[q, 0:512], sems.at[q, 0]))
        for half in range(2):
            copies.append(
                pltpu.make_async_copy(
                    parents.at[p, :, 128 * half : 128 * half + 128],
                    out.at[q, 512 + 64 * half : 576 + 64 * half],
                    sems.at[q, 1 + half],
                )
            )
    for copy in copies:
        copy.start()
    header = rows_of((HEAD_ROWS, 128), table).astype(F32).astype(BF16)
    for q in range(COLUMNS):
        out[q, BODY : BODY + HEAD_ROWS] = header
    for copy in copies:
        copy.wait()


def first_pack(parent_dest, skip_dest, base, parents, skip):
    return pl.pallas_call(
        first_kernel,
        out_shape=jax.ShapeDtypeStruct((COLUMNS, BODY + HEAD_ROWS, 128), BF16),
        in_specs=[SMEM, SMEM, SMEM, ANY, ANY],
        out_specs=VMEM,
        scratch_shapes=[
            pltpu.SMEM((2 * COLUMNS + 1,), I32),
            pltpu.SemaphoreType.DMA((COLUMNS, 3)),
        ],
        compiler_params=pltpu.CompilerParams(vmem_limit_bytes=16 * 2**20),
    )(parent_dest, skip_dest, base, parents, skip)


def second_kernel(place, came, *refs):
    outs = refs[:LINES]
    found, table, counts, source, landing, sem = refs[LINES:]
    line, column = place[0], place[1]
    for j in range(2 * LINES + 1):
        counts[j] = 0
    for j in range(2 * LINES * DEPTH + 1):
        source[j] = 0
        landing[j] = -1
    lane = lax.broadcasted_iota(I32, (COLUMNS, SLOTS, 128), 2)
    over = jnp.zeros((1, 128), I32)
    picks = []
    every = came[:, BODY : BODY + HEAD_ROWS].astype(F32).astype(I32)
    for kind in range(2):
        dest = every[:, kind * SLOTS : kind * SLOTS + SLOTS]
        live = dest >= 0
        owner = dest >> 2
        its_column = owner & 7
        mine = jnp.where(live & (its_column == column), dest, -1)
        picks.append(jnp.max(mine, axis=1))
        to_column = jnp.where(live & (its_column == lane), 1, 0)
        over = over | jnp.where(
            jnp.max(jnp.sum(to_column, axis=1), axis=0, keepdims=True) > 1, 1, 0
        )
        to_owner = jnp.where(live & (owner == lane), 1, 0)
        total = jnp.sum(jnp.sum(to_owner, axis=1), axis=0, keepdims=True)
        over = over | jnp.where(total > DEPTH, 1, 0)
    flag = jnp.max(over.astype(F32), axis=1, keepdims=True).astype(I32)
    lane = lax.broadcasted_iota(I32, (COLUMNS, 128), 1)
    found[...] = jnp.where(lane == 0, picks[0], picks[1])
    copy = pltpu.make_async_copy(found, table, sem)
    copy.start()
    copy.wait()
    for kind in range(2):
        for m in range(COLUMNS):
            dest = table[m, kind]
            live = dest >= 0
            to_line = jnp.where(live, dest >> 5, 0)
            count_at = jnp.where(live, kind * LINES + to_line, 2 * LINES)
            rank = counts[count_at]
            counts[count_at] = rank + 1
            spot = jnp.where(
                live & (rank < DEPTH),
                (kind * LINES + to_line) * DEPTH + rank,
                2 * LINES * DEPTH,
            )
            source[spot] = m
            landing[spot] = dest & 3
    for k in range(LINES):
        to_line = lax.rem(line + k, LINES)
        spots = []
        for kind, (rows, first, height) in enumerate(PIECES):
            for r in range(DEPTH):
                spot = (kind * LINES + to_line) * DEPTH + r
                spots.append(landing[spot])
                outs[k][height + r * rows : height + r * rows + rows] = came[
                    source[spot], first : first + rows
                ]
        outs[k][BODY * DEPTH : BODY * DEPTH + HEAD_ROWS] = (
            rows_of((HEAD_ROWS, 128), spots + [flag]).astype(F32).astype(BF16)
        )


def second_pack(place, came):
    message = jax.ShapeDtypeStruct((BODY * DEPTH + HEAD_ROWS, 128), BF16)
    return pl.pallas_call(
        second_kernel,
        out_shape=[message] * LINES,
        in_specs=[SMEM, VMEM],
        out_specs=[VMEM] * LINES,
        scratch_shapes=[
            pltpu.VMEM((COLUMNS, 128), I32),
            pltpu.SMEM((COLUMNS, 128), I32),
            pltpu.SMEM((2 * LINES + 1,), I32),
            pltpu.SMEM((2 * LINES * DEPTH + 1,), I32),
            pltpu.SMEM((2 * LINES * DEPTH + 1,), I32),
            pltpu.SemaphoreType.DMA,
        ],
        compiler_params=pltpu.CompilerParams(vmem_limit_bytes=16 * 2**20),
    )(place, came)


def unpack_kernel(*refs):
    came = refs[:LINES]
    own, flag_out, found, table, sem = refs[LINES:]
    lane = lax.broadcasted_iota(I32, (HEAD_ROWS, 128), 1)
    row = lax.broadcasted_iota(I32, (HEAD_ROWS, 128), 0)
    for k in range(LINES):
        header = came[k][BODY * DEPTH : BODY * DEPTH + HEAD_ROWS].astype(F32)
        found[k : k + 1] = jnp.sum(
            jnp.where(lane == row, header, 0.0), axis=0, keepdims=True
        ).astype(I32)
    found[LINES:8] = jnp.zeros((8 - LINES, 128), I32)
    copy = pltpu.make_async_copy(found, table, sem)
    copy.start()
    copy.wait()
    flag = table[0, 2 * DEPTH]
    for k in range(1, LINES):
        flag = flag | table[k, 2 * DEPTH]
    flag_out[0] = flag
    for k in range(LINES):
        for kind, (rows, first, height) in enumerate(PIECES):
            for r in range(DEPTH):
                brick = table[k, kind * DEPTH + r]

                @pl.when(brick >= 0)
                def _(k=k, rows=rows, first=first, at=height + r * rows, brick=brick):
                    own[brick, first : first + rows] = came[k][at : at + rows]


def unpack(messages):
    return pl.pallas_call(
        unpack_kernel,
        out_shape=[
            jax.ShapeDtypeStruct((BRICKS, BODY, 128), BF16),
            jax.ShapeDtypeStruct((1,), I32),
        ],
        in_specs=[VMEM] * LINES,
        out_specs=[VMEM, SMEM],
        scratch_shapes=[
            pltpu.VMEM((8, 128), I32),
            pltpu.SMEM((8, 128), I32),
            pltpu.SemaphoreType.DMA,
        ],
        compiler_params=pltpu.CompilerParams(vmem_limit_bytes=16 * 2**20),
    )(*messages)


def dense_route(parents, parent_dest, skip, skip_dest):
    halves = parents.reshape(SLOTS, 64, 2, 128).transpose(0, 2, 1, 3).reshape(SLOTS, 128, 128)
    joined = []
    for dest, payload in ((skip_dest, skip), (parent_dest, halves)):
        devices = LINES * COLUMNS
        owner = jnp.where(dest >= 0, dest // BRICKS % devices, -1)
        match = owner[None, :] == jnp.arange(devices)[:, None]
        spot = jnp.sum(jnp.where(match, dest % BRICKS + 1, 0), axis=1) - 1
        rows = jnp.einsum(
            "os,src->orc", match.astype(BF16), payload, preferred_element_type=F32
        ).astype(BF16)
        rows = lax.all_to_all(rows, "gy", 0, 0, tiled=True)
        spot = lax.all_to_all(spot, "gy", 0, 0, tiled=True)
        pick = spot[None, :] == jnp.arange(BRICKS)[:, None]
        joined.append(
            jnp.einsum(
                "bo,orc->brc", pick.astype(BF16), rows, preferred_element_type=F32
            ).astype(BF16)
        )
    return jnp.concatenate(joined, axis=1)


def conv_kernel(
    lookup, before, own, after, up_weight, conv_weight, out, pool, shifted, window
):
    row = lax.broadcasted_iota(I32, (256, 64), 0)
    column = lax.broadcasted_iota(I32, (256, 64), 1)
    in_brick = row & 127
    takes = (in_brick >> 3) * 4 + ((in_brick & 7) >> 1) == column
    spread = jnp.where(takes & ((row & 1) == (row >> 7)), 1.0, 0.0).astype(BF16)
    for group, bricks in enumerate((before, own, after)):
        spaced = []
        for b in range(BRICKS):
            pool[group * BRICKS + b, :, :, :, 128:256] = (
                bricks[b, 0:512].astype(F32).reshape(8, 8, 8, 128)
            )
            halves = [
                jnp.dot(
                    spread, bricks[b, 512 + 64 * h : 576 + 64 * h], preferred_element_type=F32
                ).astype(BF16)
                for h in range(2)
            ]
            spaced.append(
                jnp.concatenate(
                    [halves[0][:128], halves[1][:128], halves[0][128:], halves[1][128:]], axis=1
                )
            )
        spaced = jnp.concatenate(spaced, axis=0)
        for ab in range(4):
            made = jnp.dot(spaced, up_weight[ab], preferred_element_type=F32)
            made = made.astype(BF16).astype(F32).reshape(BRICKS, 4, 4, 8, 128)
            for b in range(BRICKS):
                for i in range(4):
                    for j in range(4):
                        pool[
                            group * BRICKS + b, 2 * i + ab // 2, 2 * j + ab % 2, :, 0:128
                        ] = made[b, i, j]
    pool[3 * BRICKS] = jnp.zeros((8, 8, 8, 256), F32)

    spans = {-1: (slice(7, 8), slice(0, 1)), 0: (slice(0, 8), slice(1, 9)), 1: (slice(0, 1), slice(9, 10))}

    @pl.loop(0, BRICKS)
    def _(b):
        for off_x in (-1, 0, 1):
            for off_y in (-1, 0, 1):
                from_x, to_x = spans[off_x]
                from_y, to_y = spans[off_y]
                line = []
                for off_z in (-1, 0, 1):
                    code = (off_x + 1) * 9 + (off_y + 1) * 3 + off_z + 1
                    brick = BRICKS + b if code == 13 else lookup[b * 26 + code - (code > 13)]
                    line.append(pool[brick, from_x, from_y])
                z = lax.broadcasted_iota(I32, line[1].shape, 2)
                shifted[0, to_x, to_y] = pltpu.roll(jnp.where(z == 7, line[0], line[1]), 1, 2)
                shifted[1, to_x, to_y] = line[1]
                shifted[2, to_x, to_y] = pltpu.roll(jnp.where(z == 0, line[2], line[1]), 7, 2)
        for step_y in range(3):
            for step_z in range(3):
                first = (step_y * 3 + step_z) * 256
                window[:, first : first + 256] = (
                    shifted[step_z, :, step_y : step_y + 8].reshape(640, 256).astype(BF16)
                )
        total = jnp.dot(window[0:512], conv_weight[0], preferred_element_type=F32)
        for step_x in (1, 2):
            total += jnp.dot(
                window[64 * step_x : 64 * step_x + 512],
                conv_weight[step_x],
                preferred_element_type=F32,
            )
        out[b] = jnp.maximum(total, 0.0).astype(BF16)


def refine(lookup, before, own, after, up_weight, conv_weight):
    return pl.pallas_call(
        conv_kernel,
        out_shape=jax.ShapeDtypeStruct((BRICKS, 512, 128), BF16),
        in_specs=[SMEM] + [VMEM] * 5,
        out_specs=VMEM,
        scratch_shapes=[
            pltpu.VMEM((3 * BRICKS + 1, 8, 8, 8, 256), F32),
            pltpu.VMEM((3, 10, 10, 8, 256), F32),
            pltpu.VMEM((640, 9 * 256), BF16),
        ],
        compiler_params=pltpu.CompilerParams(vmem_limit_bytes=48 * 2**20),
    )(lookup, before, own, after, up_weight, conv_weight)


def per_device(parents, parent_dest, skip, skip_dest, neighbours, up_weight, conv_weight):
    row, inner = lax.axis_index("gx"), lax.axis_index("gy")
    devices = LINES * COLUMNS
    base = (row * devices * BRICKS).reshape(1)
    place = jnp.stack([inner // COLUMNS, inner % COLUMNS])
    groups = [[x * COLUMNS + q for q in range(COLUMNS)] for x in range(LINES)]
    first = first_pack(parent_dest, skip_dest, base, parents, skip)
    came = lax.all_to_all(first, "gy", 0, 0, tiled=True, axis_index_groups=groups)
    messages = second_pack(place, came)
    arrived = [messages[0]] + [
        lax.ppermute(
            messages[k], "gy", [(i, (i + k * COLUMNS) % devices) for i in range(devices)]
        )
        for k in range(1, LINES)
    ]
    own, flag = unpack(arrived)
    own, _ = lax.while_loop(
        lambda state: state[1][0] > 0,
        lambda state: (
            dense_route(parents, parent_dest, skip, skip_dest),
            jnp.zeros_like(state[1]),
        ),
        (own, flag),
    )
    whole = lax.axis_size(("gx", "gy"))
    up = [(i, i + 1) for i in range(whole - 1)]
    before = lax.ppermute(own, ("gx", "gy"), up)
    after = lax.ppermute(own, ("gx", "gy"), [(j, i) for i, j in up])
    me = row * devices + inner
    lookup = jnp.where(neighbours >= 0, neighbours - (me - 1) * BRICKS, 3 * BRICKS)
    return refine(
        lookup.reshape(-1),
        before,
        own,
        after,
        up_weight.reshape(4, 512, 128),
        conv_weight.reshape(3, 9 * 256, 128),
    )


def solution(mesh):
    placed = (
        P(("gx", "gy"), None, None),
        P(("gx", "gy")),
        P(("gx", "gy"), None, None),
        P(("gx", "gy")),
        P(("gx", "gy"), None),
        P(),
        P(),
    )
    return jax.shard_map(
        per_device,
        mesh=mesh,
        in_specs=placed,
        out_specs=P(("gx", "gy"), None, None),
        check_vma=False,
    )
```

time: 293 us -> 87.4 us (0.30)
  local copies, waits for them, and re-layouts: 81.9 us -> 6.65 us
  other arithmetic: 62.6 us -> 0.08 us
  waiting for transfers between devices: 97.4 us -> 38 us
  Pallas kernels: 0 us -> 19.2 us
  matrix products: 14.8 us -> 0 us
  starting transfers between devices: 32.1 us -> 21.2 us
    all_to_all x4 -> x1, waiting for transfers between devices: 83.2 us -> 19.1 us  [per_device(): lax.all_to_all(first, 'gy', 0, 0, tiled=True, axis_index_groups=groups)]
    gather x32 -> x0, local copies, waits for them, and re-layouts: 46 us -> none  [the longest x26 32.8 us: assemble(): picked = jnp.take(surface, jnp.maximum(column, 0), axis=0)]
    all_to_all x4 -> x1, starting transfers between devices: 27.1 us -> 5.46 us  [per_device(): lax.all_to_all(first, 'gy', 0, 0, tiled=True, axis_index_groups=groups)]
    pallas_call x0 -> x4, Pallas kernels: none -> 19.2 us  [the longest x1 12.2 us: refine(): pl.pallas_call(conv_kernel, out_shape=jax.ShapeDtypeStruct((BRICKS, 512,...]
    another operation x26 -> x0, local copies, waits for them, and re-layouts: 18.1 us -> none  [assemble(): picked = jnp.take(surface, jnp.maximum(column, 0), axis=0)]
    gather x30 -> x0, other arithmetic: 15.5 us -> none
    dot_general x28 -> x0, matrix products: 14.8 us -> none  [the longest x27 14.3 us: convolve(): jnp.dot(window, conv_weight[tap_index], preferred_element_type=jnp.float32)]
    select_n x50 -> x1, other arithmetic: 11.9 us -> 0.01 us  [per_device(): jnp.where(neighbours >= 0, neighbours - (me - 1) * BRICKS, 3 * BRICKS)]
  transfers between devices with their start and end apart: 6 -> 6, of which waited for: 5 -> 5; matrix products, arithmetic and copies ran while one was open for 18% -> 2% of each run, Pallas kernels for 0% -> 0%
where the time goes in v1:
time: 87.4 us; the launch traced here: 86.3 us
  waiting for transfers between devices  38 us (43%)
  starting transfers between devices  21.2 us (24%)
  Pallas kernels  19.2 us (22%)
  local copies, waits for them, and re-layouts  6.65 us (8%)
  loops' own time  0.96 us (1%)
    all_to_all x1, waiting for transfers between devices, per_device(): lax.all_to_all(first, 'gy', 0, 0, tiled=True, axis_index_groups=groups)  19.1 us
    pallas_call x1, Pallas kernels, refine(): pl.pallas_call(conv_kernel, out_shape=jax.ShapeDtypeStruct((BRICKS, 512,...  12.2 us
    ppermute x3, waiting for transfers between devices, per_device(): lax.ppermute(messages[k], 'gy', [(i, (i + k * COLUMNS) % devices) for i i...  11.2 us
    ppermute x1, starting transfers between devices, per_device(): after = lax.ppermute(own, ('gx', 'gy'), [(j, i) for i, j in up])  8.08 us
    ppermute x1, waiting for transfers between devices, per_device(): before = lax.ppermute(own, ('gx', 'gy'), up)  5.99 us
    ppermute x3, starting transfers between devices, per_device(): lax.ppermute(messages[k], 'gy', [(i, (i + k * COLUMNS) % devices) for i i...  5.72 us
    all_to_all x1, starting transfers between devices, per_device(): lax.all_to_all(first, 'gy', 0, 0, tiled=True, axis_index_groups=groups)  5.46 us
    pallas_call x1, Pallas kernels, first_pack(): pl.pallas_call(first_kernel, out_shape=jax.ShapeDtypeStruct((COLUMNS, BOD...  4.32 us
  transfers between devices with their start and end apart: 6, of which 5 were waited for; matrix products, arithmetic and copies ran while one was open for 2% of the time, Pallas kernels for 0%

profile of v1, /device:TPU:16, one launch (start us, length us, event | category | flops | bytes accessed | tf_op | source)
XLA Modules:
  0.0 86.3 jit_solution(5240192636360184889)
XLA Ops:
  0.0 0.0 copy-start
  0.0 1.2 %copy-done = bf16[8,512,128]{2,1,0:T(8,128)(2,1)S(1)} copy-done((bf16[8,512,128]{2,1,0:T(8,128)(2,1)S(1)}, bf16[8,512,128]{2,1,0:T(8,128)(2,1)}, u32[]{:S(2)}) %copy-start) | copy-done | bytes 1048600
  1.2 0.0 copy-start.1
  1.2 4.3 %shard_map.73 = bf16[8,656,128]{2,1,0:T(8,128)(2,1)} custom-call(s32[8]{0:T(128)} %parent_dest.1, s32[8]{0:T(128)} %skip_dest.1, s32[1]{0:T(128)} %bitcast.12.base, bf16[8,64,256]{2,1,0:T(8,128)(2,1)} %parents.1, bf16[8,512,128]{2,1,0:T(8,128)(2,1)S(1)} %copy-done), custom_call_target="tpu_custom_call" | custom-call | tf_op jit(solution)/shard_map/pallas_call | solution.py:62
  5.6 0.0 copy-start.4
  5.6 0.0 copy-start.6
  5.6 0.0 copy-start.7
  5.6 5.5 %all-to-all-start.4 = ((bf16[8,656,128]{2,1,0:T(8,128)(2,1)}), bf16[8,656,128]{2,1,0:T(8,128)(2,1)S(1)}, u32[]{:S(2)}, u32[]{:S(2)}) async-start(bf16[8,656,128]{2,1,0:T(8,128)(2,1)} %shard_map.73), calls=%async_computation.4 | async-start | bytes 2686976 | tf_op jit(solution)/shard_map/all_to_all | solution.py:317
  11.1 0.1 pad_add_fusion.place
  11.1 19.1 %all-to-all-done.4.came = bf16[8,656,128]{2,1,0:T(8,128)(2,1)S(1)} async-done(((bf16[8,656,128]{2,1,0:T(8,128)(2,1)}), bf16[8,656,128]{2,1,0:T(8,128)(2,1)S(1)}, u32[]{:S(2)}, u32[]{:S(2)}) %all-to-all-start.4) | async-done | bytes 1343520 | tf_op jit(solution)/shard_map/all_to_all | solution.py:317
  30.2 1.4 %shard_map.74 = (bf16[1296,128]{1,0:T(8,128)(2,1)S(1)}, bf16[1296,128]{1,0:T(8,128)(2,1)S(1)}, bf16[1296,128]{1,0:T(8,128)(2,1)S(1)}, bf16[1296,128]{1,0:T(8,128)(2,1)S(1)}) custom-call(s32[2]{0:T(128)S(1)} %pad_add_fusion.place, bf16[8,656,128]{2,1,0:T(8,128)(2,1)S(1)} %all-to-all-done.4.came), custom_call_target="tpu_custom_call" | custom-call | tf_op jit(solution)/shard_map/pallas_call | solution.py:140
  31.6 1.6 %collective-permute-start = (bf16[1296,128]{1,0:T(8,128)(2,1)S(1)}, bf16[1296,128]{1,0:T(8,128)(2,1)S(1)}, u32[]{:S(2)}, u32[]{:S(2)}) collective-permute-start(bf16[1296,128]{1,0:T(8,128)(2,1)S(1)} %get-tuple-element.42), channel_id=1, source_target_pairs={{0,8},{1,9},{2,10},{3,11},{4,12},{5,13},{6,14},{7,15},{8,16},{9,17... | collective-permute-start | bytes 995336 | tf_op jit(solution)/shard_map/ppermute | solution.py:320
  33.2 2.7 %collective-permute-start.1 = (bf16[1296,128]{1,0:T(8,128)(2,1)S(1)}, bf16[1296,128]{1,0:T(8,128)(2,1)S(1)}, u32[]{:S(2)}, u32[]{:S(2)}) collective-permute-start(bf16[1296,128]{1,0:T(8,128)(2,1)S(1)} %get-tuple-element.43), channel_id=1, source_target_pairs={{0,16},{1,17},{2,18},{3,19},{4,20},{5,21},{6,22},{7,23},{8,24},{9,... | collective-permute-start | bytes 995336 | tf_op jit(solution)/shard_map/ppermute | solution.py:320
  35.9 1.4 %collective-permute-start.2 = (bf16[1296,128]{1,0:T(8,128)(2,1)S(1)}, bf16[1296,128]{1,0:T(8,128)(2,1)S(1)}, u32[]{:S(2)}, u32[]{:S(2)}) collective-permute-start(bf16[1296,128]{1,0:T(8,128)(2,1)S(1)} %get-tuple-element.44), channel_id=1, source_target_pairs={{0,24},{1,25},{2,26},{3,27},{4,28},{5,29},{6,30},{7,31},{8,0},{9,1... | collective-permute-start | bytes 995336 | tf_op jit(solution)/shard_map/ppermute | solution.py:320
  37.3 0.0 copy-done.1
  37.3 1.7 %copy.45 = bf16[8,512,128]{2,0,1:T(8,128)(2,1)} copy(bf16[8,512,128]{2,1,0:T(8,128)(2,1)S(1)} %copy-done.1) | data formatting | bytes 2097152 | tf_op jit(solution)/shard_map/while | solution.py:326
  39.1 3.5 %collective-permute-done.refs_1_ = bf16[1296,128]{1,0:T(8,128)(2,1)S(1)} collective-permute-done((bf16[1296,128]{1,0:T(8,128)(2,1)S(1)}, bf16[1296,128]{1,0:T(8,128)(2,1)S(1)}, u32[]{:S(2)}, u32[]{:S(2)}) %collective-permute-start) | collective-permute-done | bytes 331808 | tf_op jit(solution)/shard_map/ppermute | solution.py:320
  42.6 7.7 %collective-permute-done.1.refs_2_ = bf16[1296,128]{1,0:T(8,128)(2,1)S(1)} collective-permute-done((bf16[1296,128]{1,0:T(8,128)(2,1)S(1)}, bf16[1296,128]{1,0:T(8,128)(2,1)S(1)}, u32[]{:S(2)}, u32[]{:S(2)}) %collective-permute-start.1) | collective-permute-done | bytes 331808 | tf_op jit(solution)/shard_map/ppermute | solution.py:320
  50.3 0.0 collective-permute-done.2.refs_3_
  50.3 1.3 %shard_map.75 = (bf16[4,640,128]{2,1,0:T(8,128)(2,1)S(1)}, s32[1]{0:T(128)}) custom-call(bf16[1296,128]{1,0:T(8,128)(2,1)S(1)} %get-tuple-element.41.refs_0_, bf16[1296,128]{1,0:T(8,128)(2,1)S(1)} %collective-permute-done.refs_1_, bf16[1296,128]{1,0:T(8,128)(2,1)S(1)} %collective-permute-done.1.refs_2_, bf16[1296,128]{1,0:T(8,128)(2,1)S(1)} %collective-permute-done.2.refs_3_), custom_call_target="tpu_custom_call" | custom-call | tf_op jit(solution)/shard_map/pallas_call | solution.py:186
  51.6 1.4 %copy.44 = bf16[4,640,128]{2,0,1:T(4,128)(2,1)} copy(bf16[4,640,128]{2,1,0:T(8,128)(2,1)S(1)} %get-tuple-element.72) | data formatting | bytes 1310720 | tf_op jit(solution)/shard_map/while | solution.py:326
  53.0 0.0 copy-done.4
  53.0 0.0 copy-done.6
  53.0 0.0 copy-done.7
  53.0 0.0 copy-start.5
  53.0 0.0 copy-start.2
  53.0 1.0 %while.9 = (bf16[4,640,128]{2,0,1:T(4,128)(2,1)}, s32[1]{0:T(128)}, s32[8]{0:T(128)S(1)}, bf16[8,512,128]{2,0,1:T(8,128)(2,1)}, s32[8]{0:T(128)S(1)}, /*index=5*/bf16[8,64,256]{2,1,0:T(8,128)(2,1)S(1)}) while((bf16[4,640,128]{2,0,1:T(4,128)(2,1)}, s32[1]{0:T(128)}, s32[8]{0:T(128)S(1)}, bf16[8,512,128]{2,0,1:T(8,128)(2,1)}, s32[8]{0:T(128)S(1)}, ...), condition=%region_3.4_spmd, body=%region_0.3_spmd | while | flops 66194192 | bytes 41093960 | solution.py:326
  54.0 1.2 %copy.46.own = bf16[4,640,128]{2,1,0:T(8,128)(2,1)S(1)} copy(bf16[4,640,128]{2,0,1:T(4,128)(2,1)} %get-tuple-element.47) | data formatting | bytes 1310720 | tf_op jit(solution)/shard_map/while | solution.py:326
  55.2 1.9 %collective-permute-start.3 = (bf16[4,640,128]{2,1,0:T(8,128)(2,1)S(1)}, bf16[4,640,128]{2,1,0:T(8,128)(2,1)S(1)}, u32[]{:S(2)}, u32[]{:S(2)}) collective-permute-start(bf16[4,640,128]{2,1,0:T(8,128)(2,1)S(1)} %copy.46.own), channel_id=1, source_target_pairs={{0,1},{1,2},{2,3},{3,4},{4,5},{5,6},{6,7},{7,8},{8,9},{9,10},{10,1... | collective-permute-start | bytes 1966088 | tf_op jit(solution)/shard_map/ppermute | solution.py:336
  57.1 8.1 %collective-permute-start.4 = (bf16[4,640,128]{2,1,0:T(8,128)(2,1)S(1)}, bf16[4,640,128]{2,1,0:T(8,128)(2,1)}, u32[]{:S(2)}, u32[]{:S(2)}) collective-permute-start(bf16[4,640,128]{2,1,0:T(8,128)(2,1)S(1)} %copy.46.own), channel_id=1, source_target_pairs={{1,0},{2,1},{3,2},{4,3},{5,4},{6,5},{7,6},{8,7},{9,8},{10,9},{11,1... | collective-permute-start | bytes 1966088 | tf_op jit(solution)/shard_map/ppermute | solution.py:337
  65.2 0.0 copy-done.5
  65.2 0.1 reshape.106.lookup
  65.3 6.0 %collective-permute-done.3.before = bf16[4,640,128]{2,1,0:T(8,128)(2,1)S(1)} collective-permute-done((bf16[4,640,128]{2,1,0:T(8,128)(2,1)S(1)}, bf16[4,640,128]{2,1,0:T(8,128)(2,1)S(1)}, u32[]{:S(2)}, u32[]{:S(2)}) %collective-permute-start.3) | collective-permute-done | bytes 655392 | tf_op jit(solution)/shard_map/ppermute | solution.py:336
  71.3 1.8 %collective-permute-done.4.after = bf16[4,640,128]{2,1,0:T(8,128)(2,1)} collective-permute-done((bf16[4,640,128]{2,1,0:T(8,128)(2,1)S(1)}, bf16[4,640,128]{2,1,0:T(8,128)(2,1)}, u32[]{:S(2)}, u32[]{:S(2)}) %collective-permute-start.4) | collective-permute-done | bytes 655392 | tf_op jit(solution)/shard_map/ppermute | solution.py:337
  73.1 0.0 copy-done.2
  73.1 0.0 copy-start.3
  73.1 1.0 %copy-done.3 = bf16[8,256,128]{2,1,0:T(8,128)(2,1)S(1)} copy-done((bf16[8,256,128]{2,1,0:T(8,128)(2,1)S(1)}, bf16[8,256,128]{2,1,0:T(8,128)(2,1)}, u32[]{:S(2)}) %copy-start.3) | copy-done | bytes 524312
  74.1 12.2 %shard_map.76 = bf16[4,512,128]{2,1,0:T(8,128)(2,1)} custom-call(s32[104]{0:T(128)S(1)} %reshape.106.lookup, bf16[4,640,128]{2,1,0:T(8,128)(2,1)S(1)} %collective-permute-done.3.before, bf16[4,640,128]{2,1,0:T(8,128)(2,1)S(1)} %copy.46.own, bf16[4,640,128]{2,1,0:T(8,128)(2,1)} %collective-permute-done.4.after, bf16[4,512,128]{2,1,0:T(8,128)(2,1)S(1)} %bitcast.28, ...), custom_call_target="tpu_custom_call" | custom-call | tf_op jit(solution)/shard_map/pallas_call | solution.py:296
  (1 shorter events, 0.0 us)
Async XLA Ops:
  0.0 1.2 %copy-start = (bf16[8,512,128]{2,1,0:T(8,128)(2,1)S(1)}, bf16[8,512,128]{2,1,0:T(8,128)(2,1)}, u32[]{:S(2)}) copy-start(bf16[8,512,128]{2,1,0:T(8,128)(2,1)} %skip.1) | copy-start | bytes 3145732
  1.2 36.1 %copy-start.1 = (bf16[8,512,128]{2,1,0:T(8,128)(2,1)S(1)}, bf16[8,512,128]{2,1,0:T(8,128)(2,1)}, u32[]{:S(2)}) copy-start(bf16[8,512,128]{2,1,0:T(8,128)(2,1)} %skip.1) | copy-start | bytes 3145732
  5.6 47.4 %copy-start.4 = (bf16[8,64,256]{2,1,0:T(8,128)(2,1)S(1)}, bf16[8,64,256]{2,1,0:T(8,128)(2,1)}, u32[]{:S(2)}) copy-start(bf16[8,64,256]{2,1,0:T(8,128)(2,1)} %parents.1) | copy-start | bytes 786436
  5.6 47.4 %copy-start.6 = (s32[8]{0:T(128)S(1)}, s32[8]{0:T(128)}, u32[]{:S(2)}) copy-start(s32[8]{0:T(128)} %parent_dest.1) | copy-start | bytes 100
  5.6 47.4 %copy-start.7 = (s32[8]{0:T(128)S(1)}, s32[8]{0:T(128)}, u32[]{:S(2)}) copy-start(s32[8]{0:T(128)} %skip_dest.1) | copy-start | bytes 100
  5.6 24.6 %all-to-all-start.4 = ((bf16[8,656,128]{2,1,0:T(8,128)(2,1)}), bf16[8,656,128]{2,1,0:T(8,128)(2,1)S(1)}, u32[]{:S(2)}, u32[]{:S(2)}) async-start(bf16[8,656,128]{2,1,0:T(8,128)(2,1)} %shard_map.73), calls=%async_computation.4 | async-start | bytes 2686976 | tf_op jit(solution)/shard_map/all_to_all | solution.py:317
  31.6 11.0 %collective-permute-start = (bf16[1296,128]{1,0:T(8,128)(2,1)S(1)}, bf16[1296,128]{1,0:T(8,128)(2,1)S(1)}, u32[]{:S(2)}, u32[]{:S(2)}) collective-permute-start(bf16[1296,128]{1,0:T(8,128)(2,1)S(1)} %get-tuple-element.42), channel_id=1, source_target_pairs={{0,8},{1,9},{2,10},{3,11},{4,12},{5,13},{6,14},{7,15},{8,16},{9,17... | collective-permute-start | bytes 995336 | tf_op jit(solution)/shard_map/ppermute | solution.py:320
  33.2 17.2 %collective-permute-start.1 = (bf16[1296,128]{1,0:T(8,128)(2,1)S(1)}, bf16[1296,128]{1,0:T(8,128)(2,1)S(1)}, u32[]{:S(2)}, u32[]{:S(2)}) collective-permute-start(bf16[1296,128]{1,0:T(8,128)(2,1)S(1)} %get-tuple-element.43), channel_id=1, source_target_pairs={{0,16},{1,17},{2,18},{3,19},{4,20},{5,21},{6,22},{7,23},{8,24},{9,... | collective-permute-start | bytes 995336 | tf_op jit(solution)/shard_map/ppermute | solution.py:320
  35.9 14.4 %collective-permute-start.2 = (bf16[1296,128]{1,0:T(8,128)(2,1)S(1)}, bf16[1296,128]{1,0:T(8,128)(2,1)S(1)}, u32[]{:S(2)}, u32[]{:S(2)}) collective-permute-start(bf16[1296,128]{1,0:T(8,128)(2,1)S(1)} %get-tuple-element.44), channel_id=1, source_target_pairs={{0,24},{1,25},{2,26},{3,27},{4,28},{5,29},{6,30},{7,31},{8,0},{9,1... | collective-permute-start | bytes 995336 | tf_op jit(solution)/shard_map/ppermute | solution.py:320
  53.0 12.2 %copy-start.5 = (s32[4,26]{1,0:T(4,128)S(1)}, s32[4,26]{1,0:T(4,128)}, u32[]{:S(2)}) copy-start(s32[4,26]{1,0:T(4,128)} %param.13) | copy-start | bytes 1252
  53.0 20.0 %copy-start.2 = (bf16[27,256,128]{2,1,0:T(8,128)(2,1)S(1)}, bf16[27,256,128]{2,1,0:T(8,128)(2,1)}, u32[]{:S(2)}) copy-start(bf16[27,256,128]{2,1,0:T(8,128)(2,1)} %param.15) | copy-start | bytes 5308420
  55.2 16.1 %collective-permute-start.3 = (bf16[4,640,128]{2,1,0:T(8,128)(2,1)S(1)}, bf16[4,640,128]{2,1,0:T(8,128)(2,1)S(1)}, u32[]{:S(2)}, u32[]{:S(2)}) collective-permute-start(bf16[4,640,128]{2,1,0:T(8,128)(2,1)S(1)} %copy.46.own), channel_id=1, source_target_pairs={{0,1},{1,2},{2,3},{3,4},{4,5},{5,6},{6,7},{7,8},{8,9},{9,10},{10,1... | collective-permute-start | bytes 1966088 | tf_op jit(solution)/shard_map/ppermute | solution.py:336
  57.1 16.0 %collective-permute-start.4 = (bf16[4,640,128]{2,1,0:T(8,128)(2,1)S(1)}, bf16[4,640,128]{2,1,0:T(8,128)(2,1)}, u32[]{:S(2)}, u32[]{:S(2)}) collective-permute-start(bf16[4,640,128]{2,1,0:T(8,128)(2,1)S(1)} %copy.46.own), channel_id=1, source_target_pairs={{1,0},{2,1},{3,2},{4,3},{5,4},{6,5},{7,6},{8,7},{9,8},{10,9},{11,1... | collective-permute-start | bytes 1966088 | tf_op jit(solution)/shard_map/ppermute | solution.py:337
  73.1 1.0 %copy-start.3 = (bf16[8,256,128]{2,1,0:T(8,128)(2,1)S(1)}, bf16[8,256,128]{2,1,0:T(8,128)(2,1)}, u32[]{:S(2)}) copy-start(bf16[8,256,128]{2,1,0:T(8,128)(2,1)} %param.14) | copy-start | bytes 1572868

commit v2 on v1

--- a/solution.py
+++ b/solution.py
@@ -26,7 +26,7 @@
     return out
 
 
-def first_kernel(parent_dest, skip_dest, base, parents, skip, out, slot_of, sems):
+def first_kernel(parent_dest, skip_dest, base, parents, skip, out, stage, head, slot_of, sems):
     for q in range(2 * COLUMNS + 1):
         slot_of[q] = 0
     table = []
@@ -37,24 +37,31 @@
             table.append(local)
             column = lax.rem(lax.div(jnp.maximum(local, 0), BRICKS), COLUMNS)
             slot_of[jnp.where(d >= 0, kind * COLUMNS + column, 2 * COLUMNS)] = s
-    copies = []
+    head[...] = rows_of((HEAD_ROWS, 128), table).astype(F32).astype(BF16)
+    into, onward = [], []
     for q in range(COLUMNS):
         s, p = slot_of[q], slot_of[COLUMNS + q]
-        copies.append(pltpu.make_async_copy(skip.at[s], out.at[q, 0:512], sems.at[q, 0]))
-        for half in range(2):
-            copies.append(
-                pltpu.make_async_copy(
-                    parents.at[p, :, 128 * half : 128 * half + 128],
-                    out.at[q, 512 + 64 * half : 576 + 64 * half],
-                    sems.at[q, 1 + half],
-                )
+        pieces = [(skip.at[s], slice(0, 512))] + [
+            (parents.at[p, :, 128 * half : 128 * half + 128], slice(512 + 64 * half, 576 + 64 * half))
+            for half in range(2)
+        ]
+        for j, (source, rows) in enumerate(pieces):
+            into.append(pltpu.make_async_copy(source, stage.at[q, rows], sems.at[0, q, j]))
+            onward.append(
+                pltpu.make_async_copy(stage.at[q, rows], out.at[q, rows], sems.at[1, q, j])
             )
-    for copy in copies:
+        onward.append(
+            pltpu.make_async_copy(head, out.at[q, BODY : BODY + HEAD_ROWS], sems.at[1, q, 3])
+        )
+    for copy in into:
         copy.start()
-    header = rows_of((HEAD_ROWS, 128), table).astype(F32).astype(BF16)
     for q in range(COLUMNS):
-        out[q, BODY : BODY + HEAD_ROWS] = header
-    for copy in copies:
+        onward[4 * q + 3].start()
+    for q in range(COLUMNS):
+        for j in range(3):
+            into[3 * q + j].wait()
+            onward[4 * q + j].start()
+    for copy in onward:
         copy.wait()
 
 
@@ -63,12 +70,13 @@
         first_kernel,
         out_shape=jax.ShapeDtypeStruct((COLUMNS, BODY + HEAD_ROWS, 128), BF16),
         in_specs=[SMEM, SMEM, SMEM, ANY, ANY],
-        out_specs=VMEM,
-        scratch_shapes=[
+        out_specs=ANY,
+        scratch_shapes=[
+            pltpu.VMEM((COLUMNS, BODY, 128), BF16),
+            pltpu.VMEM((HEAD_ROWS, 128), BF16),
             pltpu.SMEM((2 * COLUMNS + 1,), I32),
-            pltpu.SemaphoreType.DMA((COLUMNS, 3)),
-        ],
-        compiler_params=pltpu.CompilerParams(vmem_limit_bytes=16 * 2**20),
+            pltpu.SemaphoreType.DMA((2, COLUMNS, 4)),
+        ],
     )(parent_dest, skip_dest, base, parents, skip)
 
 
@@ -200,42 +208,112 @@
     )(*messages)
 
 
-def dense_route(parents, parent_dest, skip, skip_dest):
-    halves = parents.reshape(SLOTS, 64, 2, 128).transpose(0, 2, 1, 3).reshape(SLOTS, 128, 128)
-    joined = []
-    for dest, payload in ((skip_dest, skip), (parent_dest, halves)):
-        devices = LINES * COLUMNS
-        owner = jnp.where(dest >= 0, dest // BRICKS % devices, -1)
-        match = owner[None, :] == jnp.arange(devices)[:, None]
-        spot = jnp.sum(jnp.where(match, dest % BRICKS + 1, 0), axis=1) - 1
-        rows = jnp.einsum(
-            "os,src->orc", match.astype(BF16), payload, preferred_element_type=F32
-        ).astype(BF16)
-        rows = lax.all_to_all(rows, "gy", 0, 0, tiled=True)
-        spot = lax.all_to_all(spot, "gy", 0, 0, tiled=True)
-        pick = spot[None, :] == jnp.arange(BRICKS)[:, None]
-        joined.append(
-            jnp.einsum(
-                "bo,orc->brc", pick.astype(BF16), rows, preferred_element_type=F32
-            ).astype(BF16)
-        )
-    return jnp.concatenate(joined, axis=1)
-
-
-def conv_kernel(
-    lookup, before, own, after, up_weight, conv_weight, out, pool, shifted, window
-):
+def dense_pack_kernel(parent_dest, skip_dest, base, parents, skip, out, head, sems, sem):
+    table = []
+    copies = []
+    for kind, dest in enumerate((skip_dest, parent_dest)):
+        for s in range(SLOTS):
+            local = jnp.where(dest[s] >= 0, dest[s] - base[0], -1)
+            table.append(local)
+            owner = lax.div(jnp.maximum(local, 0), BRICKS)
+            if kind == 0:
+                pieces = [(skip.at[s], out.at[owner, 0:512])]
+            else:
+                pieces = [
+                    (
+                        parents.at[s, :, 128 * half : 128 * half + 128],
+                        out.at[owner, 512 + 64 * half : 576 + 64 * half],
+                    )
+                    for half in range(2)
+                ]
+            for j, (source, target) in enumerate(pieces):
+                copies.append(
+                    (local, pltpu.make_async_copy(source, target, sems.at[s, kind + j]))
+                )
+    head[...] = rows_of((HEAD_ROWS, 128), table).astype(F32).astype(BF16)
+    for live, copy in copies:
+        pl.when(live >= 0)(copy.start)
+    for owner in range(LINES * COLUMNS):
+        copy = pltpu.make_async_copy(head, out.at[owner, BODY : BODY + HEAD_ROWS], sem)
+        copy.start()
+        copy.wait()
+    for live, copy in copies:
+        pl.when(live >= 0)(copy.wait)
+
+
+def dense_unpack_kernel(place, came, own, heads, found, table, sems, sem):
+    devices = LINES * COLUMNS
+    copy = pltpu.make_async_copy(came.at[:, BODY : BODY + HEAD_ROWS], heads, sem)
+    copy.start()
+    copy.wait()
+    me = place[0] * COLUMNS + place[1]
+    picks = []
+    for kind in range(2):
+        dest = heads[:, kind * SLOTS : kind * SLOTS + SLOTS].astype(F32).astype(I32)
+        mine = jnp.where((dest >= 0) & ((dest >> 2) == me), dest, -1)
+        picks.append(jnp.max(mine, axis=1))
+    lane = lax.broadcasted_iota(I32, (devices, 128), 1)
+    found[...] = jnp.where(lane == 0, picks[0], picks[1])
+    copy = pltpu.make_async_copy(found, table, sem)
+    copy.start()
+    copy.wait()
+    for m in range(devices):
+        for kind, (rows, first, _) in enumerate(PIECES):
+            dest = table[m, kind]
+            copy = pltpu.make_async_copy(
+                came.at[m, first : first + rows],
+                own.at[jnp.maximum(dest, 0) & 3, first : first + rows],
+                sems.at[kind],
+            )
+
+            @pl.when(dest >= 0)
+            def _(copy=copy):
+                copy.start()
+                copy.wait()
+
+
+def dense_route(place, base, parents, parent_dest, skip, skip_dest):
+    devices = LINES * COLUMNS
+    limit = pltpu.CompilerParams(vmem_limit_bytes=16 * 2**20)
+    rows = pl.pallas_call(
+        dense_pack_kernel,
+        out_shape=jax.ShapeDtypeStruct((devices, BODY + HEAD_ROWS, 128), BF16),
+        in_specs=[SMEM, SMEM, SMEM, ANY, ANY],
+        out_specs=ANY,
+        scratch_shapes=[
+            pltpu.VMEM((HEAD_ROWS, 128), BF16),
+            pltpu.SemaphoreType.DMA((SLOTS, 3)),
+            pltpu.SemaphoreType.DMA,
+        ],
+        compiler_params=limit,
+    )(parent_dest, skip_dest, base, parents, skip)
+    came = lax.all_to_all(rows, "gy", 0, 0, tiled=True)
+    return pl.pallas_call(
+        dense_unpack_kernel,
+        out_shape=jax.ShapeDtypeStruct((BRICKS, BODY, 128), BF16),
+        in_specs=[SMEM, ANY],
+        out_specs=VMEM,
+        scratch_shapes=[
+            pltpu.VMEM((devices, HEAD_ROWS, 128), BF16),
+            pltpu.VMEM((devices, 128), I32),
+            pltpu.SMEM((devices, 128), I32),
+            pltpu.SemaphoreType.DMA((2,)),
+            pltpu.SemaphoreType.DMA,
+        ],
+        compiler_params=limit,
+    )(place, came)
+
+
+def fill_pool(pool, groups, up_weight):
     row = lax.broadcasted_iota(I32, (256, 64), 0)
     column = lax.broadcasted_iota(I32, (256, 64), 1)
     in_brick = row & 127
     takes = (in_brick >> 3) * 4 + ((in_brick & 7) >> 1) == column
     spread = jnp.where(takes & ((row & 1) == (row >> 7)), 1.0, 0.0).astype(BF16)
-    for group, bricks in enumerate((before, own, after)):
+    for group, bricks in enumerate(groups):
         spaced = []
         for b in range(BRICKS):
-            pool[group * BRICKS + b, :, :, :, 128:256] = (
-                bricks[b, 0:512].astype(F32).reshape(8, 8, 8, 128)
-            )
+            pool[group * BRICKS + b, 1] = bricks[b, 0:512].astype(F32)
             halves = [
                 jnp.dot(
                     spread, bricks[b, 512 + 64 * h : 576 + 64 * h], preferred_element_type=F32
@@ -250,61 +328,178 @@
         spaced = jnp.concatenate(spaced, axis=0)
         for ab in range(4):
             made = jnp.dot(spaced, up_weight[ab], preferred_element_type=F32)
-            made = made.astype(BF16).astype(F32).reshape(BRICKS, 4, 4, 8, 128)
+            made = made.astype(BF16).astype(F32)
             for b in range(BRICKS):
                 for i in range(4):
                     for j in range(4):
-                        pool[
-                            group * BRICKS + b, 2 * i + ab // 2, 2 * j + ab % 2, :, 0:128
-                        ] = made[b, i, j]
-    pool[3 * BRICKS] = jnp.zeros((8, 8, 8, 256), F32)
-
-    spans = {-1: (slice(7, 8), slice(0, 1)), 0: (slice(0, 8), slice(1, 9)), 1: (slice(0, 1), slice(9, 10))}
-
-    @pl.loop(0, BRICKS)
-    def _(b):
+                        first = (2 * i + ab // 2) * 64 + (2 * j + ab % 2) * 8
+                        came = b * 128 + i * 32 + j * 8
+                        pool[group * BRICKS + b, 0, first : first + 8] = made[came : came + 8]
+    pool[len(groups) * BRICKS] = jnp.zeros((2, 512, 128), F32)
+
+
+def rows_from(pool, brick, rows):
+    return jnp.concatenate([pool[brick, 0, rows], pool[brick, 1, rows]], axis=1)
+
+
+def shift_rows(line):
+    z = lax.broadcasted_iota(I32, line[1].shape, 1)
+    return (
+        pltpu.roll(jnp.where(z == 7, line[0], line[1]), 1, 1),
+        line[1],
+        pltpu.roll(jnp.where(z == 0, line[2], line[1]), 7, 1),
+    )
+
+
+def code_of(off_x, off_y, off_z):
+    code = (off_x + 1) * 9 + (off_y + 1) * 3 + off_z + 1
+    return code - (code > 13)
+
+
+def near_kernel(
+    lookup, own, up_weight, pair_weight, last_weight, out, pool, shifted_pair, window_pair
+):
+    fill_pool(pool, (own,), up_weight)
+    spans = {-1: (7, 8, 0), 0: (0, 8, 1), 1: (0, 1, 9)}
+
+    for b in range(BRICKS):
+        shifted, window = shifted_pair[b % 2], window_pair[b % 2]
         for off_x in (-1, 0, 1):
             for off_y in (-1, 0, 1):
-                from_x, to_x = spans[off_x]
-                from_y, to_y = spans[off_y]
-                line = []
-                for off_z in (-1, 0, 1):
-                    code = (off_x + 1) * 9 + (off_y + 1) * 3 + off_z + 1
-                    brick = BRICKS + b if code == 13 else lookup[b * 26 + code - (code > 13)]
-                    line.append(pool[brick, from_x, from_y])
-                z = lax.broadcasted_iota(I32, line[1].shape, 2)
-                shifted[0, to_x, to_y] = pltpu.roll(jnp.where(z == 7, line[0], line[1]), 1, 2)
-                shifted[1, to_x, to_y] = line[1]
-                shifted[2, to_x, to_y] = pltpu.roll(jnp.where(z == 0, line[2], line[1]), 7, 2)
+                low_x, high_x, to_x = spans[off_x]
+                low_y, high_y, to_y = spans[off_y]
+                deep = high_y - low_y
+                bricks = [
+                    b if off_x == off_y == off_z == 0 else lookup[b * 26 + code_of(off_x, off_y, off_z)]
+                    for off_z in (-1, 0, 1)
+                ]
+                for x in range(low_x, high_x):
+                    first = x * 64 + low_y * 8
+                    line = [
+                        rows_from(pool, brick, pl.ds(first, deep * 8)).reshape(deep, 8, 256)
+                        for brick in bricks
+                    ]
+                    for step, rows in enumerate(shift_rows(line)):
+                        shifted[step, to_x + x - low_x, to_y : to_y + deep] = rows
         for step_y in range(3):
             for step_z in range(3):
                 first = (step_y * 3 + step_z) * 256
                 window[:, first : first + 256] = (
                     shifted[step_z, :, step_y : step_y + 8].reshape(640, 256).astype(BF16)
                 )
-        total = jnp.dot(window[0:512], conv_weight[0], preferred_element_type=F32)
-        for step_x in (1, 2):
-            total += jnp.dot(
-                window[64 * step_x : 64 * step_x + 512],
-                conv_weight[step_x],
+        pair = jnp.dot(window[0:576], pair_weight[...], preferred_element_type=F32)
+        last = jnp.dot(window[128:640], last_weight[...], preferred_element_type=F32)
+        out[b] = pair[0:512, 0:128] + pair[64:576, 128:256] + last
+
+
+def far_kernel(
+    lookup, before, after, near, up_weight, conv_weight, out, pool, shifted, window, total
+):
+    fill_pool(pool, (before, after), up_weight)
+    total[...] = near[...].reshape(BRICKS * 512, 128)
+    shifted[...] = jnp.zeros(shifted.shape, F32)
+
+    @pl.loop(0, BRICKS)
+    def _(b):
+        def brick(*offsets):
+            return lookup[b * 26 + code_of(*offsets)]
+
+        def keep(side):
+            for step in range(3):
+                for inner in range(3):
+                    first = (step * 3 + inner) * 256
+                    window[side, pl.ds(pl.multiple_of(b * 64, 64), 64), first : first + 256] = (
+                        shifted[side, inner, step : step + 8].reshape(64, 256).astype(BF16)
+                    )
+
+        for side, off in enumerate((-1, 1)):
+            edge = 7 if off < 0 else 0
+            for off_y in (-1, 0, 1):
+                bricks = [brick(off, off_y, off_z) for off_z in (-1, 0, 1)]
+                low, deep, to = ((7, 1, 0), (0, 8, 1), (0, 1, 9))[off_y + 1]
+                first = edge * 64 + low * 8
+                line = [
+                    rows_from(pool, n, pl.ds(first, deep * 8)).reshape(deep, 8, 256)
+                    for n in bricks
+                ]
+                for step, rows in enumerate(shift_rows(line)):
+                    shifted[side, step, to : to + deep] = rows
+            keep(side)
+            bricks = [brick(0, off, off_z) for off_z in (-1, 0, 1)]
+            for x in range(8):
+                first = x * 64 + edge * 8
+                line = [rows_from(pool, n, pl.ds(first, 8)).reshape(1, 8, 256) for n in bricks]
+                for step, rows in enumerate(shift_rows(line)):
+                    shifted[2 + side, step, 1 + x : 2 + x] = rows
+            keep(2 + side)
+            face = rows_from(pool, brick(0, 0, off), pl.ds(edge, 64, stride=8)).reshape(8, 8, 256)
+            y = lax.broadcasted_iota(I32, face.shape, 1)
+            shifted[4 + side, 0, 1:9] = jnp.where(y == 0, 0.0, pltpu.roll(face, 1, 1))
+            shifted[4 + side, 1, 1:9] = face
+            shifted[4 + side, 2, 1:9] = jnp.where(y == 7, 0.0, pltpu.roll(face, 7, 1))
+            keep(4 + side)
+
+    for side in range(2):
+        tap = 2 * side
+        added = jnp.dot(window[side], conv_weight[tap], preferred_element_type=F32)
+        for b in range(BRICKS):
+            first = b * 512 + 448 * side
+            total[first : first + 64] += added[b * 64 : b * 64 + 64]
+        added = jnp.zeros((256, 128), F32)
+        for x in range(3):
+            added += jnp.dot(
+                window[2 + side, :, x * 768 : x * 768 + 768],
+                conv_weight[x, tap * 768 : tap * 768 + 768],
                 preferred_element_type=F32,
             )
-        out[b] = jnp.maximum(total, 0.0).astype(BF16)
-
-
-def refine(lookup, before, own, after, up_weight, conv_weight):
+        for r in range(BRICKS * 8):
+            first = r * 64 + 56 * side
+            total[first : first + 8] += added[r * 8 : r * 8 + 8]
+        added = jnp.zeros((256, 128), F32)
+        for x in range(3):
+            for y in range(3):
+                added += jnp.dot(
+                    window[4 + side, :, (x * 3 + y) * 256 : (x * 3 + y) * 256 + 256],
+                    conv_weight[x, (y * 3 + tap) * 256 : (y * 3 + tap) * 256 + 256],
+                    preferred_element_type=F32,
+                )
+        at = pl.ds(7 * side, BRICKS * 64, stride=8)
+        total[at] = total[at] + added
+    out[...] = jnp.maximum(total[...], 0.0).astype(BF16).reshape(BRICKS, 512, 128)
+
+
+def convolve_near(lookup, own, up_weight, pair_weight, last_weight):
     return pl.pallas_call(
-        conv_kernel,
+        near_kernel,
+        out_shape=jax.ShapeDtypeStruct((BRICKS, 512, 128), F32),
+        in_specs=[SMEM] + [VMEM] * 4,
+        out_specs=VMEM,
+        scratch_shapes=[
+            pltpu.VMEM((BRICKS + 1, 2, 512, 128), F32),
+            [pltpu.VMEM((3, 10, 10, 8, 256), F32)] * 2,
+            [pltpu.VMEM((640, 9 * 256), BF16)] * 2,
+        ],
+        compiler_params=pltpu.CompilerParams(vmem_limit_bytes=32 * 2**20),
+        cost_estimate=pl.CostEstimate(
+            flops=10**10, bytes_accessed=4 * 10**7, transcendentals=0
+        ),
+    )(lookup, own, up_weight, pair_weight, last_weight)
+
+
+def convolve_far(lookup, before, after, near, up_weight, conv_weight):
+    return pl.pallas_call(
+        far_kernel,
         out_shape=jax.ShapeDtypeStruct((BRICKS, 512, 128), BF16),
         in_specs=[SMEM] + [VMEM] * 5,
         out_specs=VMEM,
         scratch_shapes=[
-            pltpu.VMEM((3 * BRICKS + 1, 8, 8, 8, 256), F32),
-            pltpu.VMEM((3, 10, 10, 8, 256), F32),
-            pltpu.VMEM((640, 9 * 256), BF16),
-        ],
-        compiler_params=pltpu.CompilerParams(vmem_limit_bytes=48 * 2**20),
-    )(lookup, before, own, after, up_weight, conv_weight)
+            pltpu.VMEM((2 * BRICKS + 1, 2, 512, 128), F32),
+            pltpu.VMEM((6, 3, 10, 8, 256), F32),
+            pltpu.VMEM((6, BRICKS * 64, 9 * 256), BF16),
+            pltpu.VMEM((BRICKS * 512, 128), F32),
+        ],
+        compiler_params=pltpu.CompilerParams(vmem_limit_bytes=32 * 2**20),
+    )(lookup, before, after, near, up_weight, conv_weight)
 
 
 def per_device(parents, parent_dest, skip, skip_dest, neighbours, up_weight, conv_weight):
@@ -326,7 +521,7 @@
     own, _ = lax.while_loop(
         lambda state: state[1][0] > 0,
         lambda state: (
-            dense_route(parents, parent_dest, skip, skip_dest),
+            dense_route(place, base, parents, parent_dest, skip, skip_dest),
             jnp.zeros_like(state[1]),
         ),
         (own, flag),
@@ -336,15 +531,18 @@
     before = lax.ppermute(own, ("gx", "gy"), up)
     after = lax.ppermute(own, ("gx", "gy"), [(j, i) for i, j in up])
     me = row * devices + inner
-    lookup = jnp.where(neighbours >= 0, neighbours - (me - 1) * BRICKS, 3 * BRICKS)
-    return refine(
-        lookup.reshape(-1),
-        before,
-        own,
-        after,
-        up_weight.reshape(4, 512, 128),
-        conv_weight.reshape(3, 9 * 256, 128),
+    ahead = neighbours - me * BRICKS
+    here = (neighbours >= 0) & (ahead >= 0) & (ahead < BRICKS)
+    near_lookup = jnp.where(here, ahead, BRICKS)
+    far = jnp.where(ahead < 0, ahead + BRICKS, ahead)
+    far_lookup = jnp.where((neighbours >= 0) & ~here, far, 2 * BRICKS)
+    up_weight = up_weight.reshape(4, 512, 128)
+    conv_weight = conv_weight.reshape(3, 9 * 256, 128)
+    pair_weight = jnp.concatenate([conv_weight[0], conv_weight[1]], axis=1)
+    near = convolve_near(
+        near_lookup.reshape(-1), own, up_weight, pair_weight, conv_weight[2]
     )
+    return convolve_far(far_lookup.reshape(-1), before, after, near, up_weight, conv_weight)
 
 
 def solution(mesh):

time: 87.4 us -> 75.9 us (0.87)
  waiting for transfers between devices: 38 us -> 29 us
  local copies, waits for them, and re-layouts: 6.65 us -> 2.5 us
  other arithmetic: 0.08 us -> 1.56 us
  Pallas kernels: 19.2 us -> 20.5 us
    ppermute x1, waiting for transfers between devices: 5.99 us -> 0.01 us  [per_device(): before = lax.ppermute(own, ('gx', 'gy'), up)]
    while x3 -> x0, local copies, waits for them, and re-layouts: 4.27 us -> none  [per_device(): lax.while_loop(lambda state: state[1][0] > 0, lambda state: (dense_route(...]
    ppermute x1, waiting for transfers between devices: 1.76 us -> 0.01 us  [per_device(): after = lax.ppermute(own, ('gx', 'gy'), [(j, i) for i, j in up])]
    concatenate x0 -> x1, other arithmetic: none -> 1.47 us  [per_device(): pair_weight = jnp.concatenate([conv_weight[0], conv_weight[1]], axis=1)]
    all_to_all x1, waiting for transfers between devices: 19.1 us -> 17.6 us  [per_device(): lax.all_to_all(first, 'gy', 0, 0, tiled=True, axis_index_groups=groups)]
    slice x0 -> x1, local copies, waits for them, and re-layouts: none -> 1.26 us  [per_device(): conv_weight[2]]
    unnamed x16, local copies, waits for them, and re-layouts: 2.3 us -> 1.07 us
    pallas_call x1 -> x2, Pallas kernels: 12.2 us -> 13.3 us  [the longest x1 7.72 us: convolve_near(): pl.pallas_call(near_kernel, out_shape=jax.ShapeDtypeStruct((BRICKS, 512,...]
  transfers between devices with their start and end apart: 6 -> 6, of which waited for: 5 -> 3; matrix products, arithmetic and copies ran while one was open for 2% -> 4% of each run, Pallas kernels for 0% -> 10%
where the time goes in v2:
time: 75.9 us; the launch traced here: 75.4 us
  waiting for transfers between devices  29 us (38%)
  starting transfers between devices  21 us (28%)
  Pallas kernels  20.5 us (27%)
  local copies, waits for them, and re-layouts  2.5 us (3%)
  other arithmetic  1.56 us (2%)
    all_to_all x1, waiting for transfers between devices, per_device(): lax.all_to_all(first, 'gy', 0, 0, tiled=True, axis_index_groups=groups)  17.6 us
    ppermute x3, waiting for transfers between devices, per_device(): lax.ppermute(messages[k], 'gy', [(i, (i + k * COLUMNS) % devices) for i i...  11.4 us
    ppermute x1, starting transfers between devices, per_device(): after = lax.ppermute(own, ('gx', 'gy'), [(j, i) for i, j in up])  8.04 us
    pallas_call x1, Pallas kernels, convolve_near(): pl.pallas_call(near_kernel, out_shape=jax.ShapeDtypeStruct((BRICKS, 512,...  7.72 us
    ppermute x3, starting transfers between devices, per_device(): lax.ppermute(messages[k], 'gy', [(i, (i + k * COLUMNS) % devices) for i i...  6.14 us
    pallas_call x1, Pallas kernels, convolve_far(): pl.pallas_call(far_kernel, out_shape=jax.ShapeDtypeStruct((BRICKS, 512, 1...  5.62 us
    all_to_all x1, starting transfers between devices, per_device(): lax.all_to_all(first, 'gy', 0, 0, tiled=True, axis_index_groups=groups)  4.88 us
    pallas_call x1, Pallas kernels, first_pack(): pl.pallas_call(first_kernel, out_shape=jax.ShapeDtypeStruct((COLUMNS, BOD...  4.06 us
  transfers between devices with their start and end apart: 6, of which 3 were waited for; matrix products, arithmetic and copies ran while one was open for 4% of the time, Pallas kernels for 10%

profile of v2, /device:TPU:16, one launch (start us, length us, event | category | flops | bytes accessed | tf_op | source)
XLA Modules:
  0.0 75.4 jit_solution(8594520077438078762)
XLA Ops:
  0.0 4.1 %shard_map.73 = bf16[8,656,128]{2,1,0:T(8,128)(2,1)} custom-call(s32[8]{0:T(128)} %parent_dest.1, s32[8]{0:T(128)} %skip_dest.1, s32[1]{0:T(128)} %bitcast.3.base, bf16[8,64,256]{2,1,0:T(8,128)(2,1)} %parents.1, bf16[8,512,128]{2,1,0:T(8,128)(2,1)} %skip.1), custom_call_target="tpu_custom_call" | custom-call | tf_op jit(solution)/shard_map/pallas_call | solution.py:69
  4.1 0.0 copy-start.11
  4.1 0.0 copy-start.1
  4.1 4.9 %all-to-all-start.1 = ((bf16[8,656,128]{2,1,0:T(8,128)(2,1)}), bf16[8,656,128]{2,1,0:T(8,128)(2,1)S(1)}, u32[]{:S(2)}, u32[]{:S(2)}) async-start(bf16[8,656,128]{2,1,0:T(8,128)(2,1)} %shard_map.73), calls=%async_computation.1 | async-start | bytes 2686976 | tf_op jit(solution)/shard_map/all_to_all | solution.py:512
  9.0 0.0 copy-done.11
  9.0 0.1 reshape.25.lookup
  9.1 0.1 reshape.23.lookup
  9.2 0.1 pad_add_fusion.place
  9.2 0.0 copy-done.1
  9.2 1.3 %fusion.2 = (bf16[9,256,128]{2,1,0:T(8,128)(2,1)}, bf16[9,256,128]{2,1,0:T(8,128)(2,1)}, bf16[9,256,128]{2,1,0:T(8,128)(2,1)}) fusion(bf16[27,256,128]{2,1,0:T(8,128)(2,1)S(1)} %copy-done.1), kind=kLoop, calls=%fused_computation.8 | loop fusion | bytes 3538944 | tf_op jit(solution)/shard_map/slice | solution.py:543
  10.5 17.6 %all-to-all-done.1.came = bf16[8,656,128]{2,1,0:T(8,128)(2,1)S(1)} async-done(((bf16[8,656,128]{2,1,0:T(8,128)(2,1)}), bf16[8,656,128]{2,1,0:T(8,128)(2,1)S(1)}, u32[]{:S(2)}, u32[]{:S(2)}) %all-to-all-start.1) | async-done | bytes 1343520 | tf_op jit(solution)/shard_map/all_to_all | solution.py:512
  28.1 1.4 %shard_map.74 = (bf16[1296,128]{1,0:T(8,128)(2,1)S(1)}, bf16[1296,128]{1,0:T(8,128)(2,1)S(1)}, bf16[1296,128]{1,0:T(8,128)(2,1)S(1)}, bf16[1296,128]{1,0:T(8,128)(2,1)S(1)}) custom-call(s32[2]{0:T(128)S(1)} %pad_add_fusion.place, bf16[8,656,128]{2,1,0:T(8,128)(2,1)S(1)} %all-to-all-done.1.came), custom_call_target="tpu_custom_call" | custom-call | tf_op jit(solution)/shard_map/pallas_call | solution.py:148
  29.5 1.9 %collective-permute-start = (bf16[1296,128]{1,0:T(8,128)(2,1)S(1)}, bf16[1296,128]{1,0:T(8,128)(2,1)S(1)}, u32[]{:S(2)}, u32[]{:S(2)}) collective-permute-start(bf16[1296,128]{1,0:T(8,128)(2,1)S(1)} %get-tuple-element.52), channel_id=1, source_target_pairs={{0,8},{1,9},{2,10},{3,11},{4,12},{5,13},{6,14},{7,15},{8,16},{9,17... | collective-permute-start | bytes 995336 | tf_op jit(solution)/shard_map/ppermute | solution.py:515
  31.4 2.7 %collective-permute-start.1 = (bf16[1296,128]{1,0:T(8,128)(2,1)S(1)}, bf16[1296,128]{1,0:T(8,128)(2,1)S(1)}, u32[]{:S(2)}, u32[]{:S(2)}) collective-permute-start(bf16[1296,128]{1,0:T(8,128)(2,1)S(1)} %get-tuple-element.53), channel_id=1, source_target_pairs={{0,16},{1,17},{2,18},{3,19},{4,20},{5,21},{6,22},{7,23},{8,24},{9,... | collective-permute-start | bytes 995336 | tf_op jit(solution)/shard_map/ppermute | solution.py:515
  34.1 1.6 %collective-permute-start.2 = (bf16[1296,128]{1,0:T(8,128)(2,1)S(1)}, bf16[1296,128]{1,0:T(8,128)(2,1)S(1)}, u32[]{:S(2)}, u32[]{:S(2)}) collective-permute-start(bf16[1296,128]{1,0:T(8,128)(2,1)S(1)} %get-tuple-element.54), channel_id=1, source_target_pairs={{0,24},{1,25},{2,26},{3,27},{4,28},{5,29},{6,30},{7,31},{8,0},{9,1... | collective-permute-start | bytes 995336 | tf_op jit(solution)/shard_map/ppermute | solution.py:515
  35.7 0.0 copy-start.4
  35.7 0.0 copy-start.6
  35.7 0.0 copy-start.8
  35.7 0.0 copy-start.9
  35.7 1.5 %pad_maximum_fusion.pair_weight = bf16[2304,256]{1,0:T(8,128)(2,1)S(1)} fusion(bf16[2304,128]{1,0:T(8,128)(2,1)} %bitcast.13, bf16[2304,128]{1,0:T(8,128)(2,1)} %bitcast.14), kind=kLoop, calls=%fused_computation | loop fusion | flops 2359296 | bytes 2359296 | tf_op jit(solution)/shard_map/concatenate | solution.py:541
  37.2 3.3 %collective-permute-done.refs_1_ = bf16[1296,128]{1,0:T(8,128)(2,1)S(1)} collective-permute-done((bf16[1296,128]{1,0:T(8,128)(2,1)S(1)}, bf16[1296,128]{1,0:T(8,128)(2,1)S(1)}, u32[]{:S(2)}, u32[]{:S(2)}) %collective-permute-start) | collective-permute-done | bytes 331808 | tf_op jit(solution)/shard_map/ppermute | solution.py:515
  40.4 8.1 %collective-permute-done.1.refs_2_ = bf16[1296,128]{1,0:T(8,128)(2,1)S(1)} collective-permute-done((bf16[1296,128]{1,0:T(8,128)(2,1)S(1)}, bf16[1296,128]{1,0:T(8,128)(2,1)S(1)}, u32[]{:S(2)}, u32[]{:S(2)}) %collective-permute-start.1) | collective-permute-done | bytes 331808 | tf_op jit(solution)/shard_map/ppermute | solution.py:515
  48.5 0.0 collective-permute-done.2.refs_3_
  48.5 1.6 %shard_map.75 = (bf16[4,640,128]{2,1,0:T(8,128)(2,1)}, s32[1]{0:T(128)}) custom-call(bf16[1296,128]{1,0:T(8,128)(2,1)S(1)} %get-tuple-element.51.refs_0_, bf16[1296,128]{1,0:T(8,128)(2,1)S(1)} %collective-permute-done.refs_1_, bf16[1296,128]{1,0:T(8,128)(2,1)S(1)} %collective-permute-done.1.refs_2_, bf16[1296,128]{1,0:T(8,128)(2,1)S(1)} %collective-permute-done.2.refs_3_), custom_call_target="tpu_custom_call" | custom-call | tf_op jit(solution)/shard_map/pallas_call | solution.py:194
  50.2 0.0 copy-done.4
  50.2 0.0 copy-done.6
  50.2 0.0 copy-done.8
  50.2 0.0 copy-done.9
  50.2 0.0 copy-start.2
  50.2 0.7 while.9
  51.0 1.9 %collective-permute-start.3 = (bf16[4,640,128]{2,1,0:T(8,128)(2,1)}, bf16[4,640,128]{2,1,0:T(8,128)(2,1)S(1)}, u32[]{:S(2)}, u32[]{:S(2)}) collective-permute-start(bf16[4,640,128]{2,1,0:T(8,128)(2,1)} %get-tuple-element.143), channel_id=1, source_target_pairs={{0,1},{1,2},{2,3},{3,4},{4,5},{5,6},{6,7},{7,8},{8,9},{9,10},{10,1... | collective-permute-start | bytes 1966088 | tf_op jit(solution)/shard_map/ppermute | solution.py:531
  52.9 8.0 %collective-permute-start.4 = (bf16[4,640,128]{2,1,0:T(8,128)(2,1)}, bf16[4,640,128]{2,1,0:T(8,128)(2,1)S(1)}, u32[]{:S(2)}, u32[]{:S(2)}) collective-permute-start(bf16[4,640,128]{2,1,0:T(8,128)(2,1)} %get-tuple-element.143), channel_id=1, source_target_pairs={{1,0},{2,1},{3,2},{4,3},{5,4},{6,5},{7,6},{8,7},{9,8},{10,9},{11,1... | collective-permute-start | bytes 1966088 | tf_op jit(solution)/shard_map/ppermute | solution.py:532
  60.9 0.0 copy-done.2
  60.9 0.0 copy-start.3
  61.0 1.0 %copy-done.3 = bf16[8,256,128]{2,1,0:T(8,128)(2,1)S(1)} copy-done((bf16[8,256,128]{2,1,0:T(8,128)(2,1)S(1)}, bf16[8,256,128]{2,1,0:T(8,128)(2,1)}, u32[]{:S(2)}) %copy-start.3) | copy-done | bytes 524312
  62.0 7.7 %shard_map.76.near = f32[4,512,128]{2,1,0:T(8,128)S(1)} custom-call(s32[104]{0:T(128)S(1)} %reshape.25.lookup, bf16[4,640,128]{2,1,0:T(8,128)(2,1)} %get-tuple-element.143, bf16[4,512,128]{2,1,0:T(8,128)(2,1)S(1)} %bitcast.11, bf16[2304,256]{1,0:T(8,128)(2,1)S(1)} %pad_maximum_fusion.pair_weight, bf16[2304,128]{1,0:T(8,128)(2,1)S(1)} %bitcast.10), custom_call_target="tpu_custom_call" | custom-call | flops 10000000000 | bytes 40000000 | tf_op jit(solution)/shard_map/pallas_call | solution.py:472
  69.7 0.0 collective-permute-done.3.before
  69.7 0.0 collective-permute-done.4.after
  69.7 5.6 %shard_map.77 = bf16[4,512,128]{2,1,0:T(8,128)(2,1)} custom-call(s32[104]{0:T(128)S(1)} %reshape.23.lookup, bf16[4,640,128]{2,1,0:T(8,128)(2,1)S(1)} %collective-permute-done.3.before, bf16[4,640,128]{2,1,0:T(8,128)(2,1)S(1)} %collective-permute-done.4.after, f32[4,512,128]{2,1,0:T(8,128)S(1)} %shard_map.76.near, bf16[4,512,128]{2,1,0:T(8,128)(2,1)S(1)} %bitcast.12, ...), custom_call_target="tpu_custom_call" | custom-call | tf_op jit(solution)/shard_map/pallas_call | solution.py:490
  (1 shorter events, 0.0 us)
Async XLA Ops:
  4.1 4.9 %copy-start.11 = (s32[4,26]{1,0:T(4,128)S(1)}, s32[4,26]{1,0:T(4,128)}, u32[]{:S(2)}) copy-start(s32[4,26]{1,0:T(4,128)} %param.13) | copy-start | bytes 1252
  4.1 5.2 %copy-start.1 = (bf16[27,256,128]{2,1,0:T(8,128)(2,1)S(1)}, bf16[27,256,128]{2,1,0:T(8,128)(2,1)}, u32[]{:S(2)}) copy-start(bf16[27,256,128]{2,1,0:T(8,128)(2,1)} %param.15) | copy-start | bytes 5308420
  4.1 24.0 %all-to-all-start.1 = ((bf16[8,656,128]{2,1,0:T(8,128)(2,1)}), bf16[8,656,128]{2,1,0:T(8,128)(2,1)S(1)}, u32[]{:S(2)}, u32[]{:S(2)}) async-start(bf16[8,656,128]{2,1,0:T(8,128)(2,1)} %shard_map.73), calls=%async_computation.1 | async-start | bytes 2686976 | tf_op jit(solution)/shard_map/all_to_all | solution.py:512
  29.5 10.9 %collective-permute-start = (bf16[1296,128]{1,0:T(8,128)(2,1)S(1)}, bf16[1296,128]{1,0:T(8,128)(2,1)S(1)}, u32[]{:S(2)}, u32[]{:S(2)}) collective-permute-start(bf16[1296,128]{1,0:T(8,128)(2,1)S(1)} %get-tuple-element.52), channel_id=1, source_target_pairs={{0,8},{1,9},{2,10},{3,11},{4,12},{5,13},{6,14},{7,15},{8,16},{9,17... | collective-permute-start | bytes 995336 | tf_op jit(solution)/shard_map/ppermute | solution.py:515
  31.4 17.1 %collective-permute-start.1 = (bf16[1296,128]{1,0:T(8,128)(2,1)S(1)}, bf16[1296,128]{1,0:T(8,128)(2,1)S(1)}, u32[]{:S(2)}, u32[]{:S(2)}) collective-permute-start(bf16[1296,128]{1,0:T(8,128)(2,1)S(1)} %get-tuple-element.53), channel_id=1, source_target_pairs={{0,16},{1,17},{2,18},{3,19},{4,20},{5,21},{6,22},{7,23},{8,24},{9,... | collective-permute-start | bytes 995336 | tf_op jit(solution)/shard_map/ppermute | solution.py:515
  34.1 14.4 %collective-permute-start.2 = (bf16[1296,128]{1,0:T(8,128)(2,1)S(1)}, bf16[1296,128]{1,0:T(8,128)(2,1)S(1)}, u32[]{:S(2)}, u32[]{:S(2)}) collective-permute-start(bf16[1296,128]{1,0:T(8,128)(2,1)S(1)} %get-tuple-element.54), channel_id=1, source_target_pairs={{0,24},{1,25},{2,26},{3,27},{4,28},{5,29},{6,30},{7,31},{8,0},{9,1... | collective-permute-start | bytes 995336 | tf_op jit(solution)/shard_map/ppermute | solution.py:515
  35.7 14.5 %copy-start.4 = (bf16[8,512,128]{2,1,0:T(8,128)(2,1)S(1)}, bf16[8,512,128]{2,1,0:T(8,128)(2,1)}, u32[]{:S(2)}) copy-start(bf16[8,512,128]{2,1,0:T(8,128)(2,1)} %skip.1) | copy-start | bytes 3145732
  35.7 14.5 %copy-start.6 = (bf16[8,64,256]{2,1,0:T(8,128)(2,1)S(1)}, bf16[8,64,256]{2,1,0:T(8,128)(2,1)}, u32[]{:S(2)}) copy-start(bf16[8,64,256]{2,1,0:T(8,128)(2,1)} %parents.1) | copy-start | bytes 786436
  35.7 14.5 %copy-start.8 = (s32[8]{0:T(128)S(1)}, s32[8]{0:T(128)}, u32[]{:S(2)}) copy-start(s32[8]{0:T(128)} %parent_dest.1) | copy-start | bytes 100
  35.7 14.5 %copy-start.9 = (s32[8]{0:T(128)S(1)}, s32[8]{0:T(128)}, u32[]{:S(2)}) copy-start(s32[8]{0:T(128)} %skip_dest.1) | copy-start | bytes 100
  50.2 10.7 %copy-start.2 = (bf16[9,256,128]{2,1,0:T(8,128)(2,1)S(1)}, bf16[9,256,128]{2,1,0:T(8,128)(2,1)}, u32[]{:S(2)}) copy-start(bf16[9,256,128]{2,1,0:T(8,128)(2,1)} %get-tuple-element.74) | copy-start | bytes 1769476
  51.0 18.8 %collective-permute-start.3 = (bf16[4,640,128]{2,1,0:T(8,128)(2,1)}, bf16[4,640,128]{2,1,0:T(8,128)(2,1)S(1)}, u32[]{:S(2)}, u32[]{:S(2)}) collective-permute-start(bf16[4,640,128]{2,1,0:T(8,128)(2,1)} %get-tuple-element.143), channel_id=1, source_target_pairs={{0,1},{1,2},{2,3},{3,4},{4,5},{5,6},{6,7},{7,8},{8,9},{9,10},{10,1... | collective-permute-start | bytes 1966088 | tf_op jit(solution)/shard_map/ppermute | solution.py:531
  52.9 16.8 %collective-permute-start.4 = (bf16[4,640,128]{2,1,0:T(8,128)(2,1)}, bf16[4,640,128]{2,1,0:T(8,128)(2,1)S(1)}, u32[]{:S(2)}, u32[]{:S(2)}) collective-permute-start(bf16[4,640,128]{2,1,0:T(8,128)(2,1)} %get-tuple-element.143), channel_id=1, source_target_pairs={{1,0},{2,1},{3,2},{4,3},{5,4},{6,5},{7,6},{8,7},{9,8},{10,9},{11,1... | collective-permute-start | bytes 1966088 | tf_op jit(solution)/shard_map/ppermute | solution.py:532
  60.9 1.0 %copy-start.3 = (bf16[8,256,128]{2,1,0:T(8,128)(2,1)S(1)}, bf16[8,256,128]{2,1,0:T(8,128)(2,1)}, u32[]{:S(2)}) copy-start(bf16[8,256,128]{2,1,0:T(8,128)(2,1)} %param.14) | copy-start | bytes 1572868

commit v3 on v2

--- a/solution.py
+++ b/solution.py
@@ -26,118 +26,127 @@
     return out
 
 
-def first_kernel(parent_dest, skip_dest, base, parents, skip, out, stage, head, slot_of, sems):
+WAYS = ((0, 0), (0, 1), (1, 0), (3, 0), (2, 0), (2, 1), (1, 1), (3, 1))
+
+
+def column_at(column, j):
+    along, other = WAYS[j]
+    return ((column + 2 * along) & 6) | ((column ^ other) & 1)
+
+
+def first_kernel(parent_dest, skip_dest, place, parents, skip, *refs):
+    outs = refs[:COLUMNS]
+    slot_of, sems = refs[COLUMNS:]
     for q in range(2 * COLUMNS + 1):
         slot_of[q] = 0
     table = []
     for kind, dest in enumerate((skip_dest, parent_dest)):
         for s in range(SLOTS):
             d = dest[s]
-            local = jnp.where(d >= 0, d - base[0], -1)
+            local = jnp.where(d >= 0, d - place[2], -1)
             table.append(local)
-            column = lax.rem(lax.div(jnp.maximum(local, 0), BRICKS), COLUMNS)
+            column = (local >> 2) & 7
             slot_of[jnp.where(d >= 0, kind * COLUMNS + column, 2 * COLUMNS)] = s
-    head[...] = rows_of((HEAD_ROWS, 128), table).astype(F32).astype(BF16)
-    into, onward = [], []
-    for q in range(COLUMNS):
+    copies = []
+    for j in range(COLUMNS):
+        q = column_at(place[1], j)
         s, p = slot_of[q], slot_of[COLUMNS + q]
-        pieces = [(skip.at[s], slice(0, 512))] + [
-            (parents.at[p, :, 128 * half : 128 * half + 128], slice(512 + 64 * half, 576 + 64 * half))
-            for half in range(2)
-        ]
-        for j, (source, rows) in enumerate(pieces):
-            into.append(pltpu.make_async_copy(source, stage.at[q, rows], sems.at[0, q, j]))
-            onward.append(
-                pltpu.make_async_copy(stage.at[q, rows], out.at[q, rows], sems.at[1, q, j])
+        copies.append(pltpu.make_async_copy(skip.at[s], outs[j].at[0:512], sems.at[j, 0]))
+        for half in range(2):
+            copies.append(
+                pltpu.make_async_copy(
+                    parents.at[p, :, 128 * half : 128 * half + 128],
+                    outs[j].at[512 + 64 * half : 576 + 64 * half],
+                    sems.at[j, 1 + half],
+                )
             )
-        onward.append(
-            pltpu.make_async_copy(head, out.at[q, BODY : BODY + HEAD_ROWS], sems.at[1, q, 3])
-        )
-    for copy in into:
+    for copy in copies:
         copy.start()
-    for q in range(COLUMNS):
-        onward[4 * q + 3].start()
-    for q in range(COLUMNS):
-        for j in range(3):
-            into[3 * q + j].wait()
-            onward[4 * q + j].start()
-    for copy in onward:
+    head = rows_of((HEAD_ROWS, 128), table).astype(F32).astype(BF16)
+    for j in range(COLUMNS):
+        outs[j][BODY : BODY + HEAD_ROWS] = head
+    for copy in copies:
         copy.wait()
 
 
-def first_pack(parent_dest, skip_dest, base, parents, skip):
+def first_pack(parent_dest, skip_dest, place, parents, skip):
     return pl.pallas_call(
         first_kernel,
-        out_shape=jax.ShapeDtypeStruct((COLUMNS, BODY + HEAD_ROWS, 128), BF16),
+        out_shape=[jax.ShapeDtypeStruct((BODY + HEAD_ROWS, 128), BF16)] * COLUMNS,
         in_specs=[SMEM, SMEM, SMEM, ANY, ANY],
-        out_specs=ANY,
+        out_specs=[VMEM] * COLUMNS,
         scratch_shapes=[
-            pltpu.VMEM((COLUMNS, BODY, 128), BF16),
-            pltpu.VMEM((HEAD_ROWS, 128), BF16),
             pltpu.SMEM((2 * COLUMNS + 1,), I32),
-            pltpu.SemaphoreType.DMA((2, COLUMNS, 4)),
-        ],
-    )(parent_dest, skip_dest, base, parents, skip)
-
-
-def second_kernel(place, came, *refs):
-    outs = refs[:LINES]
-    found, table, counts, source, landing, sem = refs[LINES:]
+            pltpu.SemaphoreType.DMA((COLUMNS, 3)),
+        ],
+        compiler_params=pltpu.CompilerParams(vmem_limit_bytes=FIRST_LIMIT),
+    )(parent_dest, skip_dest, place, parents, skip)
+
+
+FIRST_LIMIT = 16 * 2**20
+
+
+HOPS = (0, 2, 1, 3)
+
+
+def second_kernel(place, *refs):
+    came, outs = refs[:COLUMNS], refs[COLUMNS : COLUMNS + LINES]
+    found, table, counts, landing, sem = refs[COLUMNS + LINES :]
     line, column = place[0], place[1]
+    over = jnp.zeros((1, 128), I32)
+    totals = [jnp.zeros((1, 128), I32)] * 2
+    row = lax.broadcasted_iota(I32, (SLOTS, 128), 0)
+    lane = lax.broadcasted_iota(I32, (SLOTS, 128), 1)
+    picks = jnp.full((SLOTS, 128), -1, I32)
+    for m in range(COLUMNS):
+        every = came[m][BODY : BODY + HEAD_ROWS].astype(F32).astype(I32)
+        for kind in range(2):
+            dest = every[kind * SLOTS : kind * SLOTS + SLOTS]
+            live = dest >= 0
+            owner = dest >> 2
+            its_column = owner & 7
+            mine = jnp.where(live & (its_column == column), dest, -1)
+            picks = jnp.where(
+                (row == m) & (lane == kind), jnp.max(mine, axis=0, keepdims=True), picks
+            )
+            to_column = jnp.where(live & (its_column == lane), 1, 0)
+            over = over | jnp.where(jnp.sum(to_column, axis=0, keepdims=True) > 1, 1, 0)
+            to_owner = jnp.where(live & (owner == lane), 1, 0)
+            totals[kind] = totals[kind] + jnp.sum(to_owner, axis=0, keepdims=True)
+    found[...] = picks
+    copy = pltpu.make_async_copy(found, table, sem)
+    copy.start()
     for j in range(2 * LINES + 1):
         counts[j] = 0
     for j in range(2 * LINES * DEPTH + 1):
-        source[j] = 0
         landing[j] = -1
-    lane = lax.broadcasted_iota(I32, (COLUMNS, SLOTS, 128), 2)
-    over = jnp.zeros((1, 128), I32)
-    picks = []
-    every = came[:, BODY : BODY + HEAD_ROWS].astype(F32).astype(I32)
     for kind in range(2):
-        dest = every[:, kind * SLOTS : kind * SLOTS + SLOTS]
-        live = dest >= 0
-        owner = dest >> 2
-        its_column = owner & 7
-        mine = jnp.where(live & (its_column == column), dest, -1)
-        picks.append(jnp.max(mine, axis=1))
-        to_column = jnp.where(live & (its_column == lane), 1, 0)
-        over = over | jnp.where(
-            jnp.max(jnp.sum(to_column, axis=1), axis=0, keepdims=True) > 1, 1, 0
-        )
-        to_owner = jnp.where(live & (owner == lane), 1, 0)
-        total = jnp.sum(jnp.sum(to_owner, axis=1), axis=0, keepdims=True)
-        over = over | jnp.where(total > DEPTH, 1, 0)
+        over = over | jnp.where(totals[kind] > DEPTH, 1, 0)
     flag = jnp.max(over.astype(F32), axis=1, keepdims=True).astype(I32)
-    lane = lax.broadcasted_iota(I32, (COLUMNS, 128), 1)
-    found[...] = jnp.where(lane == 0, picks[0], picks[1])
-    copy = pltpu.make_async_copy(found, table, sem)
-    copy.start()
     copy.wait()
-    for kind in range(2):
-        for m in range(COLUMNS):
+    for m in range(COLUMNS):
+        for kind, (rows, first, height) in enumerate(PIECES):
             dest = table[m, kind]
             live = dest >= 0
-            to_line = jnp.where(live, dest >> 5, 0)
-            count_at = jnp.where(live, kind * LINES + to_line, 2 * LINES)
+            ahead = ((dest >> 5) - line) & 3
+            count_at = jnp.where(live, kind * LINES + ahead, 2 * LINES)
             rank = counts[count_at]
             counts[count_at] = rank + 1
-            spot = jnp.where(
-                live & (rank < DEPTH),
-                (kind * LINES + to_line) * DEPTH + rank,
-                2 * LINES * DEPTH,
-            )
-            source[spot] = m
-            landing[spot] = dest & 3
+            fits = live & (rank < DEPTH)
+            spot = (kind * LINES + ahead) * DEPTH + rank
+            landing[jnp.where(fits, spot, 2 * LINES * DEPTH)] = dest & 3
+            at = pl.multiple_of(height + jnp.where(fits, rank, 0) * rows, 128)
+            for k in range(LINES):
+
+                @pl.when(fits & (ahead == HOPS[k]))
+                def _(m=m, k=k, rows=rows, first=first, at=at):
+                    outs[k][pl.ds(at, rows)] = came[m][first : first + rows]
+
     for k in range(LINES):
-        to_line = lax.rem(line + k, LINES)
-        spots = []
-        for kind, (rows, first, height) in enumerate(PIECES):
-            for r in range(DEPTH):
-                spot = (kind * LINES + to_line) * DEPTH + r
-                spots.append(landing[spot])
-                outs[k][height + r * rows : height + r * rows + rows] = came[
-                    source[spot], first : first + rows
-                ]
+        spots = [
+            landing[(kind * LINES + HOPS[k]) * DEPTH + r]
+            for kind in range(2) for r in range(DEPTH)
+        ]
         outs[k][BODY * DEPTH : BODY * DEPTH + HEAD_ROWS] = (
             rows_of((HEAD_ROWS, 128), spots + [flag]).astype(F32).astype(BF16)
         )
@@ -148,23 +157,41 @@
     return pl.pallas_call(
         second_kernel,
         out_shape=[message] * LINES,
-        in_specs=[SMEM, VMEM],
+        in_specs=[SMEM] + [VMEM] * COLUMNS,
         out_specs=[VMEM] * LINES,
         scratch_shapes=[
             pltpu.VMEM((COLUMNS, 128), I32),
             pltpu.SMEM((COLUMNS, 128), I32),
             pltpu.SMEM((2 * LINES + 1,), I32),
             pltpu.SMEM((2 * LINES * DEPTH + 1,), I32),
-            pltpu.SMEM((2 * LINES * DEPTH + 1,), I32),
             pltpu.SemaphoreType.DMA,
         ],
         compiler_params=pltpu.CompilerParams(vmem_limit_bytes=16 * 2**20),
-    )(place, came)
+    )(place, *came)
+
+
+SURFACE = 352
+
+
+def keep_surface(own, surface, plain):
+    for b in range(BRICKS):
+        plain[...] = own[b, 0:SKIP_ROWS].astype(F32)
+        surface[b, 0:64] = own[b, 0:64]
+        surface[b, 64:128] = own[b, 448:512]
+        for side in range(2):
+            lines = [
+                plain[x * 64 + 56 * side : x * 64 + 56 * side + 8] for x in range(1, 7)
+            ]
+            surface[b, 128 + 48 * side : 176 + 48 * side] = jnp.concatenate(lines).astype(BF16)
+            surface[b, 224 + 64 * side : 288 + 64 * side] = plain[
+                pl.ds(7 * side, 64, stride=8)
+            ].astype(BF16)
+        surface[b, SURFACE : SURFACE + PARENT_ROWS] = own[b, SKIP_ROWS:BODY]
 
 
 def unpack_kernel(*refs):
     came = refs[:LINES]
-    own, flag_out, found, table, sem = refs[LINES:]
+    own, surface, flag_out, plain, found, table, sem = refs[LINES:]
     lane = lax.broadcasted_iota(I32, (HEAD_ROWS, 128), 1)
     row = lax.broadcasted_iota(I32, (HEAD_ROWS, 128), 0)
     for k in range(LINES):
@@ -189,17 +216,21 @@
                 def _(k=k, rows=rows, first=first, at=height + r * rows, brick=brick):
                     own[brick, first : first + rows] = came[k][at : at + rows]
 
+    keep_surface(own, surface, plain)
+
 
 def unpack(messages):
     return pl.pallas_call(
         unpack_kernel,
         out_shape=[
             jax.ShapeDtypeStruct((BRICKS, BODY, 128), BF16),
+            jax.ShapeDtypeStruct((BRICKS, SURFACE + PARENT_ROWS, 128), BF16),
             jax.ShapeDtypeStruct((1,), I32),
         ],
         in_specs=[VMEM] * LINES,
-        out_specs=[VMEM, SMEM],
+        out_specs=[VMEM, VMEM, SMEM],
         scratch_shapes=[
+            pltpu.VMEM((SKIP_ROWS, 128), F32),
             pltpu.VMEM((8, 128), I32),
             pltpu.SMEM((8, 128), I32),
             pltpu.SemaphoreType.DMA,
@@ -208,12 +239,12 @@
     )(*messages)
 
 
-def dense_pack_kernel(parent_dest, skip_dest, base, parents, skip, out, head, sems, sem):
+def dense_pack_kernel(parent_dest, skip_dest, place, parents, skip, out, head, sems, sem):
     table = []
     copies = []
     for kind, dest in enumerate((skip_dest, parent_dest)):
         for s in range(SLOTS):
-            local = jnp.where(dest[s] >= 0, dest[s] - base[0], -1)
+            local = jnp.where(dest[s] >= 0, dest[s] - place[2], -1)
             table.append(local)
             owner = lax.div(jnp.maximum(local, 0), BRICKS)
             if kind == 0:
@@ -241,7 +272,7 @@
         pl.when(live >= 0)(copy.wait)
 
 
-def dense_unpack_kernel(place, came, own, heads, found, table, sems, sem):
+def dense_unpack_kernel(place, came, own, surface, plain, heads, found, table, sems, sem):
     devices = LINES * COLUMNS
     copy = pltpu.make_async_copy(came.at[:, BODY : BODY + HEAD_ROWS], heads, sem)
     copy.start()
@@ -271,8 +302,10 @@
                 copy.start()
                 copy.wait()
 
-
-def dense_route(place, base, parents, parent_dest, skip, skip_dest):
+    keep_surface(own, surface, plain)
+
+
+def dense_route(place, parents, parent_dest, skip, skip_dest):
     devices = LINES * COLUMNS
     limit = pltpu.CompilerParams(vmem_limit_bytes=16 * 2**20)
     rows = pl.pallas_call(
@@ -286,14 +319,18 @@
             pltpu.SemaphoreType.DMA,
         ],
         compiler_params=limit,
-    )(parent_dest, skip_dest, base, parents, skip)
+    )(parent_dest, skip_dest, place, parents, skip)
     came = lax.all_to_all(rows, "gy", 0, 0, tiled=True)
     return pl.pallas_call(
         dense_unpack_kernel,
-        out_shape=jax.ShapeDtypeStruct((BRICKS, BODY, 128), BF16),
+        out_shape=[
+            jax.ShapeDtypeStruct((BRICKS, BODY, 128), BF16),
+            jax.ShapeDtypeStruct((BRICKS, SURFACE + PARENT_ROWS, 128), BF16),
+        ],
         in_specs=[SMEM, ANY],
-        out_specs=VMEM,
+        out_specs=[VMEM, VMEM],
         scratch_shapes=[
+            pltpu.VMEM((SKIP_ROWS, 128), F32),
             pltpu.VMEM((devices, HEAD_ROWS, 128), BF16),
             pltpu.VMEM((devices, 128), I32),
             pltpu.SMEM((devices, 128), I32),
@@ -304,7 +341,7 @@
     )(place, came)
 
 
-def fill_pool(pool, groups, up_weight):
+def fill_pool(pool, groups, up_weight, parents_at):
     row = lax.broadcasted_iota(I32, (256, 64), 0)
     column = lax.broadcasted_iota(I32, (256, 64), 1)
     in_brick = row & 127
@@ -313,10 +350,25 @@
     for group, bricks in enumerate(groups):
         spaced = []
         for b in range(BRICKS):
-            pool[group * BRICKS + b, 1] = bricks[b, 0:512].astype(F32)
+            into = pool.at[group * BRICKS + b, 1]
+            if parents_at == SKIP_ROWS:
+                into[...] = bricks[b, 0:SKIP_ROWS].astype(F32)
+            else:
+                into[0:64] = bricks[b, 0:64].astype(F32)
+                into[448:512] = bricks[b, 64:128].astype(F32)
+                for side in range(2):
+                    lines = bricks[b, 128 + 48 * side : 176 + 48 * side].astype(F32)
+                    for x in range(1, 7):
+                        first = x * 64 + 56 * side
+                        into[first : first + 8] = lines[x * 8 - 8 : x * 8]
+                    pool[group * BRICKS + b, 1, pl.ds(7 * side, 64, stride=8)] = bricks[
+                        b, 224 + 64 * side : 288 + 64 * side
+                    ].astype(F32)
             halves = [
                 jnp.dot(
-                    spread, bricks[b, 512 + 64 * h : 576 + 64 * h], preferred_element_type=F32
+                    spread,
+                    bricks[b, parents_at + 64 * h : parents_at + 64 * h + 64],
+                    preferred_element_type=F32,
                 ).astype(BF16)
                 for h in range(2)
             ]
@@ -326,9 +378,10 @@
                 )
             )
         spaced = jnp.concatenate(spaced, axis=0)
+        every = jnp.dot(spaced, up_weight[...], preferred_element_type=F32)
+        every = every.astype(BF16).astype(F32)
         for ab in range(4):
-            made = jnp.dot(spaced, up_weight[ab], preferred_element_type=F32)
-            made = made.astype(BF16).astype(F32)
+            made = every[:, ab * 128 : ab * 128 + 128]
             for b in range(BRICKS):
                 for i in range(4):
                     for j in range(4):
@@ -357,9 +410,9 @@
 
 
 def near_kernel(
-    lookup, own, up_weight, pair_weight, last_weight, out, pool, shifted_pair, window_pair
+    lookup, own, up_weight, pair_weight, conv_weight, out, pool, shifted_pair, window_pair
 ):
-    fill_pool(pool, (own,), up_weight)
+    fill_pool(pool, (own,), up_weight, SKIP_ROWS)
     spans = {-1: (7, 8, 0), 0: (0, 8, 1), 1: (0, 1, 9)}
 
     for b in range(BRICKS):
@@ -388,27 +441,27 @@
                     shifted[step_z, :, step_y : step_y + 8].reshape(640, 256).astype(BF16)
                 )
         pair = jnp.dot(window[0:576], pair_weight[...], preferred_element_type=F32)
-        last = jnp.dot(window[128:640], last_weight[...], preferred_element_type=F32)
+        last = jnp.dot(window[128:640], conv_weight[2], preferred_element_type=F32)
         out[b] = pair[0:512, 0:128] + pair[64:576, 128:256] + last
 
 
 def far_kernel(
     lookup, before, after, near, up_weight, conv_weight, out, pool, shifted, window, total
 ):
-    fill_pool(pool, (before, after), up_weight)
+    fill_pool(pool, (before, after), up_weight, SURFACE)
     total[...] = near[...].reshape(BRICKS * 512, 128)
     shifted[...] = jnp.zeros(shifted.shape, F32)
 
-    @pl.loop(0, BRICKS)
-    def _(b):
-        def brick(*offsets):
+    for b in range(BRICKS):
+
+        def brick(*offsets, b=b):
             return lookup[b * 26 + code_of(*offsets)]
 
-        def keep(side):
+        def keep(side, b=b):
             for step in range(3):
                 for inner in range(3):
                     first = (step * 3 + inner) * 256
-                    window[side, pl.ds(pl.multiple_of(b * 64, 64), 64), first : first + 256] = (
+                    window[side, b * 64 : b * 64 + 64, first : first + 256] = (
                         shifted[side, inner, step : step + 8].reshape(64, 256).astype(BF16)
                     )
 
@@ -468,7 +521,7 @@
     out[...] = jnp.maximum(total[...], 0.0).astype(BF16).reshape(BRICKS, 512, 128)
 
 
-def convolve_near(lookup, own, up_weight, pair_weight, last_weight):
+def convolve_near(lookup, own, up_weight, pair_weight, conv_weight):
     return pl.pallas_call(
         near_kernel,
         out_shape=jax.ShapeDtypeStruct((BRICKS, 512, 128), F32),
@@ -483,7 +536,7 @@
         cost_estimate=pl.CostEstimate(
             flops=10**10, bytes_accessed=4 * 10**7, transcendentals=0
         ),
-    )(lookup, own, up_weight, pair_weight, last_weight)
+    )(lookup, own, up_weight, pair_weight, conv_weight)
 
 
 def convolve_far(lookup, before, after, near, up_weight, conv_weight):
@@ -505,42 +558,41 @@
 def per_device(parents, parent_dest, skip, skip_dest, neighbours, up_weight, conv_weight):
     row, inner = lax.axis_index("gx"), lax.axis_index("gy")
     devices = LINES * COLUMNS
-    base = (row * devices * BRICKS).reshape(1)
-    place = jnp.stack([inner // COLUMNS, inner % COLUMNS])
-    groups = [[x * COLUMNS + q for q in range(COLUMNS)] for x in range(LINES)]
-    first = first_pack(parent_dest, skip_dest, base, parents, skip)
-    came = lax.all_to_all(first, "gy", 0, 0, tiled=True, axis_index_groups=groups)
+    place = jnp.stack([inner // COLUMNS, inner % COLUMNS, row * devices * BRICKS])
+    first = first_pack(parent_dest, skip_dest, place, parents, skip)
+    came = [first[0]]
+    for j in range(1, COLUMNS):
+        steps = [(i, i // COLUMNS * COLUMNS + column_at(i % COLUMNS, j)) for i in range(devices)]
+        came.append(lax.ppermute(first[j], "gy", steps))
     messages = second_pack(place, came)
-    arrived = [messages[0]] + [
-        lax.ppermute(
-            messages[k], "gy", [(i, (i + k * COLUMNS) % devices) for i in range(devices)]
-        )
-        for k in range(1, LINES)
-    ]
-    own, flag = unpack(arrived)
-    own, _ = lax.while_loop(
-        lambda state: state[1][0] > 0,
+    arrived = [messages[0]]
+    for k in range(1, LINES):
+        steps = [(i, (i + HOPS[k] * COLUMNS) % devices) for i in range(devices)]
+        arrived.append(lax.ppermute(messages[k], "gy", steps))
+    own, surface, flag = unpack(arrived)
+    own, surface, _ = lax.while_loop(
+        lambda state: state[2][0] > 0,
         lambda state: (
-            dense_route(place, base, parents, parent_dest, skip, skip_dest),
-            jnp.zeros_like(state[1]),
+            *dense_route(place, parents, parent_dest, skip, skip_dest),
+            jnp.zeros_like(state[2]),
         ),
-        (own, flag),
+        (own, surface, flag),
     )
     whole = lax.axis_size(("gx", "gy"))
     up = [(i, i + 1) for i in range(whole - 1)]
-    before = lax.ppermute(own, ("gx", "gy"), up)
-    after = lax.ppermute(own, ("gx", "gy"), [(j, i) for i, j in up])
+    before = lax.ppermute(surface, ("gx", "gy"), up)
+    after = lax.ppermute(surface, ("gx", "gy"), [(j, i) for i, j in up])
     me = row * devices + inner
     ahead = neighbours - me * BRICKS
     here = (neighbours >= 0) & (ahead >= 0) & (ahead < BRICKS)
     near_lookup = jnp.where(here, ahead, BRICKS)
     far = jnp.where(ahead < 0, ahead + BRICKS, ahead)
     far_lookup = jnp.where((neighbours >= 0) & ~here, far, 2 * BRICKS)
-    up_weight = up_weight.reshape(4, 512, 128)
+    up_weight = up_weight.reshape(4, 512, 128).transpose(1, 0, 2).reshape(512, 512)
     conv_weight = conv_weight.reshape(3, 9 * 256, 128)
     pair_weight = jnp.concatenate([conv_weight[0], conv_weight[1]], axis=1)
     near = convolve_near(
-        near_lookup.reshape(-1), own, up_weight, pair_weight, conv_weight[2]
+        near_lookup.reshape(-1), own, up_weight, pair_weight, conv_weight
     )
     return convolve_far(far_lookup.reshape(-1), before, after, near, up_weight, conv_weight)
 

time: 75.9 us -> 71.1 us (0.937)
  waiting for transfers between devices: 29 us -> 20.9 us
  starting transfers between devices: 21 us -> 26.2 us
  Pallas kernels: 20.5 us -> 19.7 us
    all_to_all x1 -> x0, waiting for transfers between devices: 17.6 us -> none  [per_device(): lax.all_to_all(first, 'gy', 0, 0, tiled=True, axis_index_groups=groups)]
    ppermute x5 -> x12, starting transfers between devices: 16.1 us -> 26.2 us  [the longest x7 9.85 us: per_device(): came.append(lax.ppermute(first[j], 'gy', steps))]
    ppermute x5 -> x12, waiting for transfers between devices: 11.4 us -> 20.9 us  [the longest x3 12.4 us: per_device(): arrived.append(lax.ppermute(messages[k], 'gy', steps))]
    all_to_all x1 -> x0, starting transfers between devices: 4.88 us -> none  [per_device(): lax.all_to_all(first, 'gy', 0, 0, tiled=True, axis_index_groups=groups)]
    reshape x0 -> x1, local copies, waits for them, and re-layouts: none -> 1.45 us  [per_device(): up_weight.reshape(4, 512, 128).transpose(1, 0, 2).reshape(512, 512)]
    concatenate x1, other arithmetic: 1.47 us -> 0.13 us  [per_device(): pair_weight = jnp.concatenate([conv_weight[0], conv_weight[1]], axis=1)]
    slice x1, local copies, waits for them, and re-layouts: 1.26 us -> 0.1 us  [per_device(): pair_weight = jnp.concatenate([conv_weight[0], conv_weight[1]], axis=1)]
  transfers between devices with their start and end apart: 6 -> 12, of which waited for: 3 -> 6; matrix products, arithmetic and copies ran while one was open for 4% -> 4% of each run, Pallas kernels for 10% -> 11%
where the time goes in v3:
time: 71.1 us; the launch traced here: 70.9 us
  starting transfers between devices  26.2 us (37%)
  waiting for transfers between devices  20.9 us (29%)
  Pallas kernels  19.7 us (28%)
  local copies, waits for them, and re-layouts  2.46 us (3%)
  other arithmetic  0.9 us (1%)
    ppermute x3, waiting for transfers between devices, per_device(): arrived.append(lax.ppermute(messages[k], 'gy', steps))  12.4 us
    ppermute x7, starting transfers between devices, per_device(): came.append(lax.ppermute(first[j], 'gy', steps))  9.85 us
    ppermute x7, waiting for transfers between devices, per_device(): came.append(lax.ppermute(first[j], 'gy', steps))  8.51 us
    ppermute x1, starting transfers between devices, per_device(): after = lax.ppermute(surface, ('gx', 'gy'), [(j, i) for i, j in up])  8.04 us
    pallas_call x1, Pallas kernels, convolve_near(): pl.pallas_call(near_kernel, out_shape=jax.ShapeDtypeStruct((BRICKS, 512,...  7.56 us
    ppermute x3, starting transfers between devices, per_device(): arrived.append(lax.ppermute(messages[k], 'gy', steps))  6.35 us
    pallas_call x1, Pallas kernels, convolve_far(): pl.pallas_call(far_kernel, out_shape=jax.ShapeDtypeStruct((BRICKS, 512, 1...  4.91 us
    pallas_call x1, Pallas kernels, first_pack(): pl.pallas_call(first_kernel, out_shape=[jax.ShapeDtypeStruct((BODY + HEAD...  3.62 us
  transfers between devices with their start and end apart: 12, of which 6 were waited for; matrix products, arithmetic and copies ran while one was open for 4% of the time, Pallas kernels for 11%

profile of v3, /device:TPU:16, one launch (start us, length us, event | category | flops | bytes accessed | tf_op | source)
XLA Modules:
  0.0 70.9 jit_solution(6872045549979443362)
XLA Ops:
  0.0 0.0 copy-start.1
  0.0 0.1 pad_add_fusion.place
  0.1 3.6 %shard_map.73 = (bf16[656,128]{1,0:T(8,128)(2,1)S(1)}, bf16[656,128]{1,0:T(8,128)(2,1)}, bf16[656,128]{1,0:T(8,128)(2,1)}, bf16[656,128]{1,0:T(8,128)(2,1)}, bf1...) custom-call(s32[8]{0:T(128)} %parent_dest.1, ...), custom_call_target="tpu_custom_call" | custom-call | tf_op jit(solution)/shard_map/pallas_call | solution.py:73
  3.7 0.0 copy-start.2
  3.7 0.6 copy-done.2
  4.4 0.0 collective-permute-start
  4.4 1.7 %collective-permute-start.1 = (bf16[656,128]{1,0:T(8,128)(2,1)}, bf16[656,128]{1,0:T(8,128)(2,1)S(1)}, u32[]{:S(2)}, u32[]{:S(2)}) collective-permute-start(bf16[656,128]{1,0:T(8,128)(2,1)} %get-tuple-element.64), channel_id=1, source_target_pairs={{0,2},{1,3},{2,4},{3,5},{4,6},{5,7},{6,0},{7,1},{8,10},{9,11},{10,... | collective-permute-start | bytes 503816 | tf_op jit(solution)/shard_map/ppermute | solution.py:566
  6.0 2.1 %collective-permute-start.2 = (bf16[656,128]{1,0:T(8,128)(2,1)}, bf16[656,128]{1,0:T(8,128)(2,1)S(1)}, u32[]{:S(2)}, u32[]{:S(2)}) collective-permute-start(bf16[656,128]{1,0:T(8,128)(2,1)} %get-tuple-element.65), channel_id=1, source_target_pairs={{0,6},{1,7},{2,0},{3,1},{4,2},{5,3},{6,4},{7,5},{8,14},{9,15},{10,... | collective-permute-start | bytes 503816 | tf_op jit(solution)/shard_map/ppermute | solution.py:566
  8.2 1.9 %collective-permute-start.3 = (bf16[656,128]{1,0:T(8,128)(2,1)}, bf16[656,128]{1,0:T(8,128)(2,1)S(1)}, u32[]{:S(2)}, u32[]{:S(2)}) collective-permute-start(bf16[656,128]{1,0:T(8,128)(2,1)} %get-tuple-element.66), channel_id=1, source_target_pairs={{0,4},{1,5},{2,6},{3,7},{4,0},{5,1},{6,2},{7,3},{8,12},{9,13},{10,... | collective-permute-start | bytes 503816 | tf_op jit(solution)/shard_map/ppermute | solution.py:566
  10.0 1.2 %collective-permute-start.4 = (bf16[656,128]{1,0:T(8,128)(2,1)}, bf16[656,128]{1,0:T(8,128)(2,1)S(1)}, u32[]{:S(2)}, u32[]{:S(2)}) collective-permute-start(bf16[656,128]{1,0:T(8,128)(2,1)} %get-tuple-element.67), channel_id=1, source_target_pairs={{0,5},{1,4},{2,7},{3,6},{4,1},{5,0},{6,3},{7,2},{8,13},{9,12},{10,... | collective-permute-start | bytes 503816 | tf_op jit(solution)/shard_map/ppermute | solution.py:566
  11.3 0.7 fusion.1
  11.9 0.1 reshape.22.lookup
  12.0 1.4 %copy.8 = bf16[4,512,128]{2,0,1:T(4,128)(2,1)S(1)} copy(bf16[4,512,128]{2,1,0:T(8,128)(2,1)} %bitcast.20) | data formatting | bytes 1048576 | tf_op jit(solution)/shard_map/reshape | solution.py:591
  13.5 0.1 copy.11
  13.6 0.1 reshape.21.lookup
  13.6 0.0 collective-permute-done.refs_1_
  13.7 0.1 collective-permute-start.5
  13.7 0.0 collective-permute-done.1.refs_2_
  13.7 2.9 %collective-permute-start.6 = (bf16[656,128]{1,0:T(8,128)(2,1)S(1)}, bf16[656,128]{1,0:T(8,128)(2,1)S(1)}, u32[]{:S(2)}, u32[]{:S(2)}) collective-permute-start(bf16[656,128]{1,0:T(8,128)(2,1)S(1)} %get-tuple-element.69), channel_id=1, source_target_pairs={{0,7},{1,6},{2,1},{3,0},{4,3},{5,2},{6,5},{7,4},{8,15},{9,14},{10,... | collective-permute-start | bytes 503816 | tf_op jit(solution)/shard_map/ppermute | solution.py:566
  16.6 0.0 copy-done.1
  16.6 0.1 fusion.2
  16.7 3.4 %collective-permute-done.2.refs_3_ = bf16[656,128]{1,0:T(8,128)(2,1)S(1)} collective-permute-done((bf16[656,128]{1,0:T(8,128)(2,1)}, bf16[656,128]{1,0:T(8,128)(2,1)S(1)}, u32[]{:S(2)}, u32[]{:S(2)}) %collective-permute-start.2) | collective-permute-done | bytes 167968 | tf_op jit(solution)/shard_map/ppermute | solution.py:566
  20.1 0.0 collective-permute-done.3.refs_4_
  20.1 1.3 %collective-permute-done.4.refs_5_ = bf16[656,128]{1,0:T(8,128)(2,1)S(1)} collective-permute-done((bf16[656,128]{1,0:T(8,128)(2,1)}, bf16[656,128]{1,0:T(8,128)(2,1)S(1)}, u32[]{:S(2)}, u32[]{:S(2)}) %collective-permute-start.4) | collective-permute-done | bytes 167968 | tf_op jit(solution)/shard_map/ppermute | solution.py:566
  21.4 3.8 %collective-permute-done.5.refs_6_ = bf16[656,128]{1,0:T(8,128)(2,1)S(1)} collective-permute-done((bf16[656,128]{1,0:T(8,128)(2,1)}, bf16[656,128]{1,0:T(8,128)(2,1)S(1)}, u32[]{:S(2)}, u32[]{:S(2)}) %collective-permute-start.5) | collective-permute-done | bytes 167968 | tf_op jit(solution)/shard_map/ppermute | solution.py:566
  25.2 0.0 collective-permute-done.6.refs_7_
  25.2 1.8 %shard_map.74 = (bf16[1296,128]{1,0:T(8,128)(2,1)S(1)}, bf16[1296,128]{1,0:T(8,128)(2,1)S(1)}, bf16[1296,128]{1,0:T(8,128)(2,1)S(1)}, bf16[1296,128]{1,0:T(8,128)(2,1)S(1)}) custom-call(s32[3]{0:T(128)S(1)} %pad_add_fusion.place, bf16[656,128]{1,0:T(8,128)(2,1)S(1)} %get-tuple-element.62.refs_0_, bf16[656,128]{1,0:T(8,128)(2,1)S(1)} %collective-permute-done.refs_1_, ...), custom_call_target="tpu_custom_call" | custom-call | tf_op jit(solution)/shard_map/pallas_call | solution.py:157
  27.1 3.1 %collective-permute-start.7 = (bf16[1296,128]{1,0:T(8,128)(2,1)S(1)}, bf16[1296,128]{1,0:T(8,128)(2,1)S(1)}, u32[]{:S(2)}, u32[]{:S(2)}) collective-permute-start(bf16[1296,128]{1,0:T(8,128)(2,1)S(1)} %get-tuple-element.71), channel_id=1, source_target_pairs={{0,16},{1,17},{2,18},{3,19},{4,20},{5,21},{6,22},{7,23},{8,24},{9,... | collective-permute-start | bytes 995336 | tf_op jit(solution)/shard_map/ppermute | solution.py:571
  30.2 0.9 %collective-permute-start.8 = (bf16[1296,128]{1,0:T(8,128)(2,1)S(1)}, bf16[1296,128]{1,0:T(8,128)(2,1)S(1)}, u32[]{:S(2)}, u32[]{:S(2)}) collective-permute-start(bf16[1296,128]{1,0:T(8,128)(2,1)S(1)} %get-tuple-element.72), channel_id=1, source_target_pairs={{0,8},{1,9},{2,10},{3,11},{4,12},{5,13},{6,14},{7,15},{8,16},{9,17... | collective-permute-start | bytes 995336 | tf_op jit(solution)/shard_map/ppermute | solution.py:571
  31.0 2.4 %collective-permute-start.9 = (bf16[1296,128]{1,0:T(8,128)(2,1)S(1)}, bf16[1296,128]{1,0:T(8,128)(2,1)S(1)}, u32[]{:S(2)}, u32[]{:S(2)}) collective-permute-start(bf16[1296,128]{1,0:T(8,128)(2,1)S(1)} %get-tuple-element.73), channel_id=1, source_target_pairs={{0,24},{1,25},{2,26},{3,27},{4,28},{5,29},{6,30},{7,31},{8,0},{9,1... | collective-permute-start | bytes 995336 | tf_op jit(solution)/shard_map/ppermute | solution.py:571
  33.4 0.0 copy-start.3
  33.4 0.0 copy-start.5
  33.4 0.1 pad_maximum_fusion.pair_weight
  33.6 5.8 %collective-permute-done.7.refs_1_ = bf16[1296,128]{1,0:T(8,128)(2,1)S(1)} collective-permute-done((bf16[1296,128]{1,0:T(8,128)(2,1)S(1)}, bf16[1296,128]{1,0:T(8,128)(2,1)S(1)}, u32[]{:S(2)}, u32[]{:S(2)}) %collective-permute-start.7) | collective-permute-done | bytes 331808 | tf_op jit(solution)/shard_map/ppermute | solution.py:571
  39.4 6.2 %collective-permute-done.8.refs_2_ = bf16[1296,128]{1,0:T(8,128)(2,1)S(1)} collective-permute-done((bf16[1296,128]{1,0:T(8,128)(2,1)S(1)}, bf16[1296,128]{1,0:T(8,128)(2,1)S(1)}, u32[]{:S(2)}, u32[]{:S(2)}) %collective-permute-start.8) | collective-permute-done | bytes 331808 | tf_op jit(solution)/shard_map/ppermute | solution.py:571
  45.6 0.4 collective-permute-done.9.refs_3_
  46.0 1.8 %shard_map.75 = (bf16[4,640,128]{2,1,0:T(8,128)(2,1)}, bf16[4,480,128]{2,1,0:T(8,128)(2,1)}, s32[1]{0:T(128)}) custom-call(bf16[1296,128]{1,0:T(8,128)(2,1)S(1)} %get-tuple-element.70.refs_0_, bf16[1296,128]{1,0:T(8,128)(2,1)S(1)} %collective-permute-done.7.refs_1_, bf16[1296,128]{1,0:T(8,128)(2,1)S(1)} %collective-permute-done.8.refs_2_, ...), custom_call_target="tpu_custom_call" | custom-call | tf_op jit(solution)/shard_map/pallas_call | solution.py:223
  47.8 0.0 copy-done.3
  47.8 0.0 copy-done.5
  47.8 0.0 copy-done.7
  47.8 0.0 copy-done.8
  47.8 0.6 while.11
  48.4 1.9 %collective-permute-start.10 = (bf16[4,480,128]{2,1,0:T(8,128)(2,1)}, bf16[4,480,128]{2,1,0:T(8,128)(2,1)S(1)}, u32[]{:S(2)}, u32[]{:S(2)}) collective-permute-start(bf16[4,480,128]{2,1,0:T(8,128)(2,1)} %get-tuple-element.160), channel_id=1, source_target_pairs={{0,1},{1,2},{2,3},{3,4},{4,5},{5,6},{6,7},{7,8},{8,9},{9,10},{10,1... | collective-permute-start | bytes 1474568 | tf_op jit(solution)/shard_map/ppermute | solution.py:583
  50.4 8.0 %collective-permute-start.11 = (bf16[4,480,128]{2,1,0:T(8,128)(2,1)}, bf16[4,480,128]{2,1,0:T(8,128)(2,1)S(1)}, u32[]{:S(2)}, u32[]{:S(2)}) collective-permute-start(bf16[4,480,128]{2,1,0:T(8,128)(2,1)} %get-tuple-element.160), channel_id=1, source_target_pairs={{1,0},{2,1},{3,2},{4,3},{5,4},{6,5},{7,6},{8,7},{9,8},{10,9},{11,1... | collective-permute-start | bytes 1474568 | tf_op jit(solution)/shard_map/ppermute | solution.py:584
  58.4 7.6 %shard_map.76.near = f32[4,512,128]{2,1,0:T(8,128)S(1)} custom-call(s32[104]{0:T(128)S(1)} %reshape.22.lookup, bf16[4,640,128]{2,1,0:T(8,128)(2,1)} %get-tuple-element.159, bf16[512,512]{1,0:T(8,128)(2,1)S(1)} %bitcast.15, bf16[2304,256]{1,0:T(8,128)(2,1)S(1)} %pad_maximum_fusion.pair_weight, bf16[3,2304,128]{2,1,0:T(8,128)(2,1)S(1)} %bitcast.13), custom_call_target="tpu_custom_call" | custom-call | flops 10000000000 | bytes 40000000 | tf_op jit(solution)/shard_map/pallas_call | solution.py:525
  66.0 0.0 collective-permute-done.10.before
  66.0 0.0 collective-permute-done.11.after
  66.0 4.9 %shard_map.77 = bf16[4,512,128]{2,1,0:T(8,128)(2,1)} custom-call(s32[104]{0:T(128)S(1)} %reshape.21.lookup, bf16[4,480,128]{2,1,0:T(8,128)(2,1)S(1)} %collective-permute-done.10.before, bf16[4,480,128]{2,1,0:T(8,128)(2,1)S(1)} %collective-permute-done.11.after, f32[4,512,128]{2,1,0:T(8,128)S(1)} %shard_map.76.near, bf16[512,512]{1,0:T(8,128)(2,1)S(1)} %bitcast.16, ...), custom_call_target="tpu_custom_call" | custom-call | tf_op jit(solution)/shard_map/pallas_call | solution.py:543
  (2 shorter events, 0.0 us)
Async XLA Ops:
  0.0 16.6 %copy-start.1 = (bf16[27,256,128]{2,1,0:T(8,128)(2,1)S(1)}, bf16[27,256,128]{2,1,0:T(8,128)(2,1)}, u32[]{:S(2)}) copy-start(bf16[27,256,128]{2,1,0:T(8,128)(2,1)} %param.15) | copy-start | bytes 5308420
  3.7 0.7 copy-start.2
  4.4 9.3 %collective-permute-start = (bf16[656,128]{1,0:T(8,128)(2,1)}, bf16[656,128]{1,0:T(8,128)(2,1)S(1)}, u32[]{:S(2)}, u32[]{:S(2)}) collective-permute-start(bf16[656,128]{1,0:T(8,128)(2,1)} %get-tuple-element.63), channel_id=1, source_target_pairs={{0,1},{1,0},{2,3},{3,2},{4,5},{5,4},{6,7},{7,6},{8,9},{9,8},{10,11... | collective-permute-start | bytes 503816 | tf_op jit(solution)/shard_map/ppermute | solution.py:566
  4.4 9.4 %collective-permute-start.1 = (bf16[656,128]{1,0:T(8,128)(2,1)}, bf16[656,128]{1,0:T(8,128)(2,1)S(1)}, u32[]{:S(2)}, u32[]{:S(2)}) collective-permute-start(bf16[656,128]{1,0:T(8,128)(2,1)} %get-tuple-element.64), channel_id=1, source_target_pairs={{0,2},{1,3},{2,4},{3,5},{4,6},{5,7},{6,0},{7,1},{8,10},{9,11},{10,... | collective-permute-start | bytes 503816 | tf_op jit(solution)/shard_map/ppermute | solution.py:566
  6.0 14.1 %collective-permute-start.2 = (bf16[656,128]{1,0:T(8,128)(2,1)}, bf16[656,128]{1,0:T(8,128)(2,1)S(1)}, u32[]{:S(2)}, u32[]{:S(2)}) collective-permute-start(bf16[656,128]{1,0:T(8,128)(2,1)} %get-tuple-element.65), channel_id=1, source_target_pairs={{0,6},{1,7},{2,0},{3,1},{4,2},{5,3},{6,4},{7,5},{8,14},{9,15},{10,... | collective-permute-start | bytes 503816 | tf_op jit(solution)/shard_map/ppermute | solution.py:566
  8.2 12.0 %collective-permute-start.3 = (bf16[656,128]{1,0:T(8,128)(2,1)}, bf16[656,128]{1,0:T(8,128)(2,1)S(1)}, u32[]{:S(2)}, u32[]{:S(2)}) collective-permute-start(bf16[656,128]{1,0:T(8,128)(2,1)} %get-tuple-element.66), channel_id=1, source_target_pairs={{0,4},{1,5},{2,6},{3,7},{4,0},{5,1},{6,2},{7,3},{8,12},{9,13},{10,... | collective-permute-start | bytes 503816 | tf_op jit(solution)/shard_map/ppermute | solution.py:566
  10.0 11.4 %collective-permute-start.4 = (bf16[656,128]{1,0:T(8,128)(2,1)}, bf16[656,128]{1,0:T(8,128)(2,1)S(1)}, u32[]{:S(2)}, u32[]{:S(2)}) collective-permute-start(bf16[656,128]{1,0:T(8,128)(2,1)} %get-tuple-element.67), channel_id=1, source_target_pairs={{0,5},{1,4},{2,7},{3,6},{4,1},{5,0},{6,3},{7,2},{8,13},{9,12},{10,... | collective-permute-start | bytes 503816 | tf_op jit(solution)/shard_map/ppermute | solution.py:566
  13.7 11.6 %collective-permute-start.5 = (bf16[656,128]{1,0:T(8,128)(2,1)}, bf16[656,128]{1,0:T(8,128)(2,1)S(1)}, u32[]{:S(2)}, u32[]{:S(2)}) collective-permute-start(bf16[656,128]{1,0:T(8,128)(2,1)} %copy-done.2), channel_id=1, source_target_pairs={{0,3},{1,2},{2,5},{3,4},{4,7},{5,6},{6,1},{7,0},{8,11},{9,10},{10,... | collective-permute-start | bytes 503816 | tf_op jit(solution)/shard_map/ppermute | solution.py:566
  13.7 11.5 %collective-permute-start.6 = (bf16[656,128]{1,0:T(8,128)(2,1)S(1)}, bf16[656,128]{1,0:T(8,128)(2,1)S(1)}, u32[]{:S(2)}, u32[]{:S(2)}) collective-permute-start(bf16[656,128]{1,0:T(8,128)(2,1)S(1)} %get-tuple-element.69), channel_id=1, source_target_pairs={{0,7},{1,6},{2,1},{3,0},{4,3},{5,2},{6,5},{7,4},{8,15},{9,14},{10,... | collective-permute-start | bytes 503816 | tf_op jit(solution)/shard_map/ppermute | solution.py:566
  27.1 12.3 %collective-permute-start.7 = (bf16[1296,128]{1,0:T(8,128)(2,1)S(1)}, bf16[1296,128]{1,0:T(8,128)(2,1)S(1)}, u32[]{:S(2)}, u32[]{:S(2)}) collective-permute-start(bf16[1296,128]{1,0:T(8,128)(2,1)S(1)} %get-tuple-element.71), channel_id=1, source_target_pairs={{0,16},{1,17},{2,18},{3,19},{4,20},{5,21},{6,22},{7,23},{8,24},{9,... | collective-permute-start | bytes 995336 | tf_op jit(solution)/shard_map/ppermute | solution.py:571
  30.2 15.4 %collective-permute-start.8 = (bf16[1296,128]{1,0:T(8,128)(2,1)S(1)}, bf16[1296,128]{1,0:T(8,128)(2,1)S(1)}, u32[]{:S(2)}, u32[]{:S(2)}) collective-permute-start(bf16[1296,128]{1,0:T(8,128)(2,1)S(1)} %get-tuple-element.72), channel_id=1, source_target_pairs={{0,8},{1,9},{2,10},{3,11},{4,12},{5,13},{6,14},{7,15},{8,16},{9,17... | collective-permute-start | bytes 995336 | tf_op jit(solution)/shard_map/ppermute | solution.py:571
  31.0 15.0 %collective-permute-start.9 = (bf16[1296,128]{1,0:T(8,128)(2,1)S(1)}, bf16[1296,128]{1,0:T(8,128)(2,1)S(1)}, u32[]{:S(2)}, u32[]{:S(2)}) collective-permute-start(bf16[1296,128]{1,0:T(8,128)(2,1)S(1)} %get-tuple-element.73), channel_id=1, source_target_pairs={{0,24},{1,25},{2,26},{3,27},{4,28},{5,29},{6,30},{7,31},{8,0},{9,1... | collective-permute-start | bytes 995336 | tf_op jit(solution)/shard_map/ppermute | solution.py:571
  33.4 14.4 %copy-start.3 = (bf16[8,512,128]{2,1,0:T(8,128)(2,1)S(1)}, bf16[8,512,128]{2,1,0:T(8,128)(2,1)}, u32[]{:S(2)}) copy-start(bf16[8,512,128]{2,1,0:T(8,128)(2,1)} %skip.1) | copy-start | bytes 3145732
  33.4 14.4 %copy-start.5 = (bf16[8,64,256]{2,1,0:T(8,128)(2,1)S(1)}, bf16[8,64,256]{2,1,0:T(8,128)(2,1)}, u32[]{:S(2)}) copy-start(bf16[8,64,256]{2,1,0:T(8,128)(2,1)} %parents.1) | copy-start | bytes 786436
  33.4 14.4 %copy-start.7 = (s32[8]{0:T(128)S(1)}, s32[8]{0:T(128)}, u32[]{:S(2)}) copy-start(s32[8]{0:T(128)} %parent_dest.1) | copy-start | bytes 100
  33.4 14.4 %copy-start.8 = (s32[8]{0:T(128)S(1)}, s32[8]{0:T(128)}, u32[]{:S(2)}) copy-start(s32[8]{0:T(128)} %skip_dest.1) | copy-start | bytes 100
  48.4 17.5 %collective-permute-start.10 = (bf16[4,480,128]{2,1,0:T(8,128)(2,1)}, bf16[4,480,128]{2,1,0:T(8,128)(2,1)S(1)}, u32[]{:S(2)}, u32[]{:S(2)}) collective-permute-start(bf16[4,480,128]{2,1,0:T(8,128)(2,1)} %get-tuple-element.160), channel_id=1, source_target_pairs={{0,1},{1,2},{2,3},{3,4},{4,5},{5,6},{6,7},{7,8},{8,9},{9,10},{10,1... | collective-permute-start | bytes 1474568 | tf_op jit(solution)/shard_map/ppermute | solution.py:583
  50.4 15.6 %collective-permute-start.11 = (bf16[4,480,128]{2,1,0:T(8,128)(2,1)}, bf16[4,480,128]{2,1,0:T(8,128)(2,1)S(1)}, u32[]{:S(2)}, u32[]{:S(2)}) collective-permute-start(bf16[4,480,128]{2,1,0:T(8,128)(2,1)} %get-tuple-element.160), channel_id=1, source_target_pairs={{1,0},{2,1},{3,2},{4,3},{5,4},{6,5},{7,6},{8,7},{9,8},{10,9},{11,1... | collective-permute-start | bytes 1474568 | tf_op jit(solution)/shard_map/ppermute | solution.py:584

commit v4 on v3

--- a/solution.py
+++ b/solution.py
@@ -191,26 +191,19 @@
 
 def unpack_kernel(*refs):
     came = refs[:LINES]
-    own, surface, flag_out, plain, found, table, sem = refs[LINES:]
-    lane = lax.broadcasted_iota(I32, (HEAD_ROWS, 128), 1)
-    row = lax.broadcasted_iota(I32, (HEAD_ROWS, 128), 0)
+    own, surface, flag_out, plain = refs[LINES:]
+    table = []
     for k in range(LINES):
-        header = came[k][BODY * DEPTH : BODY * DEPTH + HEAD_ROWS].astype(F32)
-        found[k : k + 1] = jnp.sum(
-            jnp.where(lane == row, header, 0.0), axis=0, keepdims=True
-        ).astype(I32)
-    found[LINES:8] = jnp.zeros((8 - LINES, 128), I32)
-    copy = pltpu.make_async_copy(found, table, sem)
-    copy.start()
-    copy.wait()
-    flag = table[0, 2 * DEPTH]
+        header = came[k][BODY * DEPTH : BODY * DEPTH + HEAD_ROWS].astype(F32).astype(I32)
+        table.append([header[j, 0] for j in range(2 * DEPTH + 1)])
+    flag = table[0][2 * DEPTH]
     for k in range(1, LINES):
-        flag = flag | table[k, 2 * DEPTH]
+        flag = flag | table[k][2 * DEPTH]
     flag_out[0] = flag
     for k in range(LINES):
         for kind, (rows, first, height) in enumerate(PIECES):
             for r in range(DEPTH):
-                brick = table[k, kind * DEPTH + r]
+                brick = table[k][kind * DEPTH + r]
 
                 @pl.when(brick >= 0)
                 def _(k=k, rows=rows, first=first, at=height + r * rows, brick=brick):
@@ -231,9 +224,6 @@
         out_specs=[VMEM, VMEM, SMEM],
         scratch_shapes=[
             pltpu.VMEM((SKIP_ROWS, 128), F32),
-            pltpu.VMEM((8, 128), I32),
-            pltpu.SMEM((8, 128), I32),
-            pltpu.SemaphoreType.DMA,
         ],
         compiler_params=pltpu.CompilerParams(vmem_limit_bytes=16 * 2**20),
     )(*messages)
@@ -410,13 +400,14 @@
 
 
 def near_kernel(
-    lookup, own, up_weight, pair_weight, conv_weight, out, pool, shifted_pair, window_pair
+    lookup, own, up_weight, pair_weight, side_weight, conv_weight, out,
+    pool, shifted_pair, window_pair, deeper_pair
 ):
     fill_pool(pool, (own,), up_weight, SKIP_ROWS)
     spans = {-1: (7, 8, 0), 0: (0, 8, 1), 1: (0, 1, 9)}
 
     for b in range(BRICKS):
-        shifted, window = shifted_pair[b % 2], window_pair[b % 2]
+        shifted, window, deeper = shifted_pair[b % 2], window_pair[b % 2], deeper_pair[b % 2]
         for off_x in (-1, 0, 1):
             for off_y in (-1, 0, 1):
                 low_x, high_x, to_x = spans[off_x]
@@ -440,9 +431,18 @@
                 window[:, first : first + 256] = (
                     shifted[step_z, :, step_y : step_y + 8].reshape(640, 256).astype(BF16)
                 )
+        for step_z in range(3):
+            deeper[:, step_z * 256 : step_z * 256 + 256] = (
+                shifted[step_z, 2:10, 0:9].reshape(576, 256).astype(BF16)
+            )
         pair = jnp.dot(window[0:576], pair_weight[...], preferred_element_type=F32)
-        last = jnp.dot(window[128:640], conv_weight[2], preferred_element_type=F32)
-        out[b] = pair[0:512, 0:128] + pair[64:576, 128:256] + last
+        side = jnp.dot(deeper[...], side_weight[...], preferred_element_type=F32)
+        side = side.reshape(8, 9, 8, 256)
+        side = (side[:, 0:8, :, 0:128] + side[:, 1:9, :, 128:256]).reshape(512, 128)
+        last = jnp.dot(
+            window[128:640, 1536:2304], conv_weight[2, 1536:2304], preferred_element_type=F32
+        )
+        out[b] = pair[0:512, 0:128] + pair[64:576, 128:256] + side + last
 
 
 def far_kernel(
@@ -452,52 +452,44 @@
     total[...] = near[...].reshape(BRICKS * 512, 128)
     shifted[...] = jnp.zeros(shifted.shape, F32)
 
-    for b in range(BRICKS):
-
-        def brick(*offsets, b=b):
-            return lookup[b * 26 + code_of(*offsets)]
-
-        def keep(side, b=b):
-            for step in range(3):
-                for inner in range(3):
-                    first = (step * 3 + inner) * 256
-                    window[side, b * 64 : b * 64 + 64, first : first + 256] = (
-                        shifted[side, inner, step : step + 8].reshape(64, 256).astype(BF16)
-                    )
-
-        for side, off in enumerate((-1, 1)):
-            edge = 7 if off < 0 else 0
+    def brick(b, *offsets):
+        return lookup[b * 26 + code_of(*offsets)]
+
+    def keep(face, b):
+        for step in range(3):
+            for inner in range(3):
+                first = (step * 3 + inner) * 256
+                window[face, b * 64 : b * 64 + 64, first : first + 256] = (
+                    shifted[face, inner, step : step + 8].reshape(64, 256).astype(BF16)
+                )
+
+    for side, off in enumerate((-1, 1)):
+        edge, tap = (7 if off < 0 else 0), 2 * side
+        for b in range(BRICKS):
             for off_y in (-1, 0, 1):
-                bricks = [brick(off, off_y, off_z) for off_z in (-1, 0, 1)]
                 low, deep, to = ((7, 1, 0), (0, 8, 1), (0, 1, 9))[off_y + 1]
                 first = edge * 64 + low * 8
                 line = [
-                    rows_from(pool, n, pl.ds(first, deep * 8)).reshape(deep, 8, 256)
-                    for n in bricks
+                    rows_from(pool, brick(b, off, off_y, off_z), pl.ds(first, deep * 8)).reshape(
+                        deep, 8, 256
+                    )
+                    for off_z in (-1, 0, 1)
                 ]
                 for step, rows in enumerate(shift_rows(line)):
                     shifted[side, step, to : to + deep] = rows
-            keep(side)
-            bricks = [brick(0, off, off_z) for off_z in (-1, 0, 1)]
+            keep(side, b)
+        added = jnp.dot(window[side], conv_weight[tap], preferred_element_type=F32)
+        for b in range(BRICKS):
+            first = b * 512 + 448 * side
+            total[first : first + 64] += added[b * 64 : b * 64 + 64]
+        for b in range(BRICKS):
+            bricks = [brick(b, 0, off, off_z) for off_z in (-1, 0, 1)]
             for x in range(8):
                 first = x * 64 + edge * 8
                 line = [rows_from(pool, n, pl.ds(first, 8)).reshape(1, 8, 256) for n in bricks]
                 for step, rows in enumerate(shift_rows(line)):
                     shifted[2 + side, step, 1 + x : 2 + x] = rows
-            keep(2 + side)
-            face = rows_from(pool, brick(0, 0, off), pl.ds(edge, 64, stride=8)).reshape(8, 8, 256)
-            y = lax.broadcasted_iota(I32, face.shape, 1)
-            shifted[4 + side, 0, 1:9] = jnp.where(y == 0, 0.0, pltpu.roll(face, 1, 1))
-            shifted[4 + side, 1, 1:9] = face
-            shifted[4 + side, 2, 1:9] = jnp.where(y == 7, 0.0, pltpu.roll(face, 7, 1))
-            keep(4 + side)
-
-    for side in range(2):
-        tap = 2 * side
-        added = jnp.dot(window[side], conv_weight[tap], preferred_element_type=F32)
-        for b in range(BRICKS):
-            first = b * 512 + 448 * side
-            total[first : first + 64] += added[b * 64 : b * 64 + 64]
+            keep(2 + side, b)
         added = jnp.zeros((256, 128), F32)
         for x in range(3):
             added += jnp.dot(
@@ -508,6 +500,13 @@
         for r in range(BRICKS * 8):
             first = r * 64 + 56 * side
             total[first : first + 8] += added[r * 8 : r * 8 + 8]
+        for b in range(BRICKS):
+            face = rows_from(pool, brick(b, 0, 0, off), pl.ds(edge, 64, stride=8)).reshape(8, 8, 256)
+            y = lax.broadcasted_iota(I32, face.shape, 1)
+            shifted[4 + side, 0, 1:9] = jnp.where(y == 0, 0.0, pltpu.roll(face, 1, 1))
+            shifted[4 + side, 1, 1:9] = face
+            shifted[4 + side, 2, 1:9] = jnp.where(y == 7, 0.0, pltpu.roll(face, 7, 1))
+            keep(4 + side, b)
         added = jnp.zeros((256, 128), F32)
         for x in range(3):
             for y in range(3):
@@ -521,22 +520,23 @@
     out[...] = jnp.maximum(total[...], 0.0).astype(BF16).reshape(BRICKS, 512, 128)
 
 
-def convolve_near(lookup, own, up_weight, pair_weight, conv_weight):
+def convolve_near(lookup, own, up_weight, pair_weight, side_weight, conv_weight):
     return pl.pallas_call(
         near_kernel,
         out_shape=jax.ShapeDtypeStruct((BRICKS, 512, 128), F32),
-        in_specs=[SMEM] + [VMEM] * 4,
+        in_specs=[SMEM] + [VMEM] * 5,
         out_specs=VMEM,
         scratch_shapes=[
             pltpu.VMEM((BRICKS + 1, 2, 512, 128), F32),
             [pltpu.VMEM((3, 10, 10, 8, 256), F32)] * 2,
             [pltpu.VMEM((640, 9 * 256), BF16)] * 2,
+            [pltpu.VMEM((576, 3 * 256), BF16)] * 2,
         ],
         compiler_params=pltpu.CompilerParams(vmem_limit_bytes=32 * 2**20),
         cost_estimate=pl.CostEstimate(
             flops=10**10, bytes_accessed=4 * 10**7, transcendentals=0
         ),
-    )(lookup, own, up_weight, pair_weight, conv_weight)
+    )(lookup, own, up_weight, pair_weight, side_weight, conv_weight)
 
 
 def convolve_far(lookup, before, after, near, up_weight, conv_weight):
@@ -591,8 +591,9 @@
     up_weight = up_weight.reshape(4, 512, 128).transpose(1, 0, 2).reshape(512, 512)
     conv_weight = conv_weight.reshape(3, 9 * 256, 128)
     pair_weight = jnp.concatenate([conv_weight[0], conv_weight[1]], axis=1)
+    side_weight = jnp.concatenate([conv_weight[2, 0:768], conv_weight[2, 768:1536]], axis=1)
     near = convolve_near(
-        near_lookup.reshape(-1), own, up_weight, pair_weight, conv_weight
+        near_lookup.reshape(-1), own, up_weight, pair_weight, side_weight, conv_weight
     )
     return convolve_far(far_lookup.reshape(-1), before, after, near, up_weight, conv_weight)
 

time: 71.1 us -> 70 us (0.985)
  waiting for transfers between devices: 20.9 us -> 16.3 us
  local copies, waits for them, and re-layouts: 2.46 us -> 5.86 us
  Pallas kernels: 19.7 us -> 18.2 us
  other arithmetic: 0.9 us -> 2.12 us
    ppermute x7, waiting for transfers between devices: 8.51 us -> 4.05 us  [per_device(): came.append(lax.ppermute(first[j], 'gy', steps))]
    slice x1, local copies, waits for them, and re-layouts: 0.1 us -> 2.37 us  [per_device(): pair_weight = jnp.concatenate([conv_weight[0], conv_weight[1]], axis=1)]
    concatenate x0 -> x1, other arithmetic: none -> 1.9 us  [per_device(): jnp.concatenate([conv_weight[2, 0:768], conv_weight[2, 768:1536]], axis=1)]
    pallas_call x1, Pallas kernels: 7.56 us -> 6.59 us  [convolve_near(): pl.pallas_call(near_kernel, out_shape=jax.ShapeDtypeStruct((BRICKS, 512,...]
    squeeze x0 -> x1, local copies, waits for them, and re-layouts: none -> 0.76 us  [per_device(): conv_weight[2, 0:768]]
  transfers between devices with their start and end apart: 12 -> 12, of which waited for: 6 -> 4; matrix products, arithmetic and copies ran while one was open for 4% -> 10% of each run, Pallas kernels for 11% -> 9%
where the time goes in v4:
time: 70 us; the launch traced here: 69.7 us
  starting transfers between devices  26.4 us (38%)
  Pallas kernels  18.2 us (26%)
  waiting for transfers between devices  16.3 us (23%)
  local copies, waits for them, and re-layouts  5.86 us (8%)
  other arithmetic  2.12 us (3%)
    ppermute x3, waiting for transfers between devices, per_device(): arrived.append(lax.ppermute(messages[k], 'gy', steps))  12.2 us
    ppermute x7, starting transfers between devices, per_device(): came.append(lax.ppermute(first[j], 'gy', steps))  10.4 us
    ppermute x1, starting transfers between devices, per_device(): after = lax.ppermute(surface, ('gx', 'gy'), [(j, i) for i, j in up])  8.04 us
    pallas_call x1, Pallas kernels, convolve_near(): pl.pallas_call(near_kernel, out_shape=jax.ShapeDtypeStruct((BRICKS, 512,...  6.59 us
    ppermute x3, starting transfers between devices, per_device(): arrived.append(lax.ppermute(messages[k], 'gy', steps))  6.11 us
    pallas_call x1, Pallas kernels, convolve_far(): pl.pallas_call(far_kernel, out_shape=jax.ShapeDtypeStruct((BRICKS, 512, 1...  4.82 us
    ppermute x7, waiting for transfers between devices, per_device(): came.append(lax.ppermute(first[j], 'gy', steps))  4.05 us
    pallas_call x1, Pallas kernels, first_pack(): pl.pallas_call(first_kernel, out_shape=[jax.ShapeDtypeStruct((BODY + HEAD...  3.42 us
  transfers between devices with their start and end apart: 12, of which 4 were waited for; matrix products, arithmetic and copies ran while one was open for 10% of the time, Pallas kernels for 9%

profile of v4, /device:TPU:16, one launch (start us, length us, event | category | flops | bytes accessed | tf_op | source)
XLA Modules:
  0.0 69.7 jit_solution(2698564025104784288)
XLA Ops:
  0.0 0.1 pad_add_fusion.place
  0.1 3.4 %shard_map.73 = (bf16[656,128]{1,0:T(8,128)(2,1)S(1)}, bf16[656,128]{1,0:T(8,128)(2,1)S(1)}, bf16[656,128]{1,0:T(8,128)(2,1)S(1)}, bf16[656,128]{1,0:T(8,128)(2,...) custom-call(s32[8]{0:T(128)} %parent_dest.1, ...), custom_call_target="tpu_custom_call" | custom-call | tf_op jit(solution)/shard_map/pallas_call | solution.py:73
  3.5 0.0 copy-start.11
  3.5 0.1 collective-permute-start
  3.6 2.1 %collective-permute-start.1 = (bf16[656,128]{1,0:T(8,128)(2,1)S(1)}, bf16[656,128]{1,0:T(8,128)(2,1)S(1)}, u32[]{:S(2)}, u32[]{:S(2)}) collective-permute-start(bf16[656,128]{1,0:T(8,128)(2,1)S(1)} %get-tuple-element.64), channel_id=1, source_target_pairs={{0,2},{1,3},{2,4},{3,5},{4,6},{5,7},{6,0},{7,1},{8,10},{9,11},{10,... | collective-permute-start | bytes 503816 | tf_op jit(solution)/shard_map/ppermute | solution.py:566
  5.7 2.3 %collective-permute-start.2 = (bf16[656,128]{1,0:T(8,128)(2,1)}, bf16[656,128]{1,0:T(8,128)(2,1)S(1)}, u32[]{:S(2)}, u32[]{:S(2)}) collective-permute-start(bf16[656,128]{1,0:T(8,128)(2,1)} %get-tuple-element.65), channel_id=1, source_target_pairs={{0,6},{1,7},{2,0},{3,1},{4,2},{5,3},{6,4},{7,5},{8,14},{9,15},{10,... | collective-permute-start | bytes 503816 | tf_op jit(solution)/shard_map/ppermute | solution.py:566
  8.0 1.6 %collective-permute-start.3 = (bf16[656,128]{1,0:T(8,128)(2,1)}, bf16[656,128]{1,0:T(8,128)(2,1)S(1)}, u32[]{:S(2)}, u32[]{:S(2)}) collective-permute-start(bf16[656,128]{1,0:T(8,128)(2,1)} %get-tuple-element.66), channel_id=1, source_target_pairs={{0,4},{1,5},{2,6},{3,7},{4,0},{5,1},{6,2},{7,3},{8,12},{9,13},{10,... | collective-permute-start | bytes 503816 | tf_op jit(solution)/shard_map/ppermute | solution.py:566
  9.6 1.4 %collective-permute-start.4 = (bf16[656,128]{1,0:T(8,128)(2,1)}, bf16[656,128]{1,0:T(8,128)(2,1)S(1)}, u32[]{:S(2)}, u32[]{:S(2)}) collective-permute-start(bf16[656,128]{1,0:T(8,128)(2,1)} %get-tuple-element.67), channel_id=1, source_target_pairs={{0,5},{1,4},{2,7},{3,6},{4,1},{5,0},{6,3},{7,2},{8,13},{9,12},{10,... | collective-permute-start | bytes 503816 | tf_op jit(solution)/shard_map/ppermute | solution.py:566
  11.0 2.4 %fusion.2 = (bf16[9,256,128]{2,1,0:T(8,128)(2,1)}, bf16[9,256,128]{2,1,0:T(8,128)(2,1)}) fusion(bf16[27,256,128]{2,1,0:T(8,128)(2,1)} %param.15), kind=kLoop, calls=%fused_computation.12 | loop fusion | bytes 2359296 | tf_op jit(solution)/shard_map/slice | solution.py:593
  13.3 0.0 copy-done.1
  13.3 0.8 %slice_bitcast_fusion.1 = (bf16[768,128]{1,0:T(8,128)(2,1)}, bf16[768,128]{1,0:T(8,128)(2,1)}) fusion(bf16[3,2304,128]{2,1,0:T(8,128)(2,1)S(1)} %bitcast.17), kind=kLoop, calls=%fused_computation.4 | loop fusion | bytes 786432 | tf_op jit(solution)/shard_map/squeeze | solution.py:594
  14.1 0.0 collective-permute-done.refs_1_
  14.1 0.1 collective-permute-start.5
  14.2 0.0 collective-permute-done.1.refs_2_
  14.2 2.9 %collective-permute-start.6 = (bf16[656,128]{1,0:T(8,128)(2,1)}, bf16[656,128]{1,0:T(8,128)(2,1)}, u32[]{:S(2)}, u32[]{:S(2)}) collective-permute-start(bf16[656,128]{1,0:T(8,128)(2,1)} %get-tuple-element.69), channel_id=1, source_target_pairs={{0,7},{1,6},{2,1},{3,0},{4,3},{5,2},{6,5},{7,4},{8,15},{9,14},{10,... | collective-permute-start | bytes 503816 | tf_op jit(solution)/shard_map/ppermute | solution.py:566
  17.1 0.0 copy-done.11
  17.1 0.1 reshape.22.lookup
  17.2 1.4 %copy.8 = bf16[4,512,128]{2,0,1:T(4,128)(2,1)S(1)} copy(bf16[4,512,128]{2,1,0:T(8,128)(2,1)} %bitcast.25) | data formatting | bytes 1048576 | tf_op jit(solution)/shard_map/reshape | solution.py:591
  18.6 0.1 copy.11
  18.7 0.1 reshape.21.lookup
  18.8 1.9 %pad_maximum_fusion.1.side_weight = bf16[768,256]{1,0:T(8,128)(2,1)} fusion(bf16[768,128]{1,0:T(8,128)(2,1)} %get-tuple-element.96, bf16[768,128]{1,0:T(8,128)(2,1)} %get-tuple-element.95), kind=kLoop, calls=%fused_computation.2 | loop fusion | flops 786432 | bytes 786432 | tf_op jit(solution)/shard_map/concatenate | solution.py:594
  20.7 0.0 collective-permute-done.2.refs_3_
  20.7 0.0 collective-permute-done.3.refs_4_
  20.7 0.2 collective-permute-done.4.refs_5_
  20.8 3.9 %collective-permute-done.5.refs_6_ = bf16[656,128]{1,0:T(8,128)(2,1)S(1)} collective-permute-done((bf16[656,128]{1,0:T(8,128)(2,1)}, bf16[656,128]{1,0:T(8,128)(2,1)S(1)}, u32[]{:S(2)}, u32[]{:S(2)}) %collective-permute-start.5) | collective-permute-done | bytes 167968 | tf_op jit(solution)/shard_map/ppermute | solution.py:566
  24.7 0.0 collective-permute-done.6.refs_7_
  24.7 2.2 %shard_map.74 = (bf16[1296,128]{1,0:T(8,128)(2,1)S(1)}, bf16[1296,128]{1,0:T(8,128)(2,1)S(1)}, bf16[1296,128]{1,0:T(8,128)(2,1)S(1)}, bf16[1296,128]{1,0:T(8,128)(2,1)S(1)}) custom-call(s32[3]{0:T(128)S(1)} %pad_add_fusion.place, bf16[656,128]{1,0:T(8,128)(2,1)S(1)} %get-tuple-element.62.refs_0_, bf16[656,128]{1,0:T(8,128)(2,1)S(1)} %collective-permute-done.refs_1_, ...), custom_call_target="tpu_custom_call" | custom-call | tf_op jit(solution)/shard_map/pallas_call | solution.py:157
  27.0 2.9 %collective-permute-start.7 = (bf16[1296,128]{1,0:T(8,128)(2,1)S(1)}, bf16[1296,128]{1,0:T(8,128)(2,1)S(1)}, u32[]{:S(2)}, u32[]{:S(2)}) collective-permute-start(bf16[1296,128]{1,0:T(8,128)(2,1)S(1)} %get-tuple-element.71), channel_id=1, source_target_pairs={{0,16},{1,17},{2,18},{3,19},{4,20},{5,21},{6,22},{7,23},{8,24},{9,... | collective-permute-start | bytes 995336 | tf_op jit(solution)/shard_map/ppermute | solution.py:571
  29.8 0.6 collective-permute-start.8
  30.5 2.6 %collective-permute-start.9 = (bf16[1296,128]{1,0:T(8,128)(2,1)S(1)}, bf16[1296,128]{1,0:T(8,128)(2,1)S(1)}, u32[]{:S(2)}, u32[]{:S(2)}) collective-permute-start(bf16[1296,128]{1,0:T(8,128)(2,1)S(1)} %get-tuple-element.73), channel_id=1, source_target_pairs={{0,24},{1,25},{2,26},{3,27},{4,28},{5,29},{6,30},{7,31},{8,0},{9,1... | collective-permute-start | bytes 995336 | tf_op jit(solution)/shard_map/ppermute | solution.py:571
  33.1 0.0 copy-done.7
  33.1 0.0 copy-done.8
  33.1 0.0 copy-start.9
  33.1 0.0 copy-start.10
  33.1 0.1 pad_maximum_fusion.pair_weight
  33.2 6.0 %collective-permute-done.7.refs_1_ = bf16[1296,128]{1,0:T(8,128)(2,1)S(1)} collective-permute-done((bf16[1296,128]{1,0:T(8,128)(2,1)S(1)}, bf16[1296,128]{1,0:T(8,128)(2,1)S(1)}, u32[]{:S(2)}, u32[]{:S(2)}) %collective-permute-start.7) | collective-permute-done | bytes 331808 | tf_op jit(solution)/shard_map/ppermute | solution.py:571
  39.2 6.2 %collective-permute-done.8.refs_2_ = bf16[1296,128]{1,0:T(8,128)(2,1)S(1)} collective-permute-done((bf16[1296,128]{1,0:T(8,128)(2,1)S(1)}, bf16[1296,128]{1,0:T(8,128)(2,1)S(1)}, u32[]{:S(2)}, u32[]{:S(2)}) %collective-permute-start.8) | collective-permute-done | bytes 331808 | tf_op jit(solution)/shard_map/ppermute | solution.py:571
  45.5 0.0 collective-permute-done.9.refs_3_
  45.5 1.2 %shard_map.75 = (bf16[4,640,128]{2,1,0:T(8,128)(2,1)}, bf16[4,480,128]{2,1,0:T(8,128)(2,1)}, s32[1]{0:T(128)}) custom-call(bf16[1296,128]{1,0:T(8,128)(2,1)S(1)} %get-tuple-element.70.refs_0_, bf16[1296,128]{1,0:T(8,128)(2,1)S(1)} %collective-permute-done.7.refs_1_, bf16[1296,128]{1,0:T(8,128)(2,1)S(1)} %collective-permute-done.8.refs_2_, ...), custom_call_target="tpu_custom_call" | custom-call | tf_op jit(solution)/shard_map/pallas_call | solution.py:216
  46.6 0.0 copy-done.3
  46.7 0.6 while.11
  47.3 1.9 %collective-permute-start.10 = (bf16[4,480,128]{2,1,0:T(8,128)(2,1)}, bf16[4,480,128]{2,1,0:T(8,128)(2,1)S(1)}, u32[]{:S(2)}, u32[]{:S(2)}) collective-permute-start(bf16[4,480,128]{2,1,0:T(8,128)(2,1)} %get-tuple-element.161), channel_id=1, source_target_pairs={{0,1},{1,2},{2,3},{3,4},{4,5},{5,6},{6,7},{7,8},{8,9},{9,10},{10,1... | collective-permute-start | bytes 1474568 | tf_op jit(solution)/shard_map/ppermute | solution.py:583
  49.2 8.0 %collective-permute-start.11 = (bf16[4,480,128]{2,1,0:T(8,128)(2,1)}, bf16[4,480,128]{2,1,0:T(8,128)(2,1)S(1)}, u32[]{:S(2)}, u32[]{:S(2)}) collective-permute-start(bf16[4,480,128]{2,1,0:T(8,128)(2,1)} %get-tuple-element.161), channel_id=1, source_target_pairs={{1,0},{2,1},{3,2},{4,3},{5,4},{6,5},{7,6},{8,7},{9,8},{10,9},{11,1... | collective-permute-start | bytes 1474568 | tf_op jit(solution)/shard_map/ppermute | solution.py:584
  57.2 1.0 %copy-done.2 = bf16[768,256]{1,0:T(8,128)(2,1)S(1)} copy-done((bf16[768,256]{1,0:T(8,128)(2,1)S(1)}, bf16[768,256]{1,0:T(8,128)(2,1)}, u32[]{:S(2)}) %copy-start.2) | copy-done | bytes 393240
  58.2 6.6 %shard_map.76.near = f32[4,512,128]{2,1,0:T(8,128)S(1)} custom-call(s32[104]{0:T(128)S(1)} %reshape.22.lookup, bf16[4,640,128]{2,1,0:T(8,128)(2,1)} %get-tuple-element.160, bf16[512,512]{1,0:T(8,128)(2,1)S(1)} %bitcast.20, bf16[2304,256]{1,0:T(8,128)(2,1)S(1)} %pad_maximum_fusion.pair_weight, bf16[768,256]{1,0:T(8,128)(2,1)S(1)} %copy-done.2, ...), custom_call_target="tpu_custom_call" | custom-call | flops 10000000000 | bytes 40000000 | tf_op jit(solution)/shard_map/pallas_call | solution.py:524
  64.8 0.0 collective-permute-done.10.before
  64.8 0.0 collective-permute-done.11.after
  64.8 4.8 %shard_map.77 = bf16[4,512,128]{2,1,0:T(8,128)(2,1)} custom-call(s32[104]{0:T(128)S(1)} %reshape.21.lookup, bf16[4,480,128]{2,1,0:T(8,128)(2,1)S(1)} %collective-permute-done.10.before, bf16[4,480,128]{2,1,0:T(8,128)(2,1)S(1)} %collective-permute-done.11.after, f32[4,512,128]{2,1,0:T(8,128)S(1)} %shard_map.76.near, bf16[512,512]{1,0:T(8,128)(2,1)S(1)} %bitcast.21, ...), custom_call_target="tpu_custom_call" | custom-call | tf_op jit(solution)/shard_map/pallas_call | solution.py:543
  (10 shorter events, 0.0 us)
Async XLA Ops:
  0.1 13.3 %copy-start.1 = (bf16[27,256,128]{2,1,0:T(8,128)(2,1)S(1)}, bf16[27,256,128]{2,1,0:T(8,128)(2,1)}, u32[]{:S(2)}) copy-start(bf16[27,256,128]{2,1,0:T(8,128)(2,1)} %param.15) | copy-start | bytes 5308420
  3.5 13.6 %copy-start.11 = (s32[4,26]{1,0:T(4,128)S(1)}, s32[4,26]{1,0:T(4,128)}, u32[]{:S(2)}) copy-start(s32[4,26]{1,0:T(4,128)} %param.13) | copy-start | bytes 1252
  3.5 10.6 %collective-permute-start = (bf16[656,128]{1,0:T(8,128)(2,1)S(1)}, bf16[656,128]{1,0:T(8,128)(2,1)S(1)}, u32[]{:S(2)}, u32[]{:S(2)}) collective-permute-start(bf16[656,128]{1,0:T(8,128)(2,1)S(1)} %get-tuple-element.63), channel_id=1, source_target_pairs={{0,1},{1,0},{2,3},{3,2},{4,5},{5,4},{6,7},{7,6},{8,9},{9,8},{10,11... | collective-permute-start | bytes 503816 | tf_op jit(solution)/shard_map/ppermute | solution.py:566
  3.6 10.5 %collective-permute-start.1 = (bf16[656,128]{1,0:T(8,128)(2,1)S(1)}, bf16[656,128]{1,0:T(8,128)(2,1)S(1)}, u32[]{:S(2)}, u32[]{:S(2)}) collective-permute-start(bf16[656,128]{1,0:T(8,128)(2,1)S(1)} %get-tuple-element.64), channel_id=1, source_target_pairs={{0,2},{1,3},{2,4},{3,5},{4,6},{5,7},{6,0},{7,1},{8,10},{9,11},{10,... | collective-permute-start | bytes 503816 | tf_op jit(solution)/shard_map/ppermute | solution.py:566
  5.7 15.0 %collective-permute-start.2 = (bf16[656,128]{1,0:T(8,128)(2,1)}, bf16[656,128]{1,0:T(8,128)(2,1)S(1)}, u32[]{:S(2)}, u32[]{:S(2)}) collective-permute-start(bf16[656,128]{1,0:T(8,128)(2,1)} %get-tuple-element.65), channel_id=1, source_target_pairs={{0,6},{1,7},{2,0},{3,1},{4,2},{5,3},{6,4},{7,5},{8,14},{9,15},{10,... | collective-permute-start | bytes 503816 | tf_op jit(solution)/shard_map/ppermute | solution.py:566
  8.0 12.7 %collective-permute-start.3 = (bf16[656,128]{1,0:T(8,128)(2,1)}, bf16[656,128]{1,0:T(8,128)(2,1)S(1)}, u32[]{:S(2)}, u32[]{:S(2)}) collective-permute-start(bf16[656,128]{1,0:T(8,128)(2,1)} %get-tuple-element.66), channel_id=1, source_target_pairs={{0,4},{1,5},{2,6},{3,7},{4,0},{5,1},{6,2},{7,3},{8,12},{9,13},{10,... | collective-permute-start | bytes 503816 | tf_op jit(solution)/shard_map/ppermute | solution.py:566
  9.6 11.3 %collective-permute-start.4 = (bf16[656,128]{1,0:T(8,128)(2,1)}, bf16[656,128]{1,0:T(8,128)(2,1)S(1)}, u32[]{:S(2)}, u32[]{:S(2)}) collective-permute-start(bf16[656,128]{1,0:T(8,128)(2,1)} %get-tuple-element.67), channel_id=1, source_target_pairs={{0,5},{1,4},{2,7},{3,6},{4,1},{5,0},{6,3},{7,2},{8,13},{9,12},{10,... | collective-permute-start | bytes 503816 | tf_op jit(solution)/shard_map/ppermute | solution.py:566
  14.1 10.6 %collective-permute-start.5 = (bf16[656,128]{1,0:T(8,128)(2,1)}, bf16[656,128]{1,0:T(8,128)(2,1)S(1)}, u32[]{:S(2)}, u32[]{:S(2)}) collective-permute-start(bf16[656,128]{1,0:T(8,128)(2,1)} %get-tuple-element.68), channel_id=1, source_target_pairs={{0,3},{1,2},{2,5},{3,4},{4,7},{5,6},{6,1},{7,0},{8,11},{9,10},{10,... | collective-permute-start | bytes 503816 | tf_op jit(solution)/shard_map/ppermute | solution.py:566
  14.2 10.6 %collective-permute-start.6 = (bf16[656,128]{1,0:T(8,128)(2,1)}, bf16[656,128]{1,0:T(8,128)(2,1)}, u32[]{:S(2)}, u32[]{:S(2)}) collective-permute-start(bf16[656,128]{1,0:T(8,128)(2,1)} %get-tuple-element.69), channel_id=1, source_target_pairs={{0,7},{1,6},{2,1},{3,0},{4,3},{5,2},{6,5},{7,4},{8,15},{9,14},{10,... | collective-permute-start | bytes 503816 | tf_op jit(solution)/shard_map/ppermute | solution.py:566
  18.8 14.3 %copy-start.7 = (bf16[9,256,128]{2,1,0:T(8,128)(2,1)S(1)}, bf16[9,256,128]{2,1,0:T(8,128)(2,1)}, u32[]{:S(2)}) copy-start(bf16[9,256,128]{2,1,0:T(8,128)(2,1)} %get-tuple-element.97) | copy-start | bytes 1769476
  18.8 14.3 %copy-start.8 = (bf16[9,256,128]{2,1,0:T(8,128)(2,1)S(1)}, bf16[9,256,128]{2,1,0:T(8,128)(2,1)}, u32[]{:S(2)}) copy-start(bf16[9,256,128]{2,1,0:T(8,128)(2,1)} %get-tuple-element.98) | copy-start | bytes 1769476
  27.0 12.3 %collective-permute-start.7 = (bf16[1296,128]{1,0:T(8,128)(2,1)S(1)}, bf16[1296,128]{1,0:T(8,128)(2,1)S(1)}, u32[]{:S(2)}, u32[]{:S(2)}) collective-permute-start(bf16[1296,128]{1,0:T(8,128)(2,1)S(1)} %get-tuple-element.71), channel_id=1, source_target_pairs={{0,16},{1,17},{2,18},{3,19},{4,20},{5,21},{6,22},{7,23},{8,24},{9,... | collective-permute-start | bytes 995336 | tf_op jit(solution)/shard_map/ppermute | solution.py:571
  29.8 15.6 %collective-permute-start.8 = (bf16[1296,128]{1,0:T(8,128)(2,1)S(1)}, bf16[1296,128]{1,0:T(8,128)(2,1)S(1)}, u32[]{:S(2)}, u32[]{:S(2)}) collective-permute-start(bf16[1296,128]{1,0:T(8,128)(2,1)S(1)} %get-tuple-element.72), channel_id=1, source_target_pairs={{0,8},{1,9},{2,10},{3,11},{4,12},{5,13},{6,14},{7,15},{8,16},{9,17... | collective-permute-start | bytes 995336 | tf_op jit(solution)/shard_map/ppermute | solution.py:571
  30.5 15.0 %collective-permute-start.9 = (bf16[1296,128]{1,0:T(8,128)(2,1)S(1)}, bf16[1296,128]{1,0:T(8,128)(2,1)S(1)}, u32[]{:S(2)}, u32[]{:S(2)}) collective-permute-start(bf16[1296,128]{1,0:T(8,128)(2,1)S(1)} %get-tuple-element.73), channel_id=1, source_target_pairs={{0,24},{1,25},{2,26},{3,27},{4,28},{5,29},{6,30},{7,31},{8,0},{9,1... | collective-permute-start | bytes 995336 | tf_op jit(solution)/shard_map/ppermute | solution.py:571
  33.1 13.6 %copy-start.3 = (bf16[8,512,128]{2,1,0:T(8,128)(2,1)S(1)}, bf16[8,512,128]{2,1,0:T(8,128)(2,1)}, u32[]{:S(2)}) copy-start(bf16[8,512,128]{2,1,0:T(8,128)(2,1)} %skip.1) | copy-start | bytes 3145732
  33.1 13.6 %copy-start.5 = (bf16[8,64,256]{2,1,0:T(8,128)(2,1)S(1)}, bf16[8,64,256]{2,1,0:T(8,128)(2,1)}, u32[]{:S(2)}) copy-start(bf16[8,64,256]{2,1,0:T(8,128)(2,1)} %parents.1) | copy-start | bytes 786436
  33.1 13.6 %copy-start.9 = (s32[8]{0:T(128)S(1)}, s32[8]{0:T(128)}, u32[]{:S(2)}) copy-start(s32[8]{0:T(128)} %parent_dest.1) | copy-start | bytes 100
  33.1 13.6 %copy-start.10 = (s32[8]{0:T(128)S(1)}, s32[8]{0:T(128)}, u32[]{:S(2)}) copy-start(s32[8]{0:T(128)} %skip_dest.1) | copy-start | bytes 100
  47.3 17.6 %collective-permute-start.10 = (bf16[4,480,128]{2,1,0:T(8,128)(2,1)}, bf16[4,480,128]{2,1,0:T(8,128)(2,1)S(1)}, u32[]{:S(2)}, u32[]{:S(2)}) collective-permute-start(bf16[4,480,128]{2,1,0:T(8,128)(2,1)} %get-tuple-element.161), channel_id=1, source_target_pairs={{0,1},{1,2},{2,3},{3,4},{4,5},{5,6},{6,7},{7,8},{8,9},{9,10},{10,1... | collective-permute-start | bytes 1474568 | tf_op jit(solution)/shard_map/ppermute | solution.py:583
  49.2 15.6 %collective-permute-start.11 = (bf16[4,480,128]{2,1,0:T(8,128)(2,1)}, bf16[4,480,128]{2,1,0:T(8,128)(2,1)S(1)}, u32[]{:S(2)}, u32[]{:S(2)}) collective-permute-start(bf16[4,480,128]{2,1,0:T(8,128)(2,1)} %get-tuple-element.161), channel_id=1, source_target_pairs={{1,0},{2,1},{3,2},{4,3},{5,4},{6,5},{7,6},{8,7},{9,8},{10,9},{11,1... | collective-permute-start | bytes 1474568 | tf_op jit(solution)/shard_map/ppermute | solution.py:584
  57.2 1.0 %copy-start.2 = (bf16[768,256]{1,0:T(8,128)(2,1)S(1)}, bf16[768,256]{1,0:T(8,128)(2,1)}, u32[]{:S(2)}) copy-start(bf16[768,256]{1,0:T(8,128)(2,1)} %pad_maximum_fusion.1.side_weight) | copy-start | bytes 1179652

commit v5 on v4

--- a/solution.py
+++ b/solution.py
@@ -331,7 +331,9 @@
     )(place, came)
 
 
-def fill_pool(pool, groups, up_weight, parents_at):
+def fill_pool(pool, groups, up_weight, up_all, parents_at):
+    for ab in range(4):
+        up_all[:, 128 * ab : 128 * ab + 128] = up_weight[ab]
     row = lax.broadcasted_iota(I32, (256, 64), 0)
     column = lax.broadcasted_iota(I32, (256, 64), 1)
     in_brick = row & 127
@@ -368,7 +370,7 @@
                 )
             )
         spaced = jnp.concatenate(spaced, axis=0)
-        every = jnp.dot(spaced, up_weight[...], preferred_element_type=F32)
+        every = jnp.dot(spaced, up_all[...], preferred_element_type=F32)
         every = every.astype(BF16).astype(F32)
         for ab in range(4):
             made = every[:, ab * 128 : ab * 128 + 128]
@@ -400,10 +402,14 @@
 
 
 def near_kernel(
-    lookup, own, up_weight, pair_weight, side_weight, conv_weight, out,
-    pool, shifted_pair, window_pair, deeper_pair
+    lookup, own, up_weight, conv_weight, out,
+    pool, shifted_pair, window_pair, deeper_pair, pair_weight, side_weight, up_all
 ):
-    fill_pool(pool, (own,), up_weight, SKIP_ROWS)
+    for half in range(2):
+        columns = slice(128 * half, 128 * half + 128)
+        pair_weight[:, columns] = conv_weight[half]
+        side_weight[:, columns] = conv_weight[2, 768 * half : 768 * half + 768]
+    fill_pool(pool, (own,), up_weight, up_all, SKIP_ROWS)
     spans = {-1: (7, 8, 0), 0: (0, 8, 1), 1: (0, 1, 9)}
 
     for b in range(BRICKS):
@@ -446,9 +452,9 @@
 
 
 def far_kernel(
-    lookup, before, after, near, up_weight, conv_weight, out, pool, shifted, window, total
+    lookup, before, after, near, up_weight, conv_weight, out, pool, shifted, window, total, up_all
 ):
-    fill_pool(pool, (before, after), up_weight, SURFACE)
+    fill_pool(pool, (before, after), up_weight, up_all, SURFACE)
     total[...] = near[...].reshape(BRICKS * 512, 128)
     shifted[...] = jnp.zeros(shifted.shape, F32)
 
@@ -520,23 +526,26 @@
     out[...] = jnp.maximum(total[...], 0.0).astype(BF16).reshape(BRICKS, 512, 128)
 
 
-def convolve_near(lookup, own, up_weight, pair_weight, side_weight, conv_weight):
+def convolve_near(lookup, own, up_weight, conv_weight):
     return pl.pallas_call(
         near_kernel,
         out_shape=jax.ShapeDtypeStruct((BRICKS, 512, 128), F32),
-        in_specs=[SMEM] + [VMEM] * 5,
+        in_specs=[SMEM] + [VMEM] * 3,
         out_specs=VMEM,
         scratch_shapes=[
             pltpu.VMEM((BRICKS + 1, 2, 512, 128), F32),
             [pltpu.VMEM((3, 10, 10, 8, 256), F32)] * 2,
             [pltpu.VMEM((640, 9 * 256), BF16)] * 2,
             [pltpu.VMEM((576, 3 * 256), BF16)] * 2,
+            pltpu.VMEM((9 * 256, 256), BF16),
+            pltpu.VMEM((3 * 256, 256), BF16),
+            pltpu.VMEM((512, 512), BF16),
         ],
         compiler_params=pltpu.CompilerParams(vmem_limit_bytes=32 * 2**20),
         cost_estimate=pl.CostEstimate(
             flops=10**10, bytes_accessed=4 * 10**7, transcendentals=0
         ),
-    )(lookup, own, up_weight, pair_weight, side_weight, conv_weight)
+    )(lookup, own, up_weight, conv_weight)
 
 
 def convolve_far(lookup, before, after, near, up_weight, conv_weight):
@@ -550,6 +559,7 @@
             pltpu.VMEM((6, 3, 10, 8, 256), F32),
             pltpu.VMEM((6, BRICKS * 64, 9 * 256), BF16),
             pltpu.VMEM((BRICKS * 512, 128), F32),
+            pltpu.VMEM((512, 512), BF16),
         ],
         compiler_params=pltpu.CompilerParams(vmem_limit_bytes=32 * 2**20),
     )(lookup, before, after, near, up_weight, conv_weight)
@@ -588,12 +598,10 @@
     near_lookup = jnp.where(here, ahead, BRICKS)
     far = jnp.where(ahead < 0, ahead + BRICKS, ahead)
     far_lookup = jnp.where((neighbours >= 0) & ~here, far, 2 * BRICKS)
-    up_weight = up_weight.reshape(4, 512, 128).transpose(1, 0, 2).reshape(512, 512)
+    up_weight = up_weight.reshape(4, 512, 128)
     conv_weight = conv_weight.reshape(3, 9 * 256, 128)
-    pair_weight = jnp.concatenate([conv_weight[0], conv_weight[1]], axis=1)
-    side_weight = jnp.concatenate([conv_weight[2, 0:768], conv_weight[2, 768:1536]], axis=1)
     near = convolve_near(
-        near_lookup.reshape(-1), own, up_weight, pair_weight, side_weight, conv_weight
+        near_lookup.reshape(-1), own, up_weight, conv_weight
     )
     return convolve_far(far_lookup.reshape(-1), before, after, near, up_weight, conv_weight)
 

time: 70 us -> 68.1 us (0.973)
  waiting for transfers between devices: 16.3 us -> 24 us
  local copies, waits for them, and re-layouts: 5.86 us -> 0.18 us
  starting transfers between devices: 26.4 us -> 24.9 us
  other arithmetic: 2.12 us -> 0.77 us
  Pallas kernels: 18.2 us -> 16.9 us
    ppermute x7, waiting for transfers between devices: 4.05 us -> 12.7 us  [per_device(): came.append(lax.ppermute(first[j], 'gy', steps))]
    slice x1 -> x0, local copies, waits for them, and re-layouts: 2.37 us -> none  [per_device(): pair_weight = jnp.concatenate([conv_weight[0], conv_weight[1]], axis=1)]
    concatenate x2 -> x0, other arithmetic: 2.03 us -> none  [the longest x1 1.9 us: per_device(): jnp.concatenate([conv_weight[2, 0:768], conv_weight[2, 768:1536]], axis=1)]
    ppermute x7, starting transfers between devices: 10.4 us -> 8.54 us  [per_device(): came.append(lax.ppermute(first[j], 'gy', steps))]
    reshape x2 -> x1, local copies, waits for them, and re-layouts: 1.53 us -> 0.08 us  [per_device(): near = convolve_near(near_lookup.reshape(-1), own, up_weight, conv_weight)]
    unnamed x19 -> x4, local copies, waits for them, and re-layouts: 1.11 us -> 0.01 us
    pallas_call x1, Pallas kernels: 3.42 us -> 2.36 us  [first_pack(): pl.pallas_call(first_kernel, out_shape=[jax.ShapeDtypeStruct((BODY + HEAD...]
    ppermute x3, waiting for transfers between devices: 12.2 us -> 11.4 us  [per_device(): arrived.append(lax.ppermute(messages[k], 'gy', steps))]
  transfers between devices with their start and end apart: 12 -> 12, of which waited for: 4 -> 7; matrix products, arithmetic and copies ran while one was open for 10% -> 1% of each run, Pallas kernels for 9% -> 10%
where the time goes in v5:
time: 68.1 us; the launch traced here: 67.7 us
  starting transfers between devices  24.9 us (37%)
  waiting for transfers between devices  24 us (35%)
  Pallas kernels  16.9 us (25%)
  loops' own time  0.79 us (1%)
  other arithmetic  0.77 us (1%)
    ppermute x7, waiting for transfers between devices, per_device(): came.append(lax.ppermute(first[j], 'gy', steps))  12.7 us
    ppermute x3, waiting for transfers between devices, per_device(): arrived.append(lax.ppermute(messages[k], 'gy', steps))  11.4 us
    ppermute x7, starting transfers between devices, per_device(): came.append(lax.ppermute(first[j], 'gy', steps))  8.54 us
    ppermute x1, starting transfers between devices, per_device(): after = lax.ppermute(surface, ('gx', 'gy'), [(j, i) for i, j in up])  8.04 us
    pallas_call x1, Pallas kernels, convolve_near(): pl.pallas_call(near_kernel, out_shape=jax.ShapeDtypeStruct((BRICKS, 512,...  6.68 us
    ppermute x3, starting transfers between devices, per_device(): arrived.append(lax.ppermute(messages[k], 'gy', steps))  6.36 us
    pallas_call x1, Pallas kernels, convolve_far(): pl.pallas_call(far_kernel, out_shape=jax.ShapeDtypeStruct((BRICKS, 512, 1...  4.91 us
    pallas_call x1, Pallas kernels, first_pack(): pl.pallas_call(first_kernel, out_shape=[jax.ShapeDtypeStruct((BODY + HEAD...  2.36 us
  transfers between devices with their start and end apart: 12, of which 7 were waited for; matrix products, arithmetic and copies ran while one was open for 1% of the time, Pallas kernels for 10%

profile of v5, /device:TPU:16, one launch (start us, length us, event | category | flops | bytes accessed | tf_op | source)
XLA Modules:
  0.0 67.7 jit_solution(6941019992986169682)
XLA Ops:
  0.0 0.1 pad_add_fusion.place
  0.1 2.4 %shard_map.73 = (bf16[656,128]{1,0:T(8,128)(2,1)S(1)}, bf16[656,128]{1,0:T(8,128)(2,1)S(1)}, bf16[656,128]{1,0:T(8,128)(2,1)S(1)}, bf16[656,128]{1,0:T(8,128)(2,...) custom-call(s32[8]{0:T(128)} %parent_dest.1, ...), custom_call_target="tpu_custom_call" | custom-call | tf_op jit(solution)/shard_map/pallas_call | solution.py:73
  2.4 0.1 collective-permute-start
  2.5 2.0 %collective-permute-start.1 = (bf16[656,128]{1,0:T(8,128)(2,1)S(1)}, bf16[656,128]{1,0:T(8,128)(2,1)S(1)}, u32[]{:S(2)}, u32[]{:S(2)}) collective-permute-start(bf16[656,128]{1,0:T(8,128)(2,1)S(1)} %get-tuple-element.64), channel_id=1, source_target_pairs={{0,2},{1,3},{2,4},{3,5},{4,6},{5,7},{6,0},{7,1},{8,10},{9,11},{10,... | collective-permute-start | bytes 503816 | tf_op jit(solution)/shard_map/ppermute | solution.py:576
  4.5 2.5 %collective-permute-start.2 = (bf16[656,128]{1,0:T(8,128)(2,1)S(1)}, bf16[656,128]{1,0:T(8,128)(2,1)S(1)}, u32[]{:S(2)}, u32[]{:S(2)}) collective-permute-start(bf16[656,128]{1,0:T(8,128)(2,1)S(1)} %get-tuple-element.65), channel_id=1, source_target_pairs={{0,6},{1,7},{2,0},{3,1},{4,2},{5,3},{6,4},{7,5},{8,14},{9,15},{10,... | collective-permute-start | bytes 503816 | tf_op jit(solution)/shard_map/ppermute | solution.py:576
  7.0 1.7 %collective-permute-start.3 = (bf16[656,128]{1,0:T(8,128)(2,1)S(1)}, bf16[656,128]{1,0:T(8,128)(2,1)S(1)}, u32[]{:S(2)}, u32[]{:S(2)}) collective-permute-start(bf16[656,128]{1,0:T(8,128)(2,1)S(1)} %get-tuple-element.66), channel_id=1, source_target_pairs={{0,4},{1,5},{2,6},{3,7},{4,0},{5,1},{6,2},{7,3},{8,12},{9,13},{10,... | collective-permute-start | bytes 503816 | tf_op jit(solution)/shard_map/ppermute | solution.py:576
  8.6 1.3 %collective-permute-start.4 = (bf16[656,128]{1,0:T(8,128)(2,1)S(1)}, bf16[656,128]{1,0:T(8,128)(2,1)S(1)}, u32[]{:S(2)}, u32[]{:S(2)}) collective-permute-start(bf16[656,128]{1,0:T(8,128)(2,1)S(1)} %get-tuple-element.67), channel_id=1, source_target_pairs={{0,5},{1,4},{2,7},{3,6},{4,1},{5,0},{6,3},{7,2},{8,13},{9,12},{10,... | collective-permute-start | bytes 503816 | tf_op jit(solution)/shard_map/ppermute | solution.py:576
  9.9 0.0 collective-permute-done.refs_1_
  9.9 0.0 collective-permute-start.5
  9.9 1.9 %collective-permute-done.1.refs_2_ = bf16[656,128]{1,0:T(8,128)(2,1)S(1)} collective-permute-done((bf16[656,128]{1,0:T(8,128)(2,1)S(1)}, bf16[656,128]{1,0:T(8,128)(2,1)S(1)}, u32[]{:S(2)}, u32[]{:S(2)}) %collective-permute-start.1) | collective-permute-done | bytes 167968 | tf_op jit(solution)/shard_map/ppermute | solution.py:576
  11.8 1.1 %collective-permute-start.6 = (bf16[656,128]{1,0:T(8,128)(2,1)S(1)}, bf16[656,128]{1,0:T(8,128)(2,1)S(1)}, u32[]{:S(2)}, u32[]{:S(2)}) collective-permute-start(bf16[656,128]{1,0:T(8,128)(2,1)S(1)} %get-tuple-element.69), channel_id=1, source_target_pairs={{0,7},{1,6},{2,1},{3,0},{4,3},{5,2},{6,5},{7,4},{8,15},{9,14},{10,... | collective-permute-start | bytes 503816 | tf_op jit(solution)/shard_map/ppermute | solution.py:576
  12.9 5.8 %collective-permute-done.2.refs_3_ = bf16[656,128]{1,0:T(8,128)(2,1)S(1)} collective-permute-done((bf16[656,128]{1,0:T(8,128)(2,1)S(1)}, bf16[656,128]{1,0:T(8,128)(2,1)S(1)}, u32[]{:S(2)}, u32[]{:S(2)}) %collective-permute-start.2) | collective-permute-done | bytes 167968 | tf_op jit(solution)/shard_map/ppermute | solution.py:576
  18.7 0.0 collective-permute-done.3.refs_4_
  18.7 1.1 %collective-permute-done.4.refs_5_ = bf16[656,128]{1,0:T(8,128)(2,1)S(1)} collective-permute-done((bf16[656,128]{1,0:T(8,128)(2,1)S(1)}, bf16[656,128]{1,0:T(8,128)(2,1)S(1)}, u32[]{:S(2)}, u32[]{:S(2)}) %collective-permute-start.4) | collective-permute-done | bytes 167968 | tf_op jit(solution)/shard_map/ppermute | solution.py:576
  19.8 3.9 %collective-permute-done.5.refs_6_ = bf16[656,128]{1,0:T(8,128)(2,1)S(1)} collective-permute-done((bf16[656,128]{1,0:T(8,128)(2,1)S(1)}, bf16[656,128]{1,0:T(8,128)(2,1)S(1)}, u32[]{:S(2)}, u32[]{:S(2)}) %collective-permute-start.5) | collective-permute-done | bytes 167968 | tf_op jit(solution)/shard_map/ppermute | solution.py:576
  23.7 0.0 collective-permute-done.6.refs_7_
  23.7 1.8 %shard_map.74 = (bf16[1296,128]{1,0:T(8,128)(2,1)S(1)}, bf16[1296,128]{1,0:T(8,128)(2,1)S(1)}, bf16[1296,128]{1,0:T(8,128)(2,1)S(1)}, bf16[1296,128]{1,0:T(8,128)(2,1)S(1)}) custom-call(s32[3]{0:T(128)S(1)} %pad_add_fusion.place, bf16[656,128]{1,0:T(8,128)(2,1)S(1)} %get-tuple-element.62.refs_0_, bf16[656,128]{1,0:T(8,128)(2,1)S(1)} %collective-permute-done.refs_1_, ...), custom_call_target="tpu_custom_call" | custom-call | tf_op jit(solution)/shard_map/pallas_call | solution.py:157
  25.5 3.1 %collective-permute-start.7 = (bf16[1296,128]{1,0:T(8,128)(2,1)S(1)}, bf16[1296,128]{1,0:T(8,128)(2,1)S(1)}, u32[]{:S(2)}, u32[]{:S(2)}) collective-permute-start(bf16[1296,128]{1,0:T(8,128)(2,1)S(1)} %get-tuple-element.71), channel_id=1, source_target_pairs={{0,16},{1,17},{2,18},{3,19},{4,20},{5,21},{6,22},{7,23},{8,24},{9,... | collective-permute-start | bytes 995336 | tf_op jit(solution)/shard_map/ppermute | solution.py:581
  28.6 0.5 collective-permute-start.8
  29.2 2.7 %collective-permute-start.9 = (bf16[1296,128]{1,0:T(8,128)(2,1)S(1)}, bf16[1296,128]{1,0:T(8,128)(2,1)S(1)}, u32[]{:S(2)}, u32[]{:S(2)}) collective-permute-start(bf16[1296,128]{1,0:T(8,128)(2,1)S(1)} %get-tuple-element.73), channel_id=1, source_target_pairs={{0,24},{1,25},{2,26},{3,27},{4,28},{5,29},{6,30},{7,31},{8,0},{9,1... | collective-permute-start | bytes 995336 | tf_op jit(solution)/shard_map/ppermute | solution.py:581
  31.9 0.7 %fusion.1 = (s32[4,26]{1,0:T(4,128)S(1)}, s32[4,26]{1,0:T(4,128)S(1)}) fusion(s32[4,26]{1,0:T(4,128)} %param.13, s32[]{:T(128)S(6)} %mul.11), kind=kLoop, calls=%fused_computation.3 | loop fusion | flops 1352 | bytes 1252 | tf_op jit(solution)/shard_map/jit(_where)/select_n | solution.py:598
  32.6 0.1 reshape.15.lookup
  32.6 0.1 reshape.14.lookup
  32.7 5.1 %collective-permute-done.7.refs_1_ = bf16[1296,128]{1,0:T(8,128)(2,1)S(1)} collective-permute-done((bf16[1296,128]{1,0:T(8,128)(2,1)S(1)}, bf16[1296,128]{1,0:T(8,128)(2,1)S(1)}, u32[]{:S(2)}, u32[]{:S(2)}) %collective-permute-start.7) | collective-permute-done | bytes 331808 | tf_op jit(solution)/shard_map/ppermute | solution.py:581
  37.8 6.2 %collective-permute-done.8.refs_2_ = bf16[1296,128]{1,0:T(8,128)(2,1)S(1)} collective-permute-done((bf16[1296,128]{1,0:T(8,128)(2,1)S(1)}, bf16[1296,128]{1,0:T(8,128)(2,1)S(1)}, u32[]{:S(2)}, u32[]{:S(2)}) %collective-permute-start.8) | collective-permute-done | bytes 331808 | tf_op jit(solution)/shard_map/ppermute | solution.py:581
  44.0 0.1 collective-permute-done.9.refs_3_
  44.1 1.2 %shard_map.75 = (bf16[4,640,128]{2,1,0:T(8,128)(2,1)}, bf16[4,480,128]{2,1,0:T(8,128)(2,1)}, s32[1]{0:T(128)}) custom-call(bf16[1296,128]{1,0:T(8,128)(2,1)S(1)} %get-tuple-element.70.refs_0_, bf16[1296,128]{1,0:T(8,128)(2,1)S(1)} %collective-permute-done.7.refs_1_, bf16[1296,128]{1,0:T(8,128)(2,1)S(1)} %collective-permute-done.8.refs_2_, ...), custom_call_target="tpu_custom_call" | custom-call | tf_op jit(solution)/shard_map/pallas_call | solution.py:216
  45.3 0.0 copy-start.1
  45.3 0.0 copy-start.2
  45.3 0.8 %while.11 = (bf16[4,640,128]{2,1,0:T(8,128)(2,1)}, bf16[4,480,128]{2,1,0:T(8,128)(2,1)}, s32[1]{0:T(128)}, s32[8]{0:T(128)}, s32[8]{0:T(128)}, /*index=5*/s32[3]...) while((bf16[4,640,128]{2,1,0:T(8,128)(2,1)}, bf16[4,480,128]{2,1,0:T(8,128)(2,1)}, s32[1]{0:T(128)}, ...), condition=%region_1.2_spmd, body=%region_0.1_spmd | while | flops 1 | bytes 37617804 | solution.py:583
  46.1 1.9 %collective-permute-start.10 = (bf16[4,480,128]{2,1,0:T(8,128)(2,1)}, bf16[4,480,128]{2,1,0:T(8,128)(2,1)S(1)}, u32[]{:S(2)}, u32[]{:S(2)}) collective-permute-start(bf16[4,480,128]{2,1,0:T(8,128)(2,1)} %get-tuple-element.77), channel_id=1, source_target_pairs={{0,1},{1,2},{2,3},{3,4},{4,5},{5,6},{6,7},{7,8},{8,9},{9,10},{10,1... | collective-permute-start | bytes 1474568 | tf_op jit(solution)/shard_map/ppermute | solution.py:593
  48.0 8.0 %collective-permute-start.11 = (bf16[4,480,128]{2,1,0:T(8,128)(2,1)}, bf16[4,480,128]{2,1,0:T(8,128)(2,1)S(1)}, u32[]{:S(2)}, u32[]{:S(2)}) collective-permute-start(bf16[4,480,128]{2,1,0:T(8,128)(2,1)} %get-tuple-element.77), channel_id=1, source_target_pairs={{1,0},{2,1},{3,2},{4,3},{5,4},{6,5},{7,6},{8,7},{9,8},{10,9},{11,1... | collective-permute-start | bytes 1474568 | tf_op jit(solution)/shard_map/ppermute | solution.py:594
  56.1 0.0 copy-done.1
  56.1 0.0 copy-done.2
  56.1 6.7 %shard_map.76.near = f32[4,512,128]{2,1,0:T(8,128)S(1)} custom-call(s32[104]{0:T(128)S(1)} %reshape.15.lookup, bf16[4,640,128]{2,1,0:T(8,128)(2,1)} %get-tuple-element.78.own, bf16[4,512,128]{2,1,0:T(8,128)(2,1)S(1)} %bitcast.8, bf16[3,2304,128]{2,1,0:T(8,128)(2,1)S(1)} %bitcast.6), custom_call_target="tpu_custom_call" | custom-call | flops 10000000000 | bytes 40000000 | tf_op jit(solution)/shard_map/pallas_call | solution.py:530
  62.8 0.0 collective-permute-done.10.before
  62.8 0.0 collective-permute-done.11.after
  62.8 4.9 %shard_map.77 = bf16[4,512,128]{2,1,0:T(8,128)(2,1)} custom-call(s32[104]{0:T(128)S(1)} %reshape.14.lookup, bf16[4,480,128]{2,1,0:T(8,128)(2,1)S(1)} %collective-permute-done.10.before, bf16[4,480,128]{2,1,0:T(8,128)(2,1)S(1)} %collective-permute-done.11.after, f32[4,512,128]{2,1,0:T(8,128)S(1)} %shard_map.76.near, bf16[4,512,128]{2,1,0:T(8,128)(2,1)S(1)} %bitcast.9, ...), custom_call_target="tpu_custom_call" | custom-call | tf_op jit(solution)/shard_map/pallas_call | solution.py:552
Async XLA Ops:
  2.4 7.5 %collective-permute-start = (bf16[656,128]{1,0:T(8,128)(2,1)S(1)}, bf16[656,128]{1,0:T(8,128)(2,1)S(1)}, u32[]{:S(2)}, u32[]{:S(2)}) collective-permute-start(bf16[656,128]{1,0:T(8,128)(2,1)S(1)} %get-tuple-element.63), channel_id=1, source_target_pairs={{0,1},{1,0},{2,3},{3,2},{4,5},{5,4},{6,7},{7,6},{8,9},{9,8},{10,11... | collective-permute-start | bytes 503816 | tf_op jit(solution)/shard_map/ppermute | solution.py:576
  2.5 9.2 %collective-permute-start.1 = (bf16[656,128]{1,0:T(8,128)(2,1)S(1)}, bf16[656,128]{1,0:T(8,128)(2,1)S(1)}, u32[]{:S(2)}, u32[]{:S(2)}) collective-permute-start(bf16[656,128]{1,0:T(8,128)(2,1)S(1)} %get-tuple-element.64), channel_id=1, source_target_pairs={{0,2},{1,3},{2,4},{3,5},{4,6},{5,7},{6,0},{7,1},{8,10},{9,11},{10,... | collective-permute-start | bytes 503816 | tf_op jit(solution)/shard_map/ppermute | solution.py:576
  4.5 14.1 %collective-permute-start.2 = (bf16[656,128]{1,0:T(8,128)(2,1)S(1)}, bf16[656,128]{1,0:T(8,128)(2,1)S(1)}, u32[]{:S(2)}, u32[]{:S(2)}) collective-permute-start(bf16[656,128]{1,0:T(8,128)(2,1)S(1)} %get-tuple-element.65), channel_id=1, source_target_pairs={{0,6},{1,7},{2,0},{3,1},{4,2},{5,3},{6,4},{7,5},{8,14},{9,15},{10,... | collective-permute-start | bytes 503816 | tf_op jit(solution)/shard_map/ppermute | solution.py:576
  7.0 11.7 %collective-permute-start.3 = (bf16[656,128]{1,0:T(8,128)(2,1)S(1)}, bf16[656,128]{1,0:T(8,128)(2,1)S(1)}, u32[]{:S(2)}, u32[]{:S(2)}) collective-permute-start(bf16[656,128]{1,0:T(8,128)(2,1)S(1)} %get-tuple-element.66), channel_id=1, source_target_pairs={{0,4},{1,5},{2,6},{3,7},{4,0},{5,1},{6,2},{7,3},{8,12},{9,13},{10,... | collective-permute-start | bytes 503816 | tf_op jit(solution)/shard_map/ppermute | solution.py:576
  8.6 11.2 %collective-permute-start.4 = (bf16[656,128]{1,0:T(8,128)(2,1)S(1)}, bf16[656,128]{1,0:T(8,128)(2,1)S(1)}, u32[]{:S(2)}, u32[]{:S(2)}) collective-permute-start(bf16[656,128]{1,0:T(8,128)(2,1)S(1)} %get-tuple-element.67), channel_id=1, source_target_pairs={{0,5},{1,4},{2,7},{3,6},{4,1},{5,0},{6,3},{7,2},{8,13},{9,12},{10,... | collective-permute-start | bytes 503816 | tf_op jit(solution)/shard_map/ppermute | solution.py:576
  9.9 13.8 %collective-permute-start.5 = (bf16[656,128]{1,0:T(8,128)(2,1)S(1)}, bf16[656,128]{1,0:T(8,128)(2,1)S(1)}, u32[]{:S(2)}, u32[]{:S(2)}) collective-permute-start(bf16[656,128]{1,0:T(8,128)(2,1)S(1)} %get-tuple-element.68), channel_id=1, source_target_pairs={{0,3},{1,2},{2,5},{3,4},{4,7},{5,6},{6,1},{7,0},{8,11},{9,10},{10,... | collective-permute-start | bytes 503816 | tf_op jit(solution)/shard_map/ppermute | solution.py:576
  11.8 11.9 %collective-permute-start.6 = (bf16[656,128]{1,0:T(8,128)(2,1)S(1)}, bf16[656,128]{1,0:T(8,128)(2,1)S(1)}, u32[]{:S(2)}, u32[]{:S(2)}) collective-permute-start(bf16[656,128]{1,0:T(8,128)(2,1)S(1)} %get-tuple-element.69), channel_id=1, source_target_pairs={{0,7},{1,6},{2,1},{3,0},{4,3},{5,2},{6,5},{7,4},{8,15},{9,14},{10,... | collective-permute-start | bytes 503816 | tf_op jit(solution)/shard_map/ppermute | solution.py:576
  25.5 12.3 %collective-permute-start.7 = (bf16[1296,128]{1,0:T(8,128)(2,1)S(1)}, bf16[1296,128]{1,0:T(8,128)(2,1)S(1)}, u32[]{:S(2)}, u32[]{:S(2)}) collective-permute-start(bf16[1296,128]{1,0:T(8,128)(2,1)S(1)} %get-tuple-element.71), channel_id=1, source_target_pairs={{0,16},{1,17},{2,18},{3,19},{4,20},{5,21},{6,22},{7,23},{8,24},{9,... | collective-permute-start | bytes 995336 | tf_op jit(solution)/shard_map/ppermute | solution.py:581
  28.6 15.4 %collective-permute-start.8 = (bf16[1296,128]{1,0:T(8,128)(2,1)S(1)}, bf16[1296,128]{1,0:T(8,128)(2,1)S(1)}, u32[]{:S(2)}, u32[]{:S(2)}) collective-permute-start(bf16[1296,128]{1,0:T(8,128)(2,1)S(1)} %get-tuple-element.72), channel_id=1, source_target_pairs={{0,8},{1,9},{2,10},{3,11},{4,12},{5,13},{6,14},{7,15},{8,16},{9,17... | collective-permute-start | bytes 995336 | tf_op jit(solution)/shard_map/ppermute | solution.py:581
  29.2 14.9 %collective-permute-start.9 = (bf16[1296,128]{1,0:T(8,128)(2,1)S(1)}, bf16[1296,128]{1,0:T(8,128)(2,1)S(1)}, u32[]{:S(2)}, u32[]{:S(2)}) collective-permute-start(bf16[1296,128]{1,0:T(8,128)(2,1)S(1)} %get-tuple-element.73), channel_id=1, source_target_pairs={{0,24},{1,25},{2,26},{3,27},{4,28},{5,29},{6,30},{7,31},{8,0},{9,1... | collective-permute-start | bytes 995336 | tf_op jit(solution)/shard_map/ppermute | solution.py:581
  45.3 10.8 %copy-start.1 = (bf16[27,256,128]{2,1,0:T(8,128)(2,1)S(1)}, bf16[27,256,128]{2,1,0:T(8,128)(2,1)}, u32[]{:S(2)}) copy-start(bf16[27,256,128]{2,1,0:T(8,128)(2,1)} %param.15) | copy-start | bytes 5308420
  45.3 10.8 %copy-start.2 = (bf16[8,256,128]{2,1,0:T(8,128)(2,1)S(1)}, bf16[8,256,128]{2,1,0:T(8,128)(2,1)}, u32[]{:S(2)}) copy-start(bf16[8,256,128]{2,1,0:T(8,128)(2,1)} %param.14) | copy-start | bytes 1572868
  46.1 16.7 %collective-permute-start.10 = (bf16[4,480,128]{2,1,0:T(8,128)(2,1)}, bf16[4,480,128]{2,1,0:T(8,128)(2,1)S(1)}, u32[]{:S(2)}, u32[]{:S(2)}) collective-permute-start(bf16[4,480,128]{2,1,0:T(8,128)(2,1)} %get-tuple-element.77), channel_id=1, source_target_pairs={{0,1},{1,2},{2,3},{3,4},{4,5},{5,6},{6,7},{7,8},{8,9},{9,10},{10,1... | collective-permute-start | bytes 1474568 | tf_op jit(solution)/shard_map/ppermute | solution.py:593
  48.0 14.8 %collective-permute-start.11 = (bf16[4,480,128]{2,1,0:T(8,128)(2,1)}, bf16[4,480,128]{2,1,0:T(8,128)(2,1)S(1)}, u32[]{:S(2)}, u32[]{:S(2)}) collective-permute-start(bf16[4,480,128]{2,1,0:T(8,128)(2,1)} %get-tuple-element.77), channel_id=1, source_target_pairs={{1,0},{2,1},{3,2},{4,3},{5,4},{6,5},{7,6},{8,7},{9,8},{10,9},{11,1... | collective-permute-start | bytes 1474568 | tf_op jit(solution)/shard_map/ppermute | solution.py:594
